TPU v7x, 128 devices: a whole 4x4x4 slice. The times are simulated.
128 devices in a mesh: replica: 8 (over y_lo, z), fsdp: 16 (over x, y_hi, core).
Axes of the slice: x: 4, y: 4 (y_hi: 2, y_lo: 2; y = y_hi * 2 + y_lo), z: 4, core: 2. Of those that a mesh axis runs over, the one named last changes fastest.
Arguments:
- activations: bfloat16 [8, 16, 256, 2304], P('replica', 'fsdp'), may hold values from -180 to 180
- labels: int32 [8, 16, 256], P('replica', 'fsdp'), may hold values from 0 to 255
- own_q: bfloat16 [8, 2304, 1024], P('replica', 'fsdp'), may hold values from -1 to 1
- own_k: bfloat16 [8, 2304, 512], P('replica', 'fsdp'), may hold values from -0.375 to 0.375
- own_v: bfloat16 [8, 2304, 512], P('replica', 'fsdp'), may hold values from -0.125 to 0.125
- own_o: bfloat16 [8, 1024, 2304], P('replica', 'fsdp'), may hold values from -0.1875 to 0.1875
- peer_q: bfloat16 [8, 2304, 1024], P('replica', 'fsdp'), may hold values from -1 to 1
- peer_k: bfloat16 [8, 2304, 512], P('replica', 'fsdp'), may hold values from -0.375 to 0.375
- peer_v: bfloat16 [8, 2304, 512], P('replica', 'fsdp'), may hold values from -0.125 to 0.125
- peer_o: bfloat16 [8, 1024, 2304], P('replica', 'fsdp'), may hold values from -0.1875 to 0.1875
- norm_gains: float32 [2, 2304], replicated, may hold values from 0.1 to 1.9
- label_head: bfloat16 [2304, 256], replicated, may hold values from -1 to 1
Outputs:
- token_loss: float32 [8, 16, 256], P('replica', 'fsdp')
- grad_q: float32 [8, 2304, 1024], P('replica', 'fsdp')
- grad_k: float32 [8, 2304, 512], P('replica', 'fsdp')
- grad_v: float32 [8, 2304, 512], P('replica', 'fsdp')
- grad_o: float32 [8, 1024, 2304], P('replica', 'fsdp')
All inputs are finite; a program needn't handle non-finite values.
Results may differ from a plain program's by a relative error of at most 0.03.
The roundings to bfloat16 on the way count: a program that leaves them out, or rounds other values in their place, can miss the bound.
Values may be sent and summed in bfloat16 or wider, within the bound.
No kernel may reach another device: no remote copies, remote signals or barrier semaphores. Data moves between devices by JAX's collectives and lax.ppermute only.
A program may use at most 128 MiB of HBM per device.

v0:
```python
import math

import jax
import jax.numpy as jnp
from jax import lax
from jax.sharding import PartitionSpec as P

HEAD = 256


EPSILON = 1e-06
ATTN_CAP = 50.0
LABEL_CAP = 30.0
MASKED = -1e30


def passed_along(value, axis, steps):
    count = lax.axis_size(axis)
    pairs = [(source, (source + steps) % count) for source in range(count)]
    return lax.ppermute(value, axis, pairs)


def rms_scale(values, gain):
    return values * lax.rsqrt(jnp.mean(values * values, -1, keepdims=True) + EPSILON) * gain


def project(flattened, weight_q, weight_k, weight_v):
    queries = jnp.dot(flattened, weight_q, preferred_element_type=jnp.float32).astype(jnp.bfloat16)
    key_rows = jnp.dot(flattened, weight_k, preferred_element_type=jnp.float32).astype(jnp.bfloat16)
    values = jnp.dot(flattened, weight_v, preferred_element_type=jnp.float32).astype(jnp.bfloat16)
    return (queries, key_rows, values)


def attention_core(queries, key_rows, values, seq_count, seq_length):
    head_count = queries.shape[1] // HEAD
    groups = key_rows.shape[1] // HEAD
    group_size = head_count // groups
    queries = queries.reshape(seq_count, seq_length, groups, group_size, HEAD)
    key_rows = key_rows.reshape(seq_count, seq_length, groups, HEAD)
    values = values.reshape(seq_count, seq_length, groups, HEAD)
    scores = jnp.einsum("bqgsd,bkgd->bgsqk", queries, key_rows, preferred_element_type=jnp.float32)
    scores = ATTN_CAP * jnp.tanh(scores / math.sqrt(HEAD) / ATTN_CAP)
    causal = jnp.arange(seq_length)[:, None] >= jnp.arange(seq_length)[None, :]
    masked = jnp.where(causal, scores, jnp.float32(MASKED))
    top = lax.stop_gradient(jnp.max(masked, -1, keepdims=True))
    expwts = jnp.where(causal, jnp.exp(masked - top), jnp.float32(0.0))
    probabilities = (expwts / jnp.sum(expwts, -1, keepdims=True)).astype(jnp.bfloat16)
    context = jnp.einsum(
        "bgsqk,bkgd->bqgsd", probabilities, values, preferred_element_type=jnp.float32
    )
    return context.astype(jnp.bfloat16).reshape(seq_count * seq_length, head_count * HEAD)


def attend(normed, weight_q, weight_k, weight_v, weight_o):
    seq_count, seq_length, feature_dim = normed.shape
    flattened = normed.reshape(seq_count * seq_length, feature_dim)
    queries, key_rows, values = project(flattened, weight_q, weight_k, weight_v)
    context = attention_core(queries, key_rows, values, seq_count, seq_length)
    return jnp.dot(context, weight_o, preferred_element_type=jnp.float32).reshape(
        seq_count, seq_length, feature_dim
    )


def label_logp(hidden, norm_gains, label_head):
    seq_count, seq_length, feature_dim = hidden.shape
    final_normed = rms_scale(hidden, norm_gains[1]).astype(jnp.bfloat16)
    logits = jnp.dot(
        final_normed.reshape(seq_count * seq_length, feature_dim),
        label_head,
        preferred_element_type=jnp.float32,
    )
    logits = LABEL_CAP * jnp.tanh(logits / LABEL_CAP)
    log_probs = logits - jnp.log(jnp.sum(jnp.exp(logits), -1, keepdims=True))
    return log_probs.reshape(seq_count, seq_length, label_head.shape[1])


def forward_logp(block_acts, weight_set, norm_gains, label_head):
    widened = block_acts.astype(jnp.float32)
    normed = rms_scale(widened, norm_gains[0]).astype(jnp.bfloat16)
    hidden = widened + attend(normed, weight_set[0], weight_set[1], weight_set[2], weight_set[3])
    return label_logp(hidden, norm_gains, label_head)


def token_losses(log_probs, peer_lp, block_labels):
    classes = jnp.arange(log_probs.shape[-1], dtype=jnp.int32)
    picked = jnp.sum(jnp.where(block_labels[..., None] == classes, log_probs, jnp.float32(0.0)), -1)
    diverge = jnp.sum(jnp.exp(peer_lp) * (peer_lp - log_probs), -1)
    return diverge - picked


def loss_parts(weight_set, block_acts, block_labels, peer_lp, norm_gains, label_head):
    log_probs = forward_logp(block_acts, weight_set, norm_gains, label_head)
    losses = token_losses(log_probs, peer_lp, block_labels)
    return (jnp.sum(losses) / losses.shape[1], losses)


def body(
    activations,
    labels,
    own_q,
    own_k,
    own_v,
    own_o,
    peer_q,
    peer_k,
    peer_v,
    peer_o,
    norm_gains,
    label_head,
):
    peer_parts = passed_along((peer_q, peer_k, peer_v, peer_o), "replica", 1)
    own_full = (
        lax.all_gather(own_q, "fsdp", axis=1, tiled=True),
        lax.all_gather(own_k, "fsdp", axis=1, tiled=True),
        lax.all_gather(own_v, "fsdp", axis=1, tiled=True),
        lax.all_gather(own_o, "fsdp", axis=1, tiled=True),
    )
    peer_full = (
        lax.all_gather(peer_parts[0], "fsdp", axis=1, tiled=True),
        lax.all_gather(peer_parts[1], "fsdp", axis=1, tiled=True),
        lax.all_gather(peer_parts[2], "fsdp", axis=1, tiled=True),
        lax.all_gather(peer_parts[3], "fsdp", axis=1, tiled=True),
    )
    own_set = tuple((weight[0] for weight in own_full))
    peer_set = tuple((weight[0] for weight in peer_full))
    block_acts = activations[0]
    block_labels = labels[0]
    peer_lp = forward_logp(block_acts, peer_set, norm_gains, label_head)
    loss_sum, pullback, losses = jax.vjp(
        lambda weight_set: loss_parts(
            weight_set, block_acts, block_labels, peer_lp, norm_gains, label_head
        ),
        own_set,
        has_aux=True,
    )
    (gradient,) = pullback(jnp.ones_like(loss_sum))
    gradient = lax.optimization_barrier(gradient)
    summed = (
        lax.psum_scatter(
            gradient[0].astype(jnp.float32).astype(jnp.bfloat16),
            "fsdp",
            scatter_dimension=0,
            tiled=True,
        ).astype(jnp.float32),
        lax.psum_scatter(
            gradient[1].astype(jnp.float32).astype(jnp.bfloat16),
            "fsdp",
            scatter_dimension=0,
            tiled=True,
        ).astype(jnp.float32),
        lax.psum_scatter(
            gradient[2].astype(jnp.float32).astype(jnp.bfloat16),
            "fsdp",
            scatter_dimension=0,
            tiled=True,
        ).astype(jnp.float32),
        lax.psum_scatter(
            gradient[3].astype(jnp.float32).astype(jnp.bfloat16),
            "fsdp",
            scatter_dimension=0,
            tiled=True,
        ).astype(jnp.float32),
    )
    return (losses[None], summed[0][None], summed[1][None], summed[2][None], summed[3][None])


def solution(mesh):
    placed = (
        P("replica", "fsdp", None, None),
        P("replica", "fsdp", None),
        P("replica", "fsdp", None),
        P("replica", "fsdp", None),
        P("replica", "fsdp", None),
        P("replica", "fsdp", None),
        P("replica", "fsdp", None),
        P("replica", "fsdp", None),
        P("replica", "fsdp", None),
        P("replica", "fsdp", None),
        P(),
        P(),
    )
    return jax.shard_map(
        body,
        mesh=mesh,
        in_specs=placed,
        out_specs=(
            P("replica", "fsdp", None),
            P("replica", "fsdp", None),
            P("replica", "fsdp", None),
            P("replica", "fsdp", None),
            P("replica", "fsdp", None),
        ),
        check_vma=False,
    )
```

profile of v0, /device:TPU:96, one launch (start us, length us, event | category | flops | bytes accessed | tf_op | source)
XLA Modules:
  0.0 807.3 jit_solution(3229070865511573617)
XLA Ops:
  9.0 5.6 collective-permute-done.1
  15.3 2.5 collective-permute-start
  17.8 3.0 collective-permute-done
  22.1 4.5 collective-permute-start.2
  26.6 4.6 collective-permute-done.2
  32.1 4.6 collective-permute-start.3
  36.6 4.6 collective-permute-done.3
  42.8 0.9 slice_reduce_fusion
  43.9 17.2 %all-gather.19.cloned.1.call-done = bf16[1,2304,512]{2,1,0:T(8,128)(2,1)} async-done(((bf16[1,144,512]{2,1,0:T(8,128)(2,1)}), bf16[1,2304,512]{2,1,0:T(8,128)(2,1)}) %all-gather.19.cloned.1.call-update) | async-done | bytes 2359312 | tf_op jit(solution)/shard_map/all_gather | solution.py:114
  61.1 2.5 fusion.53
  63.7 0.9 copy.37
  64.6 47.2 %all-gather.17.cloned.1.call-done = bf16[1,2304,512]{2,1,0:T(8,128)(2,1)} async-done(((bf16[1,144,512]{2,1,0:T(8,128)(2,1)}), bf16[1,2304,512]{2,1,0:T(8,128)(2,1)}) %all-gather.17.cloned.1.call-update) | async-done | bytes 2359312 | tf_op jit(solution)/shard_map/all_gather | solution.py:115
  111.7 2.5 fusion.50
  114.2 0.8 reshape.469
  115.0 47.9 %all-gather.11.cloned.1.call-done = bf16[1,2304,512]{2,1,0:T(8,128)(2,1)} async-done(((bf16[1,144,512]{2,1,0:T(8,128)(2,1)}), bf16[1,2304,512]{2,1,0:T(8,128)(2,1)}) %all-gather.11.cloned.1.call-update) | async-done | bytes 2359312 | tf_op jit(solution)/shard_map/all_gather | solution.py:120
  162.9 2.5 fusion.47
  165.4 0.8 reshape.465
  166.2 47.8 %all-gather.9.cloned.1.call-done = bf16[1,2304,512]{2,1,0:T(8,128)(2,1)} async-done(((bf16[1,144,512]{2,1,0:T(8,128)(2,1)}), bf16[1,2304,512]{2,1,0:T(8,128)(2,1)}) %all-gather.9.cloned.1.call-update) | async-done | bytes 2359312 | tf_op jit(solution)/shard_map/all_gather | solution.py:121
  213.9 2.5 fusion.44
  216.4 0.9 copy.41
  217.3 55.6 %all-gather.21.cloned.1.call-done = bf16[1,2304,1024]{2,1,0:T(8,128)(2,1)} async-done(((bf16[1,144,1024]{2,1,0:T(8,128)(2,1)}), bf16[1,2304,1024]{2,1,0:T(8,128)(2,1)}) %all-gather.21.cloned.1.call-update) | async-done | bytes 4718608 | tf_op jit(solution)/shard_map/all_gather | solution.py:113
  272.9 3.8 fusion.36
  276.9 55.6 %all-gather.13.cloned.1.call-done = bf16[1,2304,1024]{2,1,0:T(8,128)(2,1)} async-done(((bf16[1,144,1024]{2,1,0:T(8,128)(2,1)}), bf16[1,2304,1024]{2,1,0:T(8,128)(2,1)}) %all-gather.13.cloned.1.call-update) | async-done | bytes 4718608 | tf_op jit(solution)/shard_map/all_gather | solution.py:119
  332.5 4.6 fusion.33
  337.0 1.4 reshape.466
  338.5 1.4 fusion.132
  339.9 1.6 fusion.83
  342.0 50.2 %all-gather.15.cloned.1.call-done = bf16[1,1024,2304]{2,1,0:T(8,128)(2,1)} async-done(((bf16[1,64,2304]{2,1,0:T(8,128)(2,1)}), bf16[1,1024,2304]{2,1,0:T(8,128)(2,1)}) %all-gather.15.cloned.1.call-update) | async-done | bytes 4718608 | tf_op jit(solution)/shard_map/all_gather | solution.py:122
  392.2 3.9 multiply_reduce_fusion.2
  398.2 53.1 %all-gather.23.cloned.1.call-done = bf16[1,1024,2304]{2,1,0:T(8,128)(2,1)} async-done(((bf16[1,64,2304]{2,1,0:T(8,128)(2,1)}), bf16[1,1024,2304]{2,1,0:T(8,128)(2,1)}) %all-gather.23.cloned.1.call-update) | async-done | bytes 4718608 | tf_op jit(solution)/shard_map/all_gather | solution.py:116
  451.3 3.9 multiply_reduce_fusion.1
  455.3 0.9 exponential_reduce_fusion.1
  457.2 1.4 copy-done.4
  458.6 3.8 convolution_convert_fusion
  462.5 5.3 fusion.39
  470.0 0.8 fusion.56
  470.9 0.8 convolution_convert_fusion.6
  471.8 2.4 convolution_convert_fusion.2
  474.2 2.3 convolution_convert_fusion.3
  476.5 3.7 convolution_convert_fusion.1
  482.7 68.6 %reduce-scatter.9.cloned.1.call-done = bf16[144,512]{1,0:T(8,128)(2,1)} async-done(((bf16[2304,512]{1,0:T(8,128)(2,1)}), bf16[144,512]{1,0:T(8,128)(2,1)}) %reduce-scatter.9.cloned.1.call-update) | async-done | bytes 147472 | tf_op jit(solution)/shard_map/reduce_scatter | solution.py:151
  551.3 1.7 bitcast_convert_fusion.2
  552.9 73.5 %reduce-scatter.7.cloned.1.call-done = bf16[144,512]{1,0:T(8,128)(2,1)} async-done(((bf16[2304,512]{1,0:T(8,128)(2,1)}), bf16[144,512]{1,0:T(8,128)(2,1)}) %reduce-scatter.7.cloned.1.call-update) | async-done | bytes 147472 | tf_op jit(solution)/shard_map/reduce_scatter | solution.py:145
  626.4 1.7 bitcast_convert_fusion.3
  628.1 84.4 %reduce-scatter.11.cloned.1.call-done = bf16[64,2304]{1,0:T(8,128)(2,1)} async-done(((bf16[1024,2304]{1,0:T(8,128)(2,1)}), bf16[64,2304]{1,0:T(8,128)(2,1)}) %reduce-scatter.11.cloned.1.call-update) | async-done | bytes 294928 | tf_op jit(solution)/shard_map/reduce_scatter | solution.py:157
  712.5 1.8 bitcast_convert_fusion
  714.4 84.3 %reduce-scatter.5.cloned.1.call-done = bf16[144,1024]{1,0:T(8,128)(2,1)} async-done(((bf16[2304,1024]{1,0:T(8,128)(2,1)}), bf16[144,1024]{1,0:T(8,128)(2,1)}) %reduce-scatter.5.cloned.1.call-update) | async-done | bytes 294928 | tf_op jit(solution)/shard_map/reduce_scatter | solution.py:139
  798.6 1.8 bitcast_convert_fusion.1
  (85 shorter events, 14.8 us)
Async XLA Ops:
  7.2 389.0 %copy-start = (bf16[2304,256]{1,0:T(8,128)(2,1)S(1)}, bf16[2304,256]{1,0:T(8,128)(2,1)}, u32[]{:S(2)}) copy-start(bf16[2304,256]{1,0:T(8,128)(2,1)} %param.23) | copy-start | bytes 3538948
  7.2 36.4 %copy-start.2 = (bf16[1,1,256,2304]{3,2,1,0:T(8,128)(2,1)S(1)}, bf16[1,1,256,2304]{3,2,1,0:T(8,128)(2,1)}, u32[]{:S(2)}) copy-start(bf16[1,1,256,2304]{3,2,1,0:T(8,128)(2,1)} %param.12) | copy-start | bytes 3538948
  7.2 53.9 %all-gather.19.cloned.1.call-start = ((), (), s32[]{:S(2)}) async-start(), calls=%async_computation.9 | async-start | bytes 2506752 | tf_op jit(solution)/shard_map/all_gather | solution.py:114
  7.9 103.8 %all-gather.17.cloned.1.call-start = ((), (), s32[]{:S(2)}) async-start(), calls=%async_computation.8 | async-start | bytes 2506752 | tf_op jit(solution)/shard_map/all_gather | solution.py:115
  8.7 154.2 %all-gather.11.cloned.1.call-start = ((), (), s32[]{:S(2)}) async-start(), calls=%async_computation.5 | async-start | bytes 2506752 | tf_op jit(solution)/shard_map/all_gather | solution.py:120
  8.7 5.9 collective-permute-start.1
  14.6 0.7 copy-start.16
  15.3 198.7 %all-gather.9.cloned.1.call-start = ((), (), s32[]{:S(2)}) async-start(), calls=%async_computation.4 | async-start | bytes 2506752 | tf_op jit(solution)/shard_map/all_gather | solution.py:121
  15.3 5.5 collective-permute-start
  20.8 0.7 copy-start.17
  21.5 251.4 %all-gather.21.cloned.1.call-start = ((), (), s32[]{:S(2)}) async-start(), calls=%async_computation.10 | async-start | bytes 5013504 | tf_op jit(solution)/shard_map/all_gather | solution.py:113
  22.1 310.4 %all-gather.13.cloned.1.call-start = ((), (), s32[]{:S(2)}) async-start(), calls=%async_computation.6 | async-start | bytes 5013504 | tf_op jit(solution)/shard_map/all_gather | solution.py:119
  22.1 9.2 %collective-permute-start.2 = (bf16[1,144,1024]{2,1,0:T(8,128)(2,1)}, bf16[1,144,1024]{2,1,0:T(8,128)(2,1)S(1)}, u32[]{:S(2)}, u32[]{:S(2)}) collective-permute-start(bf16[1,144,1024]{2,1,0:T(8,128)(2,1)} %param.18), channel_id=1, source_target_pairs={{0,16},{16,32},{32,48},{48,64},{64,80},{80,96},{96,112},{112,0},{1... | collective-permute-start | bytes 884744 | tf_op jit(solution)/shard_map/ppermute | solution.py:20
  31.3 0.7 copy-start.10
  32.0 360.2 %all-gather.15.cloned.1.call-start = ((), (), s32[]{:S(2)}) async-start(), calls=%async_computation.7 | async-start | bytes 5013504 | tf_op jit(solution)/shard_map/all_gather | solution.py:122
  32.1 9.1 %collective-permute-start.3 = (bf16[1,64,2304]{2,1,0:T(8,128)(2,1)}, bf16[1,64,2304]{2,1,0:T(8,128)(2,1)S(1)}, u32[]{:S(2)}, u32[]{:S(2)}) collective-permute-start(bf16[1,64,2304]{2,1,0:T(8,128)(2,1)} %param.21), channel_id=1, source_target_pairs={{0,16},{16,32},{32,48},{48,64},{64,80},{80,96},{96,112},{112,0},{1... | collective-permute-start | bytes 884744 | tf_op jit(solution)/shard_map/ppermute | solution.py:20
  41.2 0.7 copy-start.9
  41.9 409.4 %all-gather.23.cloned.1.call-start = ((), (), s32[]{:S(2)}) async-start(), calls=%async_computation.11 | async-start | bytes 5013504 | tf_op jit(solution)/shard_map/all_gather | solution.py:116
  42.7 508.6 %reduce-scatter.9.cloned.1.call-start = ((), (), s32[]{:S(2)}) async-start(), calls=%async_computation.14 | async-start | bytes 2506752 | tf_op jit(solution)/shard_map/reduce_scatter | solution.py:151
  276.9 63.0 %copy-start.7 = (bf16[256,1024]{0,1:T(8,128)(2,1)}, bf16[256,1024]{0,1:T(8,128)(2,1)S(1)}, u32[]{:S(2)}) copy-start(bf16[256,1024]{0,1:T(8,128)(2,1)S(1)} %copy.53) | copy-start | bytes 1572868
  338.5 1.5 copy-start.11
  339.9 1.6 copy-start.15
  396.1 1.2 copy-start.5
  396.2 1.5 copy-start.13
  455.2 1.9 copy-start.3
  455.3 1.0 copy-start.18
  457.2 1.5 copy-start.4
  462.5 5.5 copy-start.6
  468.0 1.0 copy-start.14
  468.9 1.0 copy-start.8
  470.0 0.9 copy-start.12
  480.2 146.2 %reduce-scatter.7.cloned.1.call-start = ((), (), s32[]{:S(2)}) async-start(), calls=%async_computation.13 | async-start | bytes 2506752 | tf_op jit(solution)/shard_map/reduce_scatter | solution.py:145
  480.8 231.8 %reduce-scatter.11.cloned.1.call-start = ((), (), s32[]{:S(2)}) async-start(), calls=%async_computation.15 | async-start | bytes 5013504 | tf_op jit(solution)/shard_map/reduce_scatter | solution.py:157
  481.5 317.1 %reduce-scatter.5.cloned.1.call-start = ((), (), s32[]{:S(2)}) async-start(), calls=%async_computation.12 | async-start | bytes 5013504 | tf_op jit(solution)/shard_map/reduce_scatter | solution.py:139
  482.1 318.3 %copy-start.1 = (bf16[2304,256]{1,0:T(8,128)(2,1)S(1)}, bf16[2304,256]{1,0:T(8,128)(2,1)}, u32[]{:S(2)}) copy-start(bf16[2304,256]{1,0:T(8,128)(2,1)} %param.23) | copy-start | bytes 3538948
Sparse Core Ops, SparseCore 0:
  10.4 50.6 all-gather.18
  63.5 48.1 all-gather.16
  114.7 48.1 all-gather.10
  165.7 48.1 all-gather.8
  216.2 56.6 all-gather.20
  275.7 56.6 all-gather.12
  335.5 56.6 all-gather.14
  394.6 56.6 all-gather.22
  480.3 70.9 reduce-scatter.8
  555.1 71.2 reduce-scatter.6
  630.5 81.9 reduce-scatter.10
  717.0 81.5 reduce-scatter.4
where the time goes:
time: 809 us; the launch traced here: 807 us
  waiting for transfers between devices  708 us (88%)
  matrix products  52.7 us (7%)
  between operations  14.6 us (2%)
  starting transfers between devices  12.3 us (2%)
  local copies, waits for them, and re-layouts  11.7 us (1%)
  other arithmetic  8.34 us (1%)
    reduce_scatter x1, waiting for transfers between devices, body(): lax.psum_scatter(gradient[3].astype(jnp.float32).astype(jnp.bfloat16), 'f...  84.4 us
    reduce_scatter x1, waiting for transfers between devices, body(): lax.psum_scatter(gradient[0].astype(jnp.float32).astype(jnp.bfloat16), 'f...  84.3 us
    reduce_scatter x1, waiting for transfers between devices, body(): lax.psum_scatter(gradient[1].astype(jnp.float32).astype(jnp.bfloat16), 'f...  73.5 us
    reduce_scatter x1, waiting for transfers between devices, body(): lax.psum_scatter(gradient[2].astype(jnp.float32).astype(jnp.bfloat16), 'f...  68.6 us
    all_gather x1, waiting for transfers between devices, body(): lax.all_gather(own_q, 'fsdp', axis=1, tiled=True)  55.6 us
    all_gather x1, waiting for transfers between devices, body(): lax.all_gather(peer_parts[0], 'fsdp', axis=1, tiled=True)  55.6 us
    all_gather x1, waiting for transfers between devices, body(): lax.all_gather(own_o, 'fsdp', axis=1, tiled=True)  53.1 us
    all_gather x1, waiting for transfers between devices, body(): lax.all_gather(peer_parts[3], 'fsdp', axis=1, tiled=True)  50.2 us
  transfers between devices with their start and end apart: 16, of which 16 were waited for; matrix products, arithmetic and copies ran while one was open for 5% of the time, Pallas kernels for 0%

commit v1 on v0

v1 whole, which is shorter than its diff:
```python
import functools
import math

import jax
import jax.numpy as jnp
from jax import lax
from jax.experimental import pallas as pl
from jax.experimental.pallas import tpu as pltpu
from jax.sharding import PartitionSpec as P

SEQ, D, HEAD, HQ, HK, LABELS = 256, 2304, 256, 4, 2, 256
QKV_PANELS, O_PANELS = 8, 9
QKV_ROWS, O_ROWS = 144, 64
THIRD = 576
PACKED = 3 * THIRD
EPSILON = 1e-06
ATTN_CAP = 50.0
LABEL_CAP = 30.0
MASKED = -1e30
VMEM_LIMIT = 56 * 1024 * 1024
F32, BF16 = jnp.float32, jnp.bfloat16

N_FSDP = 16


def moved(value, target):
    return lax.ppermute(value, "fsdp", [(i, target(i)) for i in range(N_FSDP)])


def to_core(i):
    return i ^ 1


def to_y(i):
    return i ^ 2


def to_next_x(i):
    return (i + 4) % N_FSDP


def to_prev_x(i):
    return (i - 4) % N_FSDP


together = lax.optimization_barrier


def pack(w_q, w_k, w_v, w_o):
    panels = [w_q[:, HEAD * p : HEAD * (p + 1)] for p in range(4)]
    panels += [w_k[:, HEAD * p : HEAD * (p + 1)] for p in range(2)]
    panels += [w_v[:, HEAD * p : HEAD * (p + 1)] for p in range(2)]
    panels += [w_o[:, HEAD * p : HEAD * (p + 1)] for p in range(O_PANELS)]
    return jnp.concatenate(panels, 0)


def across_chips(shard):
    y0 = moved(shard, to_y)
    a1 = moved(shard, to_prev_x)
    a3 = moved(shard, to_next_x)
    return y0, a1, a3


def second_step(y0, a1, a3):
    return moved(a1, to_y), moved(y0, to_next_x), moved(a1, to_prev_x)


def third_step(o1, o3, a2):
    return (
        moved(a2[:THIRD], to_y),
        moved(o3[THIRD : 2 * THIRD], to_next_x),
        moved(o1[2 * THIRD :], to_prev_x),
    )


def whole(dx, dy):
    return (0, dx, dy, 0, 0, 3)


def swapped(arrays, metas):
    joined = jnp.concatenate(arrays, 0)
    met, row = [], 0
    for array, meta in zip(arrays, metas):
        for _, dx, dy, _, first, count in meta:
            met.append((row, dx, dy, 1, first, count))
        row += array.shape[0]
    return moved(joined, to_core), met


META = {
    "shard": [whole(0, 0)],
    "y0": [whole(0, 1)],
    "a1": [whole(1, 0)],
    "a3": [whole(3, 0)],
    "o1": [whole(1, 1)],
    "o3": [whole(3, 1)],
    "a2": [whole(2, 0)],
    "oA": [(0, 2, 1, 0, 0, 1)],
    "oB": [(0, 2, 1, 0, 1, 1)],
    "oC": [(0, 2, 1, 0, 2, 1)],
}


def rms(values, gain):
    mean = jnp.sum(values * values, -1, keepdims=True) * (1.0 / D)
    return values * lax.rsqrt(mean + EPSILON) * gain


def load_weights(position, metas, pieces, wqkv, wo, sems):
    x = position // 4
    y = (position // 2) % 2
    core = position % 2
    for ref, meta in zip(pieces, metas):
        for row, dx, dy, dc, first, count in meta:
            owner = ((x + dx) % 4) * 4
            owner = owner + (y if dy == 0 else 1 - y) * 2
            owner = owner + (core if dc == 0 else 1 - core)
            for third in range(first, first + count):
                at = row + THIRD * (third - first)
                if third < 2:
                    rows = pl.ds(pl.multiple_of(owner * QKV_ROWS, 16), QKV_ROWS)
                    for p in range(4):
                        pltpu.make_async_copy(
                            ref.at[pl.ds(at + QKV_ROWS * p, QKV_ROWS)],
                            wqkv.at[4 * third + p, rows],
                            sems.at[0],
                        ).start()
                else:
                    rows = pl.ds(pl.multiple_of(owner * O_ROWS, 16), O_ROWS)
                    for p in range(O_PANELS):
                        pltpu.make_async_copy(
                            ref.at[pl.ds(at + O_ROWS * p, O_ROWS)],
                            wo.at[p, rows],
                            sems.at[1],
                        ).start()


def wait_for(ref, sem):
    pltpu.make_async_copy(ref, ref, sem).wait()


def causal_mask():
    row = lax.broadcasted_iota(jnp.int32, (SEQ, SEQ), 0)
    col = lax.broadcasted_iota(jnp.int32, (SEQ, SEQ), 1)
    return row >= col


def nt(a, b):
    return lax.dot_general(a, b, (((1,), (1,)), ((), ())), preferred_element_type=F32)


def tn(a, b):
    return lax.dot_general(a, b, (((0,), (0,)), ((), ())), preferred_element_type=F32)


def nn(a, b):
    return jnp.dot(a, b, preferred_element_type=F32)


def probabilities(query, key, causal):
    capped = jnp.tanh(nt(query, key) * (1.0 / (math.sqrt(HEAD) * ATTN_CAP)))
    scores = jnp.where(causal, ATTN_CAP * capped, MASKED)
    top = jnp.max(scores, -1, keepdims=True)
    weights = jnp.where(causal, jnp.exp(scores - top), 0.0)
    return weights / jnp.sum(weights, -1, keepdims=True), capped


def layer(x_ref, gains_ref, head_ref, normed, qkv, context, hidden, wqkv, wo, sems):
    normed[...] = rms(x_ref[...].astype(F32), gains_ref[0:1, :]).astype(BF16)
    wait_for(wqkv, sems.at[0])

    def one_panel(p, carry):
        qkv[p] = nn(normed[...], wqkv[p]).astype(BF16)
        return carry

    lax.fori_loop(0, QKV_PANELS, one_panel, 0)
    causal = causal_mask()
    for h in range(HQ):
        group = h // (HQ // HK)
        probs, _ = probabilities(qkv[h], qkv[HQ + group], causal)
        context[:, HEAD * h : HEAD * (h + 1)] = nn(
            probs.astype(BF16), qkv[HQ + HK + group]
        ).astype(BF16)
    wait_for(wo, sems.at[1])

    def one_out(p, carry):
        cols = pl.ds(pl.multiple_of(p * HEAD, HEAD), HEAD)
        hidden[:, cols] = x_ref[:, cols].astype(F32) + nn(context[...], wo[p])
        return carry

    lax.fori_loop(0, O_PANELS, one_out, 0)
    final = rms(hidden[...], gains_ref[1:2, :]).astype(BF16)
    logits = LABEL_CAP * jnp.tanh(nn(final, head_ref[...]) * (1.0 / LABEL_CAP))
    return logits, logits - jnp.log(jnp.sum(jnp.exp(logits), -1, keepdims=True))


def own_kernel(metas, pos_ref, x_ref, gains_ref, head_ref, *refs):
    pieces, refs = refs[: len(metas)], refs[len(metas) :]
    nsel, csel, qkv, hidden, logits, wo, normed, context, wqkv, sems = refs
    load_weights(pos_ref[0], metas, pieces, wqkv, wo, sems)
    out, _ = layer(x_ref, gains_ref, head_ref, normed, qkv, context, hidden, wqkv, wo, sems)
    logits[...] = out
    for core in range(2):
        for chip in range(8):
            at = QKV_ROWS * (2 * chip + core)
            nsel[core, :, QKV_ROWS * chip : QKV_ROWS * (chip + 1)] = normed[:, at : at + QKV_ROWS]
            at = O_ROWS * (2 * chip + core)
            csel[core, :, O_ROWS * chip : O_ROWS * (chip + 1)] = context[:, at : at + O_ROWS]


def peer_kernel(metas, pos_ref, x_ref, gains_ref, head_ref, labels_ref, own_logits, own_hidden, *refs):
    pieces, refs = refs[: len(metas)], refs[len(metas) :]
    loss, dhidden, normed, qkv, context, hidden, wqkv, wo, sems = refs
    load_weights(pos_ref[0], metas, pieces, wqkv, wo, sems)
    _, peer_lp = layer(x_ref, gains_ref, head_ref, normed, qkv, context, hidden, wqkv, wo, sems)
    logits = own_logits[...]
    own_lp = logits - jnp.log(jnp.sum(jnp.exp(logits), -1, keepdims=True))
    peer = jnp.exp(peer_lp)
    hot = labels_ref[...] == lax.broadcasted_iota(jnp.int32, (SEQ, LABELS), 1)
    picked = jnp.sum(jnp.where(hot, own_lp, 0.0), -1, keepdims=True)
    loss[...] = jnp.sum(peer * (peer_lp - own_lp), -1, keepdims=True) - picked
    d_lp = (jnp.where(hot, 1.0, 0.0) + peer) * (-1.0 / SEQ)
    d_logits = d_lp - jnp.exp(own_lp) * jnp.sum(d_lp, -1, keepdims=True)
    capped = logits * (1.0 / LABEL_CAP)
    d_raw = (d_logits * (1.0 - capped * capped)).astype(BF16)
    d_final = nt(d_raw, head_ref[...]).astype(BF16).astype(F32) * gains_ref[1:2, :]
    own = own_hidden[...]
    scale = lax.rsqrt(jnp.sum(own * own, -1, keepdims=True) * (1.0 / D) + EPSILON)
    along = jnp.sum(d_final * own, -1, keepdims=True) * (1.0 / D)
    dhidden[...] = (d_final * scale - own * (scale * scale * scale * along)).astype(BF16)


def attention_back_kernel(dhidden, wo, qkv, dqkv, dcontext):
    dcontext[...] = jnp.zeros_like(dcontext)

    def one_panel(p, carry):
        cols = pl.ds(pl.multiple_of(p * HEAD, HEAD), HEAD)
        dcontext[...] += nt(dhidden[:, cols], wo[p])
        return carry

    lax.fori_loop(0, O_PANELS, one_panel, 0)
    causal = causal_mask()
    for group in range(HK):
        key, value = qkv[HQ + group], qkv[HQ + HK + group]
        d_key = jnp.zeros((SEQ, HEAD), F32)
        d_value = jnp.zeros((SEQ, HEAD), F32)
        for h in range(group * (HQ // HK), (group + 1) * (HQ // HK)):
            query = qkv[h]
            probs, capped = probabilities(query, key, causal)
            d_out = dcontext[:, HEAD * h : HEAD * (h + 1)].astype(BF16)
            d_value += tn(probs.astype(BF16), d_out)
            d_probs = nt(d_out, value).astype(BF16).astype(F32)
            d_scores = probs * (d_probs - jnp.sum(d_probs * probs, -1, keepdims=True))
            d_raw = (d_scores * (1.0 - capped * capped) * (1.0 / math.sqrt(HEAD))).astype(BF16)
            dqkv[h] = nn(d_raw, key).astype(BF16)
            d_key += tn(d_raw, query)
        dqkv[HQ + group] = d_key.astype(BF16)
        dqkv[HQ + HK + group] = d_value.astype(BF16)


CHIPS = [(0, 0), (1, 0), (2, 0), (3, 0), (0, 1), (1, 1), (2, 1), (3, 1)]


def chip_index(position, dx, dy):
    x = position // 4
    y = (position // 2) % 2
    return ((x + dx) % 4) * 2 + (y if dy == 0 else 1 - y)


def out_grad_kernel(pos_ref, mine, other, d_mine, d_other, *refs):
    outs, lhs = refs[:8], refs[8]
    lhs[:, 0:SEQ] = mine[...].T
    lhs[:, SEQ : 2 * SEQ] = other[...].T
    for out, (dx, dy) in zip(outs, CHIPS):
        rows = pl.ds(pl.multiple_of(chip_index(pos_ref[0], dx, dy) * O_ROWS, 16), O_ROWS)

        def one_panel(p, carry, out=out, rows=rows):
            cols = pl.ds(pl.multiple_of(p * HEAD, HEAD), HEAD)
            total = nn(lhs[rows, 0:SEQ], d_mine[:, cols])
            total += nn(lhs[rows, SEQ : 2 * SEQ], d_other[:, cols])
            out[pl.ds(pl.multiple_of(p * O_ROWS, 16), O_ROWS)] = total.astype(BF16)
            return carry

        lax.fori_loop(0, O_PANELS, one_panel, 0)


def qkv_grad_kernel(pos_ref, mine, other, d_mine, d_other, *refs):
    outs, lhs = refs[:8], refs[8]
    lhs[:, 0:SEQ] = mine[...].T
    lhs[:, SEQ : 2 * SEQ] = other[...].T
    for out, (dx, dy) in zip(outs, CHIPS):
        rows = pl.ds(pl.multiple_of(chip_index(pos_ref[0], dx, dy) * QKV_ROWS, 16), QKV_ROWS)

        def one_panel(p, carry, out=out, rows=rows):
            total = nn(lhs[rows, 0:SEQ], d_mine[p])
            total += nn(lhs[rows, SEQ : 2 * SEQ], d_other[p])
            out[pl.ds(pl.multiple_of(p * QKV_ROWS, 16), QKV_ROWS)] = total.astype(BF16)
            return carry

        lax.fori_loop(0, QKV_PANELS, one_panel, 0)


SMEM = pl.BlockSpec(memory_space=pltpu.SMEM)
VMEM = pl.BlockSpec(memory_space=pltpu.VMEM)
ANY = pl.BlockSpec(memory_space=pl.ANY)


def cost(flops, moved_bytes):
    return pl.CostEstimate(flops=flops, bytes_accessed=moved_bytes, transcendentals=0)


def shape(dims, kind=BF16):
    return jax.ShapeDtypeStruct(dims, kind)


def weight_scratch():
    return [
        pltpu.VMEM((QKV_PANELS, D, HEAD), BF16),
    ]


PARAMS = pltpu.CompilerParams(vmem_limit_bytes=VMEM_LIMIT)


def own_pass(position, x, gains, head, arrays, metas):
    return pl.pallas_call(
        functools.partial(own_kernel, metas),
        out_shape=[
            shape((2, SEQ, D // 2)),
            shape((2, SEQ, HQ * HEAD // 2)),
            shape((QKV_PANELS, SEQ, HEAD)),
            shape((SEQ, D), F32),
            shape((SEQ, LABELS), F32),
            shape((O_PANELS, HQ * HEAD, HEAD)),
        ],
        in_specs=[SMEM, VMEM, VMEM, VMEM] + [ANY] * len(arrays),
        out_specs=[VMEM] * 6,
        scratch_shapes=[
            pltpu.VMEM((SEQ, D), BF16),
            pltpu.VMEM((SEQ, HQ * HEAD), BF16),
            pltpu.VMEM((QKV_PANELS, D, HEAD), BF16),
            pltpu.SemaphoreType.DMA((2,)),
        ],
        compiler_params=PARAMS,
        cost_estimate=cost(4_000_000_000, 40_000_000),
        name="own_pass",
    )(position, x, gains, head, *arrays)


def peer_pass(position, x, gains, head, labels, own_logits, own_hidden, arrays, metas):
    return pl.pallas_call(
        functools.partial(peer_kernel, metas),
        out_shape=[shape((SEQ, 1), F32), shape((SEQ, D))],
        in_specs=[SMEM] + [VMEM] * 6 + [ANY] * len(arrays),
        out_specs=[VMEM] * 2,
        scratch_shapes=[
            pltpu.VMEM((SEQ, D), BF16),
            pltpu.VMEM((QKV_PANELS, SEQ, HEAD), BF16),
            pltpu.VMEM((SEQ, HQ * HEAD), BF16),
            pltpu.VMEM((SEQ, D), F32),
            pltpu.VMEM((QKV_PANELS, D, HEAD), BF16),
            pltpu.VMEM((O_PANELS, HQ * HEAD, HEAD), BF16),
            pltpu.SemaphoreType.DMA((2,)),
        ],
        compiler_params=PARAMS,
        cost_estimate=cost(4_000_000_000, 40_000_000),
        name="peer_pass",
    )(position, x, gains, head, labels, own_logits, own_hidden, *arrays)


def attention_back(dhidden, wo, qkv):
    return pl.pallas_call(
        attention_back_kernel,
        out_shape=shape((QKV_PANELS, SEQ, HEAD)),
        in_specs=[VMEM] * 3,
        out_specs=VMEM,
        scratch_shapes=[pltpu.VMEM((SEQ, HQ * HEAD), F32)],
        compiler_params=PARAMS,
        cost_estimate=cost(2_000_000_000, 16_000_000),
        name="attention_back",
    )(dhidden, wo, qkv)


def weight_grads(kernel, rows, panels, position, mine, other, d_mine, d_other, name):
    return pl.pallas_call(
        kernel,
        out_shape=[shape((rows * panels, HEAD))] * 8,
        in_specs=[SMEM] + [VMEM] * 4,
        out_specs=[VMEM] * 8,
        scratch_shapes=[pltpu.VMEM((8 * rows, 2 * SEQ), BF16)],
        compiler_params=PARAMS,
        cost_estimate=cost(2 * 8 * rows * 2 * SEQ * panels * HEAD, 10_000_000),
        name=name,
    )(position, mine, other, d_mine, d_other)


def added(first, *others):
    total = first.astype(F32)
    for value in others:
        total = total + value.astype(F32)
    return total


def reduce_scattered(blocks):
    s0, a1, a2, a3, o0, o1, o2, o3 = blocks
    t = o2.shape[0] // 3
    in_a, in_b, in_c = together(
        (
            moved(o2[:t], to_y),
            moved(o2[t : 2 * t], to_prev_x),
            moved(o2[2 * t :], to_next_x),
        )
    )
    a2 = jnp.concatenate([added(a2[:t], in_a).astype(BF16), a2[t:]], 0)
    o3 = jnp.concatenate([o3[:t], added(o3[t : 2 * t], in_b).astype(BF16), o3[2 * t :]], 0)
    o1 = jnp.concatenate([o1[: 2 * t], added(o1[2 * t :], in_c).astype(BF16)], 0)
    in_a1, in_o0, in_a1y = together(
        (moved(a2, to_next_x), moved(o3, to_prev_x), moved(o1, to_y))
    )
    a1 = added(a1, in_a1, in_a1y).astype(BF16)
    o0 = added(o0, in_o0).astype(BF16)
    last = together((moved(a1, to_next_x), moved(a3, to_prev_x), moved(o0, to_y)))
    return added(s0, *last)


def body(
    activations,
    labels,
    own_q,
    own_k,
    own_v,
    own_o,
    peer_q,
    peer_k,
    peer_v,
    peer_o,
    norm_gains,
    label_head,
):
    me = lax.axis_index("fsdp")
    core = me % 2
    position = me.astype(jnp.int32).reshape(1)
    x = activations[0, 0]

    own = pack(own_q[0], own_k[0], own_v[0], own_o[0])
    peer = pack(peer_q[0], peer_k[0], peer_v[0], peer_o[0])
    replicas = lax.axis_size("replica")
    peer = lax.ppermute(peer, "replica", [(i, (i + 1) % replicas) for i in range(replicas)])

    y0, a1, a3, own = together((*across_chips(own), own))
    o1, o3, a2 = together(second_step(y0, a1, a3))
    oA, oB, oC, peer = together((*third_step(o1, o3, a2), peer))
    names = ["shard", "y0", "a1", "a3", "o1", "o3", "a2", "oA", "oB", "oC"]
    arrays = [own, y0, a1, a3, o1, o3, a2, oA, oB, oC]
    metas = [META[n] for n in names]
    swap, met = swapped(arrays, metas)

    y0, a1, a3, peer, swap = together((*across_chips(peer), peer, swap))
    nsel, csel, qkv, hidden, logits, wo = own_pass(
        position, x, norm_gains, label_head, arrays + [swap], metas + [met]
    )
    n_mine = lax.dynamic_index_in_dim(nsel, core, 0, keepdims=False)
    n_other = moved(lax.dynamic_index_in_dim(nsel, 1 - core, 0, keepdims=False), to_core)
    c_mine = lax.dynamic_index_in_dim(csel, core, 0, keepdims=False)
    c_other = moved(lax.dynamic_index_in_dim(csel, 1 - core, 0, keepdims=False), to_core)

    swap1, met1 = swapped([peer, y0, a1, a3], [META[n] for n in names[:4]])
    o1, o3, a2, swap1 = together((*second_step(y0, a1, a3), swap1))
    swap2, met2 = swapped([o1, o3, a2], [META[n] for n in names[4:7]])
    oA, oB, oC, swap2 = together((*third_step(o1, o3, a2), swap2))
    swap3, met3 = swapped([oA, oB, oC], [META[n] for n in names[7:]])
    n_other, c_other, swap3 = together((n_other, c_other, swap3))

    loss, dhidden = peer_pass(
        position,
        x,
        norm_gains,
        label_head,
        labels[0, 0].reshape(SEQ, 1),
        logits,
        hidden,
        [peer, y0, a1, a3, o1, o3, a2, oA, oB, oC, swap1, swap2, swap3],
        metas + [met1, met2, met3],
    )
    d_other = moved(dhidden, to_core)
    dqkv = attention_back(dhidden, wo, qkv)
    out_blocks = weight_grads(
        out_grad_kernel, O_ROWS, O_PANELS, position, c_mine, c_other, dhidden, d_other, "out_grads"
    )
    dqkv_other = moved(dqkv, to_core)
    qkv_blocks = weight_grads(
        qkv_grad_kernel, QKV_ROWS, QKV_PANELS, position, n_mine, n_other, dqkv, dqkv_other, "qkv_grads"
    )
    grad_out = reduce_scattered(out_blocks).reshape(O_PANELS, O_ROWS, HEAD)
    grad_qkv = reduce_scattered(qkv_blocks).reshape(QKV_PANELS, QKV_ROWS, HEAD)

    def side_by_side(panels):
        return jnp.concatenate([panels[p] for p in range(panels.shape[0])], -1)[None]

    return (
        loss.reshape(1, 1, SEQ),
        side_by_side(grad_qkv[0:4]),
        side_by_side(grad_qkv[4:6]),
        side_by_side(grad_qkv[6:8]),
        side_by_side(grad_out),
    )


def solution(mesh):
    weights = P("replica", "fsdp", None)
    return jax.shard_map(
        body,
        mesh=mesh,
        in_specs=(P("replica", "fsdp", None, None), weights, *([weights] * 8), P(), P()),
        out_specs=(weights,) * 5,
        check_vma=False,
    )
```

time: 809 us -> 328 us (0.41)
  waiting for transfers between devices: 708 us -> 125 us
  Pallas kernels: 0 us -> 78.7 us
  matrix products: 52.7 us -> 0 us
  starting transfers between devices: 12.3 us -> 57.4 us
  local copies, waits for them, and re-layouts: 11.7 us -> 44.7 us
  between operations: 14.6 us -> 1.35 us
  other arithmetic: 8.34 us -> 17.8 us
    all_gather x8 -> x0, waiting for transfers between devices: 375 us -> none  [the longest x1 55.6 us: body(): lax.all_gather(own_q, 'fsdp', axis=1, tiled=True)]
    reduce_scatter x4 -> x0, waiting for transfers between devices: 311 us -> none  [the longest x1 84.4 us: body(): lax.psum_scatter(gradient[3].astype(jnp.float32).astype(jnp.bfloat16), 'f...]
    ppermute x4 -> x45, waiting for transfers between devices: 17.8 us -> 125 us  [the longest x44 125 us: moved(): return lax.ppermute(value, 'fsdp', [(i, target(i)) for i in range(N_FSDP)])]
    pallas_call x0 -> x5, Pallas kernels: none -> 78.7 us  [the longest x2 33.1 us: weight_grads(): pl.pallas_call(kernel, out_shape=[shape((rows * panels, HEAD))] * 8, in_s...]
    dot_general x24 -> x0, matrix products: 52.7 us -> none  [the longest x4 16.9 us: attend(): jnp.dot(context, weight_o, preferred_element_type=jnp.float32)]
    ppermute x4 -> x45, starting transfers between devices: 11.8 us -> 57.4 us  [the longest x44 57.4 us: moved(): return lax.ppermute(value, 'fsdp', [(i, target(i)) for i in range(N_FSDP)])]
    unnamed x38 -> x115, local copies, waits for them, and re-layouts: 5.7 us -> 30.2 us
    convert_element_type x0 -> x10, other arithmetic: none -> 9.72 us  [the longest x2 2.77 us: reduce_scattered(): a1 = added(a1, in_a1, in_a1y).astype(BF16)]
  transfers between devices with their start and end apart: 16 -> 45, of which waited for: 16 -> 20; matrix products, arithmetic and copies ran while one was open for 5% -> 12% of each run, Pallas kernels for 0% -> 16%
where the time goes in v1:
time: 328 us; the launch traced here: 325 us
  waiting for transfers between devices  125 us (38%)
  Pallas kernels  78.7 us (24%)
  starting transfers between devices  57.4 us (18%)
  local copies, waits for them, and re-layouts  44.7 us (14%)
  other arithmetic  17.8 us (5%)
    ppermute x44, waiting for transfers between devices, moved(): return lax.ppermute(value, 'fsdp', [(i, target(i)) for i in range(N_FSDP)])  125 us
    ppermute x44, starting transfers between devices, moved(): return lax.ppermute(value, 'fsdp', [(i, target(i)) for i in range(N_FSDP)])  57.4 us
    pallas_call x2, Pallas kernels, weight_grads(): pl.pallas_call(kernel, out_shape=[shape((rows * panels, HEAD))] * 8, in_s...  33.1 us
    unnamed x115, local copies, waits for them, and re-layouts  30.2 us
    pallas_call x1, Pallas kernels, peer_pass(): pl.pallas_call(functools.partial(peer_kernel, metas), out_shape=[shape((S...  18.6 us
    pallas_call x1, Pallas kernels, own_pass(): pl.pallas_call(functools.partial(own_kernel, metas), out_shape=[shape((2,...  18.1 us
    pallas_call x1, Pallas kernels, attention_back(): pl.pallas_call(attention_back_kernel, out_shape=shape((QKV_PANELS, SEQ, H...  8.97 us
  transfers between devices with their start and end apart: 45, of which 20 were waited for; matrix products, arithmetic and copies ran while one was open for 12% of the time, Pallas kernels for 16%

profile of v1, /device:TPU:96, one launch (start us, length us, event | category | flops | bytes accessed | tf_op | source)
XLA Modules:
  0.0 324.9 jit_solution(505801866810585084)
XLA Ops:
  14.6 3.2 collective-permute-start
  17.8 2.8 collective-permute-start.1
  34.5 4.1 %collective-permute-done.refs_1_ = bf16[1728,256]{1,0:T(8,128)(2,1)S(1)} collective-permute-done((bf16[1728,256]{1,0:T(8,128)(2,1)S(1)}, bf16[1728,256]{1,0:T(8,128)(2,1)S(1)}, u32[]{:S(2)}, u32[]{:S(2)}) %collective-permute-start) | collective-permute-done | bytes 884768 | tf_op jit(solution)/shard_map/ppermute | solution.py:27
  39.2 3.4 %collective-permute-done.2.refs_3_ = bf16[1728,256]{1,0:T(8,128)(2,1)S(1)} collective-permute-done((bf16[1728,256]{1,0:T(8,128)(2,1)S(1)}, bf16[1728,256]{1,0:T(8,128)(2,1)S(1)}, u32[]{:S(2)}, u32[]{:S(2)}) %collective-permute-start.2) | collective-permute-done | bytes 884768 | tf_op jit(solution)/shard_map/ppermute | solution.py:27
  42.9 1.8 collective-permute-start.5
  45.3 30.2 %collective-permute-done.3.refs_4_ = bf16[1728,256]{1,0:T(8,128)(2,1)S(1)} collective-permute-done((bf16[1728,256]{1,0:T(8,128)(2,1)S(1)}, bf16[1728,256]{1,0:T(8,128)(2,1)S(1)}, u32[]{:S(2)}, u32[]{:S(2)}) %collective-permute-start.3) | collective-permute-done | bytes 884768 | tf_op jit(solution)/shard_map/ppermute | solution.py:27
  75.5 3.3 %collective-permute-start.6 = (bf16[576,256]{1,0:T(8,128)(2,1)S(1)}, bf16[576,256]{1,0:T(8,128)(2,1)S(1)}, u32[]{:S(2)}, u32[]{:S(2)}) collective-permute-start(bf16[576,256]{1,0:T(8,128)(2,1)S(1)} %slice.279), channel_id=1, source_target_pairs={{0,2},{1,3},{2,0},{3,1},{4,6},{5,7},{6,4},{7,5},{8,10},{9,11},{10,... | collective-permute-start | bytes 884744 | tf_op jit(solution)/shard_map/ppermute | solution.py:27
  78.8 1.6 collective-permute-start.7
  80.3 1.8 collective-permute-start.8
  82.4 2.5 collective-permute-done.6.refs_7_
  84.9 2.7 collective-permute-done.7.refs_8_
  88.4 2.9 collective-permute-start.11
  91.3 20.2 %collective-permute-done.10.refs_1_ = bf16[1728,256]{1,0:T(8,128)(2,1)S(1)} collective-permute-done((bf16[1728,256]{1,0:T(8,128)(2,1)S(1)}, bf16[1728,256]{1,0:T(8,128)(2,1)S(1)}, u32[]{:S(2)}, u32[]{:S(2)}) %collective-permute-start.10) | collective-permute-done | bytes 884768 | tf_op jit(solution)/shard_map/ppermute | solution.py:27
  111.5 2.4 collective-permute-done.12.refs_3_
  114.9 3.2 collective-permute-start.14
  118.1 3.2 collective-permute-start.16
  121.3 17.1 %collective-permute-done.14.refs_4_ = bf16[1728,256]{1,0:T(8,128)(2,1)S(1)} collective-permute-done((bf16[1728,256]{1,0:T(8,128)(2,1)S(1)}, bf16[1728,256]{1,0:T(8,128)(2,1)S(1)}, u32[]{:S(2)}, u32[]{:S(2)}) %collective-permute-start.14) | collective-permute-done | bytes 884768 | tf_op jit(solution)/shard_map/ppermute | solution.py:27
  138.4 2.6 collective-permute-done.15.refs_5_
  141.1 1.9 pad_maximum_fusion.1
  144.0 3.2 collective-permute-start.20
  147.2 6.8 %collective-permute-done.18.refs_7_ = bf16[576,256]{1,0:T(8,128)(2,1)S(1)} collective-permute-done((bf16[576,256]{1,0:T(8,128)(2,1)S(1)}, bf16[576,256]{1,0:T(8,128)(2,1)S(1)}, u32[]{:S(2)}, u32[]{:S(2)}) %collective-permute-start.18) | collective-permute-done | bytes 294944 | tf_op jit(solution)/shard_map/ppermute | solution.py:27
  154.5 18.1 %own_pass.1 = (bf16[2,256,1152]{2,1,0:T(8,128)(2,1)}, bf16[2,256,512]{2,1,0:T(8,128)(2,1)}, bf16[8,256,256]{2,1,0:T(8,128)(2,1)}, f32[256,2304]{1,0:T(8,128)}, f...) custom-call(s32[1]{0:T(128)} %bitcast.pos_ref, bf16[256,2304]{1,0:T(8,128)(2,1)} %bitcast.27, f32[2,2304]{1,0:T(2,128)} %gains_ref.3, ...), custom_call_target="tpu_custom_call" | custom-call | flops 4000000000 | bytes 40000000 | tf_op jit(solution)/shard_map/own_pass/pallas_call | solution.py:326
  172.6 2.2 dynamic-slice_bitcast_fusion
  175.2 1.8 dynamic-slice_bitcast_fusion.2
  179.5 18.6 %peer_pass.1 = (f32[256,1]{1,0:T(8,128)}, bf16[256,2304]{1,0:T(8,128)(2,1)}) custom-call(s32[1]{0:T(128)} %bitcast.pos_ref, bf16[256,2304]{1,0:T(8,128)(2,1)} %bitcast.28, f32[2,2304]{1,0:T(2,128)} %gains_ref.3, bf16[2304,256]{1,0:T(8,128)(2,1)} %head_ref.3, s32[256,1]{1,0:T(8,128)} %copy.17.labels_ref, f32[256,256]{1,0:T(8,128)} %get-tuple-element.86.own_logits, ...), custom_call_target="tpu_custom_call" | custom-call | flops 4000000000 | bytes 40000000 | tf_op jit(solution)/shard_map/peer_pass/pallas_call | solution.py:351
  198.0 9.0 %attention_back.1.d_mine = bf16[8,256,256]{2,1,0:T(8,128)(2,1)} custom-call(bf16[256,2304]{1,0:T(8,128)(2,1)} %get-tuple-element.105.dhidden.d_mine, bf16[9,1024,256]{2,1,0:T(8,128)(2,1)} %get-tuple-element.106.wo, bf16[8,256,256]{2,1,0:T(8,128)(2,1)} %get-tuple-element.107.qkv), custom_call_target="tpu_custom_call" | custom-call | flops 2000000000 | bytes 16000000 | tf_op jit(solution)/shard_map/attention_back/pallas_call | solution.py:372
  207.5 2.4 collective-permute-done.25.d_other
  210.9 17.2 %qkv_grads.1 = (bf16[1152,256]{1,0:T(8,128)(2,1)}, bf16[1152,256]{1,0:T(8,128)(2,1)}, bf16[1152,256]{1,0:T(8,128)(2,1)}, bf16[1152,256]{1,0:T(8,128)(2,1)}, bf16...) custom-call(s32[1]{0:T(128)} %bitcast.pos_ref, ...), custom_call_target="tpu_custom_call" | custom-call | flops 2415919104 | bytes 10000000 | tf_op jit(solution)/shard_map/qkv_grads/pallas_call | solution.py:385
  229.1 1.2 fusion.2
  230.3 3.0 collective-permute-start.26
  233.3 2.9 collective-permute-start.27
  237.3 1.0 fusion.1
  239.4 15.9 %out_grads.1 = (bf16[576,256]{1,0:T(8,128)(2,1)}, bf16[576,256]{1,0:T(8,128)(2,1)}, bf16[576,256]{1,0:T(8,128)(2,1)}, bf16[576,256]{1,0:T(8,128)(2,1)}, bf16[576...) custom-call(s32[1]{0:T(128)} %bitcast.pos_ref, ...), custom_call_target="tpu_custom_call" | custom-call | flops 1207959552 | bytes 10000000 | tf_op jit(solution)/shard_map/out_grads/pallas_call | solution.py:385
  257.9 3.2 collective-permute-start.37
  265.3 3.3 %collective-permute-start.30 = (bf16[1152,256]{1,0:T(8,128)(2,1)S(1)}, bf16[1152,256]{1,0:T(8,128)(2,1)S(1)}, u32[]{:S(2)}, u32[]{:S(2)}) collective-permute-start(bf16[1152,256]{1,0:T(8,128)(2,1)S(1)} %pad_maximum_fusion.4), channel_id=1, source_target_pairs={{0,12},{1,13},{2,14},{3,15},{4,0},{5,1},{6,2},{7,3},{8,4},{9,5},{1... | collective-permute-start | bytes 1769480 | tf_op jit(solution)/shard_map/ppermute | solution.py:27
  272.8 3.2 collective-permute-start.40
  277.7 2.9 collective-permute-start.41
  280.6 5.7 %collective-permute-done.39 = bf16[576,256]{1,0:T(8,128)(2,1)S(1)} collective-permute-done((bf16[576,256]{1,0:T(8,128)(2,1)S(1)}, bf16[576,256]{1,0:T(8,128)(2,1)S(1)}, u32[]{:S(2)}, u32[]{:S(2)}) %collective-permute-start.39) | collective-permute-done | bytes 294944 | tf_op jit(solution)/shard_map/ppermute | solution.py:27
  286.3 2.9 collective-permute-start.31
  289.3 1.6 reduce
  291.6 1.1 add_convert_fusion.2
  292.7 1.2 add_convert_fusion.3
  294.0 2.0 collective-permute-start.42
  296.9 7.0 %collective-permute-done.31 = bf16[1152,256]{1,0:T(8,128)(2,1)} collective-permute-done((bf16[1152,256]{1,0:T(8,128)(2,1)S(1)}, bf16[1152,256]{1,0:T(8,128)(2,1)}, u32[]{:S(2)}, u32[]{:S(2)}) %collective-permute-start.31) | collective-permute-done | bytes 589856 | tf_op jit(solution)/shard_map/ppermute | solution.py:27
  303.9 1.5 add_convert_fusion.1
  305.6 4.1 %collective-permute-done.43 = bf16[576,256]{1,0:T(8,128)(2,1)S(1)} collective-permute-done((bf16[576,256]{1,0:T(8,128)(2,1)}, bf16[576,256]{1,0:T(8,128)(2,1)S(1)}, u32[]{:S(2)}, u32[]{:S(2)}) %collective-permute-start.43) | collective-permute-done | bytes 294944 | tf_op jit(solution)/shard_map/ppermute | solution.py:27
  311.1 5.5 %collective-permute-done.32 = bf16[1152,256]{1,0:T(8,128)(2,1)S(1)} collective-permute-done((bf16[1152,256]{1,0:T(8,128)(2,1)S(1)}, bf16[1152,256]{1,0:T(8,128)(2,1)S(1)}, u32[]{:S(2)}, u32[]{:S(2)}) %collective-permute-start.32) | collective-permute-done | bytes 589856 | tf_op jit(solution)/shard_map/ppermute | solution.py:27
  316.6 6.2 %collective-permute-done.34 = bf16[1152,256]{1,0:T(8,128)(2,1)S(1)} collective-permute-done((bf16[1152,256]{1,0:T(8,128)(2,1)S(1)}, bf16[1152,256]{1,0:T(8,128)(2,1)S(1)}, u32[]{:S(2)}, u32[]{:S(2)}) %collective-permute-start.34) | collective-permute-done | bytes 589856 | tf_op jit(solution)/shard_map/ppermute | solution.py:27
  (208 shorter events, 57.9 us)
Async XLA Ops:
  14.6 24.0 %collective-permute-start = (bf16[1728,256]{1,0:T(8,128)(2,1)S(1)}, bf16[1728,256]{1,0:T(8,128)(2,1)S(1)}, u32[]{:S(2)}, u32[]{:S(2)}) collective-permute-start(bf16[1728,256]{1,0:T(8,128)(2,1)S(1)} %constant_dynamic-update-slice_fusion.refs_0_), channel_id=1, source_target_pairs={{0,2},{1,3},{2,0},{3,1},{4,6},{5,7},{6,4},{7,5},{8,10},{9,11},{10,... | collective-permute-start | bytes 2654216 | tf_op jit(solution)/shard_map/ppermute | solution.py:27
  17.8 21.4 %collective-permute-start.1 = (bf16[1728,256]{1,0:T(8,128)(2,1)S(1)}, bf16[1728,256]{1,0:T(8,128)(2,1)S(1)}, u32[]{:S(2)}, u32[]{:S(2)}) collective-permute-start(bf16[1728,256]{1,0:T(8,128)(2,1)S(1)} %constant_dynamic-update-slice_fusion.refs_0_), channel_id=1, source_target_pairs={{0,12},{1,13},{2,14},{3,15},{4,0},{5,1},{6,2},{7,3},{8,4},{9,5},{1... | collective-permute-start | bytes 2654216 | tf_op jit(solution)/shard_map/ppermute | solution.py:27
  20.5 22.0 %collective-permute-start.2 = (bf16[1728,256]{1,0:T(8,128)(2,1)S(1)}, bf16[1728,256]{1,0:T(8,128)(2,1)S(1)}, u32[]{:S(2)}, u32[]{:S(2)}) collective-permute-start(bf16[1728,256]{1,0:T(8,128)(2,1)S(1)} %constant_dynamic-update-slice_fusion.refs_0_), channel_id=1, source_target_pairs={{0,4},{1,5},{2,6},{3,7},{4,8},{5,9},{6,10},{7,11},{8,12},{9,13},{1... | collective-permute-start | bytes 2654216 | tf_op jit(solution)/shard_map/ppermute | solution.py:27
  34.5 47.9 %collective-permute-start.9 = (bf16[1728,256]{1,0:T(8,128)(2,1)S(1)}, bf16[1728,256]{1,0:T(8,128)(2,1)S(1)}, u32[]{:S(2)}, u32[]{:S(2)}) collective-permute-start(bf16[1728,256]{1,0:T(8,128)(2,1)S(1)} %constant_dynamic-update-slice_fusion.17), channel_id=1, source_target_pairs={{0,16},{16,32},{32,48},{48,64},{64,80},{80,96},{96,112},{112,0},{1... | collective-permute-start | bytes 2654216 | tf_op jit(solution)/shard_map/ppermute | solution.py:448
  42.6 32.8 %collective-permute-start.3 = (bf16[1728,256]{1,0:T(8,128)(2,1)S(1)}, bf16[1728,256]{1,0:T(8,128)(2,1)S(1)}, u32[]{:S(2)}, u32[]{:S(2)}) collective-permute-start(bf16[1728,256]{1,0:T(8,128)(2,1)S(1)} %collective-permute-done.1.refs_2_), channel_id=1, source_target_pairs={{0,2},{1,3},{2,0},{3,1},{4,6},{5,7},{6,4},{7,5},{8,10},{9,11},{10,... | collective-permute-start | bytes 2654216 | tf_op jit(solution)/shard_map/ppermute | solution.py:27
  42.9 32.5 %collective-permute-start.5 = (bf16[1728,256]{1,0:T(8,128)(2,1)S(1)}, bf16[1728,256]{1,0:T(8,128)(2,1)S(1)}, u32[]{:S(2)}, u32[]{:S(2)}) collective-permute-start(bf16[1728,256]{1,0:T(8,128)(2,1)S(1)} %collective-permute-done.1.refs_2_), channel_id=1, source_target_pairs={{0,12},{1,13},{2,14},{3,15},{4,0},{5,1},{6,2},{7,3},{8,4},{9,5},{1... | collective-permute-start | bytes 2654216 | tf_op jit(solution)/shard_map/ppermute | solution.py:27
  44.7 30.7 %collective-permute-start.4 = (bf16[1728,256]{1,0:T(8,128)(2,1)S(1)}, bf16[1728,256]{1,0:T(8,128)(2,1)S(1)}, u32[]{:S(2)}, u32[]{:S(2)}) collective-permute-start(bf16[1728,256]{1,0:T(8,128)(2,1)S(1)} %collective-permute-done.refs_1_), channel_id=1, source_target_pairs={{0,4},{1,5},{2,6},{3,7},{4,8},{5,9},{6,10},{7,11},{8,12},{9,13},{1... | collective-permute-start | bytes 2654216 | tf_op jit(solution)/shard_map/ppermute | solution.py:27
  75.5 9.5 %collective-permute-start.6 = (bf16[576,256]{1,0:T(8,128)(2,1)S(1)}, bf16[576,256]{1,0:T(8,128)(2,1)S(1)}, u32[]{:S(2)}, u32[]{:S(2)}) collective-permute-start(bf16[576,256]{1,0:T(8,128)(2,1)S(1)} %slice.279), channel_id=1, source_target_pairs={{0,2},{1,3},{2,0},{3,1},{4,6},{5,7},{6,4},{7,5},{8,10},{9,11},{10,... | collective-permute-start | bytes 884744 | tf_op jit(solution)/shard_map/ppermute | solution.py:27
  78.8 8.9 %collective-permute-start.7 = (bf16[576,256]{1,0:T(8,128)(2,1)S(1)}, bf16[576,256]{1,0:T(8,128)(2,1)S(1)}, u32[]{:S(2)}, u32[]{:S(2)}) collective-permute-start(bf16[576,256]{1,0:T(8,128)(2,1)S(1)} %slice.280), channel_id=1, source_target_pairs={{0,4},{1,5},{2,6},{3,7},{4,8},{5,9},{6,10},{7,11},{8,12},{9,13},{1... | collective-permute-start | bytes 884744 | tf_op jit(solution)/shard_map/ppermute | solution.py:27
  80.3 7.4 %collective-permute-start.8 = (bf16[576,256]{1,0:T(8,128)(2,1)S(1)}, bf16[576,256]{1,0:T(8,128)(2,1)S(1)}, u32[]{:S(2)}, u32[]{:S(2)}) collective-permute-start(bf16[576,256]{1,0:T(8,128)(2,1)S(1)} %slice.281), channel_id=1, source_target_pairs={{0,12},{1,13},{2,14},{3,15},{4,0},{5,1},{6,2},{7,3},{8,4},{9,5},{1... | collective-permute-start | bytes 884744 | tf_op jit(solution)/shard_map/ppermute | solution.py:27
  82.4 32.2 %copy-start.8 = (bf16[1728,256]{1,0:T(8,128)(2,1)}, bf16[1728,256]{1,0:T(8,128)(2,1)S(1)}, u32[]{:S(2)}) copy-start(bf16[1728,256]{1,0:T(8,128)(2,1)S(1)} %collective-permute-done.9.refs_0_) | copy-start | bytes 2654212
  87.8 26.1 %collective-permute-start.13 = (bf16[13824,256]{1,0:T(8,128)(2,1)S(1)}, bf16[13824,256]{1,0:T(8,128)(2,1)}, u32[]{:S(2)}, u32[]{:S(2)}) collective-permute-start(bf16[13824,256]{1,0:T(8,128)(2,1)S(1)} %constant_dynamic-update-slice_fusion.34), channel_id=1, source_target_pairs={{0,1},{1,0},{2,3},{3,2},{4,5},{5,4},{6,7},{7,6},{8,9},{9,8},{10,11... | collective-permute-start | bytes 21233672 | tf_op jit(solution)/shard_map/ppermute | solution.py:27
  87.9 23.6 %collective-permute-start.10 = (bf16[1728,256]{1,0:T(8,128)(2,1)S(1)}, bf16[1728,256]{1,0:T(8,128)(2,1)S(1)}, u32[]{:S(2)}, u32[]{:S(2)}) collective-permute-start(bf16[1728,256]{1,0:T(8,128)(2,1)S(1)} %collective-permute-done.9.refs_0_), channel_id=1, source_target_pairs={{0,2},{1,3},{2,0},{3,1},{4,6},{5,7},{6,4},{7,5},{8,10},{9,11},{10,... | collective-permute-start | bytes 2654216 | tf_op jit(solution)/shard_map/ppermute | solution.py:27
  88.4 23.1 %collective-permute-start.11 = (bf16[1728,256]{1,0:T(8,128)(2,1)S(1)}, bf16[1728,256]{1,0:T(8,128)(2,1)S(1)}, u32[]{:S(2)}, u32[]{:S(2)}) collective-permute-start(bf16[1728,256]{1,0:T(8,128)(2,1)S(1)} %collective-permute-done.9.refs_0_), channel_id=1, source_target_pairs={{0,12},{1,13},{2,14},{3,15},{4,0},{5,1},{6,2},{7,3},{8,4},{9,5},{1... | collective-permute-start | bytes 2654216 | tf_op jit(solution)/shard_map/ppermute | solution.py:27
  91.3 22.6 %collective-permute-start.12 = (bf16[1728,256]{1,0:T(8,128)(2,1)S(1)}, bf16[1728,256]{1,0:T(8,128)(2,1)S(1)}, u32[]{:S(2)}, u32[]{:S(2)}) collective-permute-start(bf16[1728,256]{1,0:T(8,128)(2,1)S(1)} %collective-permute-done.9.refs_0_), channel_id=1, source_target_pairs={{0,4},{1,5},{2,6},{3,7},{4,8},{5,9},{6,10},{7,11},{8,12},{9,13},{1... | collective-permute-start | bytes 2654216 | tf_op jit(solution)/shard_map/ppermute | solution.py:27
  114.8 26.2 %collective-permute-start.17 = (bf16[6912,256]{1,0:T(8,128)(2,1)S(1)}, bf16[6912,256]{1,0:T(8,128)(2,1)}, u32[]{:S(2)}, u32[]{:S(2)}) collective-permute-start(bf16[6912,256]{1,0:T(8,128)(2,1)S(1)} %pad_maximum_fusion), channel_id=1, source_target_pairs={{0,1},{1,0},{2,3},{3,2},{4,5},{5,4},{6,7},{7,6},{8,9},{9,8},{10,11... | collective-permute-start | bytes 10616840 | tf_op jit(solution)/shard_map/ppermute | solution.py:27
  114.9 23.6 %collective-permute-start.14 = (bf16[1728,256]{1,0:T(8,128)(2,1)S(1)}, bf16[1728,256]{1,0:T(8,128)(2,1)S(1)}, u32[]{:S(2)}, u32[]{:S(2)}) collective-permute-start(bf16[1728,256]{1,0:T(8,128)(2,1)S(1)} %collective-permute-done.11.refs_2_), channel_id=1, source_target_pairs={{0,2},{1,3},{2,0},{3,1},{4,6},{5,7},{6,4},{7,5},{8,10},{9,11},{10,... | collective-permute-start | bytes 2654216 | tf_op jit(solution)/shard_map/ppermute | solution.py:27
  118.1 23.0 %collective-permute-start.15 = (bf16[1728,256]{1,0:T(8,128)(2,1)S(1)}, bf16[1728,256]{1,0:T(8,128)(2,1)S(1)}, u32[]{:S(2)}, u32[]{:S(2)}) collective-permute-start(bf16[1728,256]{1,0:T(8,128)(2,1)S(1)} %collective-permute-done.10.refs_1_), channel_id=1, source_target_pairs={{0,4},{1,5},{2,6},{3,7},{4,8},{5,9},{6,10},{7,11},{8,12},{9,13},{1... | collective-permute-start | bytes 2654216 | tf_op jit(solution)/shard_map/ppermute | solution.py:27
  118.1 23.0 %collective-permute-start.16 = (bf16[1728,256]{1,0:T(8,128)(2,1)S(1)}, bf16[1728,256]{1,0:T(8,128)(2,1)S(1)}, u32[]{:S(2)}, u32[]{:S(2)}) collective-permute-start(bf16[1728,256]{1,0:T(8,128)(2,1)S(1)} %collective-permute-done.11.refs_2_), channel_id=1, source_target_pairs={{0,12},{1,13},{2,14},{3,15},{4,0},{5,1},{6,2},{7,3},{8,4},{9,5},{1... | collective-permute-start | bytes 2654216 | tf_op jit(solution)/shard_map/ppermute | solution.py:27
  142.9 11.2 %collective-permute-start.21 = (bf16[5184,256]{1,0:T(8,128)(2,1)}, bf16[5184,256]{1,0:T(8,128)(2,1)}, u32[]{:S(2)}, u32[]{:S(2)}) collective-permute-start(bf16[5184,256]{1,0:T(8,128)(2,1)} %pad_maximum_fusion.1), channel_id=1, source_target_pairs={{0,1},{1,0},{2,3},{3,2},{4,5},{5,4},{6,7},{7,6},{8,9},{9,8},{10,11... | collective-permute-start | bytes 7962632 | tf_op jit(solution)/shard_map/ppermute | solution.py:27
  143.1 11.0 %collective-permute-start.18 = (bf16[576,256]{1,0:T(8,128)(2,1)S(1)}, bf16[576,256]{1,0:T(8,128)(2,1)S(1)}, u32[]{:S(2)}, u32[]{:S(2)}) collective-permute-start(bf16[576,256]{1,0:T(8,128)(2,1)S(1)} %slice.299), channel_id=1, source_target_pairs={{0,2},{1,3},{2,0},{3,1},{4,6},{5,7},{6,4},{7,5},{8,10},{9,11},{10,... | collective-permute-start | bytes 884744 | tf_op jit(solution)/shard_map/ppermute | solution.py:27
  144.0 10.1 %collective-permute-start.19 = (bf16[576,256]{1,0:T(8,128)(2,1)S(1)}, bf16[576,256]{1,0:T(8,128)(2,1)S(1)}, u32[]{:S(2)}, u32[]{:S(2)}) collective-permute-start(bf16[576,256]{1,0:T(8,128)(2,1)S(1)} %slice.300), channel_id=1, source_target_pairs={{0,4},{1,5},{2,6},{3,7},{4,8},{5,9},{6,10},{7,11},{8,12},{9,13},{1... | collective-permute-start | bytes 884744 | tf_op jit(solution)/shard_map/ppermute | solution.py:27
  144.0 10.1 %collective-permute-start.20 = (bf16[576,256]{1,0:T(8,128)(2,1)S(1)}, bf16[576,256]{1,0:T(8,128)(2,1)S(1)}, u32[]{:S(2)}, u32[]{:S(2)}) collective-permute-start(bf16[576,256]{1,0:T(8,128)(2,1)S(1)} %slice.301), channel_id=1, source_target_pairs={{0,12},{1,13},{2,14},{3,15},{4,0},{5,1},{6,2},{7,3},{8,4},{9,5},{1... | collective-permute-start | bytes 884744 | tf_op jit(solution)/shard_map/ppermute | solution.py:27
  154.2 24.3 %collective-permute-start.24 = (bf16[1728,256]{1,0:T(8,128)(2,1)S(1)}, bf16[1728,256]{1,0:T(8,128)(2,1)S(1)}, u32[]{:S(2)}, u32[]{:S(2)}) collective-permute-start(bf16[1728,256]{1,0:T(8,128)(2,1)S(1)} %pad_maximum_fusion.2), channel_id=1, source_target_pairs={{0,1},{1,0},{2,3},{3,2},{4,5},{5,4},{6,7},{7,6},{8,9},{9,8},{10,11... | collective-permute-start | bytes 2654216 | tf_op jit(solution)/shard_map/ppermute | solution.py:27
  174.7 3.8 %collective-permute-start.22 = (bf16[256,1152]{1,0:T(8,128)(2,1)S(1)}, bf16[256,1152]{1,0:T(8,128)(2,1)S(1)}, u32[]{:S(2)}, u32[]{:S(2)}) collective-permute-start(bf16[256,1152]{1,0:T(8,128)(2,1)S(1)} %get-tuple-element.152), channel_id=1, source_target_pairs={{0,1},{1,0},{2,3},{3,2},{4,5},{5,4},{6,7},{7,6},{8,9},{9,8},{10,11... | collective-permute-start | bytes 1769480 | tf_op jit(solution)/shard_map/ppermute | solution.py:27
  177.0 1.5 collective-permute-start.23
  207.0 2.9 collective-permute-start.25
  207.2 31.2 %collective-permute-start.35 = (bf16[256,2304]{1,0:T(8,128)(2,1)S(1)}, bf16[256,2304]{1,0:T(8,128)(2,1)S(1)}, u32[]{:S(2)}, u32[]{:S(2)}) collective-permute-start(bf16[256,2304]{1,0:T(8,128)(2,1)S(1)} %copy-done.14), channel_id=1, source_target_pairs={{0,1},{1,0},{2,3},{3,2},{4,5},{5,4},{6,7},{7,6},{8,9},{9,8},{10,11... | collective-permute-start | bytes 3538952 | tf_op jit(solution)/shard_map/ppermute | solution.py:27
  230.3 32.7 %collective-permute-start.26 = (bf16[384,256]{1,0:T(8,128)(2,1)S(1)}, bf16[384,256]{1,0:T(8,128)(2,1)S(1)}, u32[]{:S(2)}, u32[]{:S(2)}) collective-permute-start(bf16[384,256]{1,0:T(8,128)(2,1)S(1)} %get-tuple-element.157), channel_id=1, source_target_pairs={{0,2},{1,3},{2,0},{3,1},{4,6},{5,7},{6,4},{7,5},{8,10},{9,11},{10,... | collective-permute-start | bytes 589832 | tf_op jit(solution)/shard_map/ppermute | solution.py:27
  233.3 29.8 %collective-permute-start.27 = (bf16[384,256]{1,0:T(8,128)(2,1)S(1)}, bf16[384,256]{1,0:T(8,128)(2,1)S(1)}, u32[]{:S(2)}, u32[]{:S(2)}) collective-permute-start(bf16[384,256]{1,0:T(8,128)(2,1)S(1)} %get-tuple-element.156), channel_id=1, source_target_pairs={{0,12},{1,13},{2,14},{3,15},{4,0},{5,1},{6,2},{7,3},{8,4},{9,5},{1... | collective-permute-start | bytes 589832 | tf_op jit(solution)/shard_map/ppermute | solution.py:27
  236.3 26.9 %collective-permute-start.28 = (bf16[384,256]{1,0:T(8,128)(2,1)S(1)}, bf16[384,256]{1,0:T(8,128)(2,1)S(1)}, u32[]{:S(2)}, u32[]{:S(2)}) collective-permute-start(bf16[384,256]{1,0:T(8,128)(2,1)S(1)} %get-tuple-element.155), channel_id=1, source_target_pairs={{0,4},{1,5},{2,6},{3,7},{4,8},{5,9},{6,10},{7,11},{8,12},{9,13},{1... | collective-permute-start | bytes 589832 | tf_op jit(solution)/shard_map/ppermute | solution.py:27
  257.2 12.3 %collective-permute-start.36 = (bf16[192,256]{1,0:T(8,128)(2,1)S(1)}, bf16[192,256]{1,0:T(8,128)(2,1)S(1)}, u32[]{:S(2)}, u32[]{:S(2)}) collective-permute-start(bf16[192,256]{1,0:T(8,128)(2,1)S(1)} %get-tuple-element.164), channel_id=1, source_target_pairs={{0,2},{1,3},{2,0},{3,1},{4,6},{5,7},{6,4},{7,5},{8,10},{9,11},{10,... | collective-permute-start | bytes 294920 | tf_op jit(solution)/shard_map/ppermute | solution.py:27
  257.9 11.7 %collective-permute-start.37 = (bf16[192,256]{1,0:T(8,128)(2,1)S(1)}, bf16[192,256]{1,0:T(8,128)(2,1)S(1)}, u32[]{:S(2)}, u32[]{:S(2)}) collective-permute-start(bf16[192,256]{1,0:T(8,128)(2,1)S(1)} %get-tuple-element.163), channel_id=1, source_target_pairs={{0,12},{1,13},{2,14},{3,15},{4,0},{5,1},{6,2},{7,3},{8,4},{9,5},{1... | collective-permute-start | bytes 294920 | tf_op jit(solution)/shard_map/ppermute | solution.py:27
  263.0 7.0 %collective-permute-start.38 = (bf16[192,256]{1,0:T(8,128)(2,1)S(1)}, bf16[192,256]{1,0:T(8,128)(2,1)S(1)}, u32[]{:S(2)}, u32[]{:S(2)}) collective-permute-start(bf16[192,256]{1,0:T(8,128)(2,1)S(1)} %get-tuple-element.162), channel_id=1, source_target_pairs={{0,4},{1,5},{2,6},{3,7},{4,8},{5,9},{6,10},{7,11},{8,12},{9,13},{1... | collective-permute-start | bytes 294920 | tf_op jit(solution)/shard_map/ppermute | solution.py:27
  264.2 29.8 %collective-permute-start.29 = (bf16[1152,256]{1,0:T(8,128)(2,1)S(1)}, bf16[1152,256]{1,0:T(8,128)(2,1)}, u32[]{:S(2)}, u32[]{:S(2)}) collective-permute-start(bf16[1152,256]{1,0:T(8,128)(2,1)S(1)} %pad_maximum_fusion.3), channel_id=1, source_target_pairs={{0,4},{1,5},{2,6},{3,7},{4,8},{5,9},{6,10},{7,11},{8,12},{9,13},{1... | collective-permute-start | bytes 1769480 | tf_op jit(solution)/shard_map/ppermute | solution.py:27
  265.3 38.6 %copy-start.24 = (bf16[1152,256]{1,0:T(8,128)(2,1)S(1)}, bf16[1152,256]{1,0:T(8,128)(2,1)}, u32[]{:S(2)}) copy-start(bf16[1152,256]{1,0:T(8,128)(2,1)} %get-tuple-element.109) | copy-start | bytes 1769476
  265.3 30.7 %collective-permute-start.30 = (bf16[1152,256]{1,0:T(8,128)(2,1)S(1)}, bf16[1152,256]{1,0:T(8,128)(2,1)S(1)}, u32[]{:S(2)}, u32[]{:S(2)}) collective-permute-start(bf16[1152,256]{1,0:T(8,128)(2,1)S(1)} %pad_maximum_fusion.4), channel_id=1, source_target_pairs={{0,12},{1,13},{2,14},{3,15},{4,0},{5,1},{6,2},{7,3},{8,4},{9,5},{1... | collective-permute-start | bytes 1769480 | tf_op jit(solution)/shard_map/ppermute | solution.py:27
  271.0 15.3 %collective-permute-start.39 = (bf16[576,256]{1,0:T(8,128)(2,1)S(1)}, bf16[576,256]{1,0:T(8,128)(2,1)S(1)}, u32[]{:S(2)}, u32[]{:S(2)}) collective-permute-start(bf16[576,256]{1,0:T(8,128)(2,1)S(1)} %pad_maximum_fusion.6), channel_id=1, source_target_pairs={{0,4},{1,5},{2,6},{3,7},{4,8},{5,9},{6,10},{7,11},{8,12},{9,13},{1... | collective-permute-start | bytes 884744 | tf_op jit(solution)/shard_map/ppermute | solution.py:27
  272.0 33.5 %copy-start.23 = (bf16[1152,256]{1,0:T(8,128)(2,1)S(1)}, bf16[1152,256]{1,0:T(8,128)(2,1)}, u32[]{:S(2)}) copy-start(bf16[1152,256]{1,0:T(8,128)(2,1)} %get-tuple-element.120) | copy-start | bytes 1769476
  272.8 18.1 %collective-permute-start.40 = (bf16[576,256]{1,0:T(8,128)(2,1)}, bf16[576,256]{1,0:T(8,128)(2,1)}, u32[]{:S(2)}, u32[]{:S(2)}) collective-permute-start(bf16[576,256]{1,0:T(8,128)(2,1)} %pad_maximum_fusion.7), channel_id=1, source_target_pairs={{0,12},{1,13},{2,14},{3,15},{4,0},{5,1},{6,2},{7,3},{8,4},{9,5},{1... | collective-permute-start | bytes 884744 | tf_op jit(solution)/shard_map/ppermute | solution.py:27
  277.7 13.9 %collective-permute-start.41 = (bf16[576,256]{1,0:T(8,128)(2,1)}, bf16[576,256]{1,0:T(8,128)(2,1)}, u32[]{:S(2)}, u32[]{:S(2)}) collective-permute-start(bf16[576,256]{1,0:T(8,128)(2,1)} %pad_maximum_fusion.8), channel_id=1, source_target_pairs={{0,2},{1,3},{2,0},{3,1},{4,6},{5,7},{6,4},{7,5},{8,10},{9,11},{10,... | collective-permute-start | bytes 884744 | tf_op jit(solution)/shard_map/ppermute | solution.py:27
  286.3 17.5 %collective-permute-start.31 = (bf16[1152,256]{1,0:T(8,128)(2,1)S(1)}, bf16[1152,256]{1,0:T(8,128)(2,1)}, u32[]{:S(2)}, u32[]{:S(2)}) collective-permute-start(bf16[1152,256]{1,0:T(8,128)(2,1)S(1)} %pad_maximum_fusion.5), channel_id=1, source_target_pairs={{0,2},{1,3},{2,0},{3,1},{4,6},{5,7},{6,4},{7,5},{8,10},{9,11},{10,... | collective-permute-start | bytes 1769480 | tf_op jit(solution)/shard_map/ppermute | solution.py:27
  290.8 20.2 %collective-permute-start.33 = (bf16[1152,256]{1,0:T(8,128)(2,1)}, bf16[1152,256]{1,0:T(8,128)(2,1)S(1)}, u32[]{:S(2)}, u32[]{:S(2)}) collective-permute-start(bf16[1152,256]{1,0:T(8,128)(2,1)} %get-tuple-element.119), channel_id=1, source_target_pairs={{0,12},{1,13},{2,14},{3,15},{4,0},{5,1},{6,2},{7,3},{8,4},{9,5},{1... | collective-permute-start | bytes 1769480 | tf_op jit(solution)/shard_map/ppermute | solution.py:27
  291.5 18.2 %collective-permute-start.43 = (bf16[576,256]{1,0:T(8,128)(2,1)}, bf16[576,256]{1,0:T(8,128)(2,1)S(1)}, u32[]{:S(2)}, u32[]{:S(2)}) collective-permute-start(bf16[576,256]{1,0:T(8,128)(2,1)} %get-tuple-element.137), channel_id=1, source_target_pairs={{0,12},{1,13},{2,14},{3,15},{4,0},{5,1},{6,2},{7,3},{8,4},{9,5},{1... | collective-permute-start | bytes 884744 | tf_op jit(solution)/shard_map/ppermute | solution.py:27
  294.0 16.8 %collective-permute-start.42 = (bf16[576,256]{1,0:T(8,128)(2,1)S(1)}, bf16[576,256]{1,0:T(8,128)(2,1)S(1)}, u32[]{:S(2)}, u32[]{:S(2)}) collective-permute-start(bf16[576,256]{1,0:T(8,128)(2,1)S(1)} %add_convert_fusion.3), channel_id=1, source_target_pairs={{0,4},{1,5},{2,6},{3,7},{4,8},{5,9},{6,10},{7,11},{8,12},{9,13},{1... | collective-permute-start | bytes 884744 | tf_op jit(solution)/shard_map/ppermute | solution.py:27
  296.0 14.8 %collective-permute-start.44 = (bf16[576,256]{1,0:T(8,128)(2,1)S(1)}, bf16[576,256]{1,0:T(8,128)(2,1)S(1)}, u32[]{:S(2)}, u32[]{:S(2)}) collective-permute-start(bf16[576,256]{1,0:T(8,128)(2,1)S(1)} %add_convert_fusion.2), channel_id=1, source_target_pairs={{0,2},{1,3},{2,0},{3,1},{4,6},{5,7},{6,4},{7,5},{8,10},{9,11},{10,... | collective-permute-start | bytes 884744 | tf_op jit(solution)/shard_map/ppermute | solution.py:27
  305.4 11.2 %collective-permute-start.32 = (bf16[1152,256]{1,0:T(8,128)(2,1)S(1)}, bf16[1152,256]{1,0:T(8,128)(2,1)S(1)}, u32[]{:S(2)}, u32[]{:S(2)}) collective-permute-start(bf16[1152,256]{1,0:T(8,128)(2,1)S(1)} %add_convert_fusion.1), channel_id=1, source_target_pairs={{0,4},{1,5},{2,6},{3,7},{4,8},{5,9},{6,10},{7,11},{8,12},{9,13},{1... | collective-permute-start | bytes 1769480 | tf_op jit(solution)/shard_map/ppermute | solution.py:27
  309.8 13.0 %collective-permute-start.34 = (bf16[1152,256]{1,0:T(8,128)(2,1)S(1)}, bf16[1152,256]{1,0:T(8,128)(2,1)S(1)}, u32[]{:S(2)}, u32[]{:S(2)}) collective-permute-start(bf16[1152,256]{1,0:T(8,128)(2,1)S(1)} %add_convert_fusion), channel_id=1, source_target_pairs={{0,2},{1,3},{2,0},{3,1},{4,6},{5,7},{6,4},{7,5},{8,10},{9,11},{10,... | collective-permute-start | bytes 1769480 | tf_op jit(solution)/shard_map/ppermute | solution.py:27
  (30 other events, 372.6 us)

commit v2 on v1

v2 whole, which is shorter than its diff:
```python
import functools
import math

import jax
import jax.numpy as jnp
from jax import lax
from jax.experimental import pallas as pl
from jax.experimental.pallas import tpu as pltpu
from jax.sharding import PartitionSpec as P

SEQ, D, HEAD, HQ, HK, LABELS = 256, 2304, 256, 4, 2, 256
QKV_PANELS, O_PANELS = 8, 9
QKV_ROWS, O_ROWS = 144, 64
THIRD = 576
PACKED = 3 * THIRD
EPSILON = 1e-06
ATTN_CAP = 50.0
LABEL_CAP = 30.0
MASKED = -1e30
F32, BF16 = jnp.float32, jnp.bfloat16

N_FSDP = 16


SMEM = pl.BlockSpec(memory_space=pltpu.SMEM)
VMEM = pl.BlockSpec(memory_space=pltpu.VMEM)
ANY = pl.BlockSpec(memory_space=pl.ANY)


def cost(flops, moved_bytes):
    return pl.CostEstimate(flops=flops, bytes_accessed=moved_bytes, transcendentals=0)


def shape(dims, kind=BF16):
    return jax.ShapeDtypeStruct(dims, kind)


def limit(mebibytes):
    return pltpu.CompilerParams(vmem_limit_bytes=mebibytes * 1024 * 1024)


def moved(value, target):
    return lax.ppermute(value, "fsdp", [(i, target(i)) for i in range(N_FSDP)])


def to_core(i):
    return i ^ 1


def to_y(i):
    return i ^ 2


def to_next_x(i):
    return (i + 4) % N_FSDP


def to_prev_x(i):
    return (i - 4) % N_FSDP


together = lax.optimization_barrier


def pack_kernel(w_q, w_k, w_v, w_o, out):
    row = 0
    for ref in (w_q, w_k, w_v, w_o):
        rows, cols = ref.shape
        for p in range(cols // HEAD):
            out[row : row + rows] = ref[:, HEAD * p : HEAD * (p + 1)]
            row += rows


def pack(w_q, w_k, w_v, w_o):
    return pl.pallas_call(
        pack_kernel,
        out_shape=shape((PACKED, HEAD)),
        in_specs=[VMEM] * 4,
        out_specs=VMEM,
        compiler_params=limit(8),
        cost_estimate=cost(0, 4_000_000),
        name="pack",
    )(w_q, w_k, w_v, w_o)


QKV_PART = QKV_PANELS * QKV_ROWS

SLOTS = [(0, 0), (3, 0), (0, 1), (1, 0), (2, 0), (3, 1), (1, 1), (2, 1)]
SLOT_ROWS = 2 * QKV_ROWS
OWN_EARLY, PEER_EARLY = 4, 3


def rms(values, gain):
    mean = jnp.sum(values * values, -1, keepdims=True) * (1.0 / D)
    return values * lax.rsqrt(mean + EPSILON) * gain


def chip_index(position, dx, dy):
    x = position // 4
    y = (position // 2) % 2
    return ((x + dx) % 4) * 2 + (y if dy == 0 else 1 - y)


def device_index(position, dx, dy, dc):
    core = position % 2
    return chip_index(position, dx, dy) * 2 + (core if dc == 0 else 1 - core)


def panel_copies(sources, refs, height, rows, target, sem):
    for panel, row in enumerate(rows):
        for piece, at, first, last in sources:
            if first <= row < last:
                pltpu.make_async_copy(
                    refs[piece].at[pl.ds(at + row - first, height)], target(panel), sem
                ).start()


def load_qkv(slots, refs, wqkv, sem):
    for slot, cores in enumerate(slots):
        for dc, sources in enumerate(cores):
            to = 2 * QKV_ROWS * slot + QKV_ROWS * dc
            panel_copies(
                sources,
                refs,
                QKV_ROWS,
                range(0, QKV_PART, QKV_ROWS),
                lambda p, to=to: wqkv.at[p, pl.ds(to, QKV_ROWS)],
                sem,
            )


def load_out(position, chips, slots, refs, wo, sem):
    for (dx, dy), cores in zip(chips, slots):
        for dc, sources in enumerate(cores):
            owner = device_index(position, dx, dy, dc)
            to = pl.ds(pl.multiple_of(owner * O_ROWS, 16), O_ROWS)
            panel_copies(
                sources,
                refs,
                O_ROWS,
                range(QKV_PART, PACKED, O_ROWS),
                lambda p, to=to: wo.at[to, pl.ds(HEAD * p, HEAD)],
                sem,
            )


def wait_for(ref, sem):
    pltpu.make_async_copy(ref, ref, sem).wait()


def causal_mask():
    row = lax.broadcasted_iota(jnp.int32, (SEQ, SEQ), 0)
    col = lax.broadcasted_iota(jnp.int32, (SEQ, SEQ), 1)
    return row >= col


def nt(a, b):
    return lax.dot_general(a, b, (((1,), (1,)), ((), ())), preferred_element_type=F32)


def tn(a, b):
    return lax.dot_general(a, b, (((0,), (0,)), ((), ())), preferred_element_type=F32)


def nn(a, b):
    return jnp.dot(a, b, preferred_element_type=F32)


def probabilities(query, key, causal):
    capped = jnp.tanh(nt(query, key) * (1.0 / (math.sqrt(HEAD) * ATTN_CAP)))
    scores = jnp.where(causal, ATTN_CAP * capped, MASKED)
    top = jnp.max(scores, -1, keepdims=True)
    weights = jnp.where(causal, jnp.exp(scores - top), 0.0)
    return weights / jnp.sum(weights, -1, keepdims=True), capped


def prepare_kernel(pos_ref, x_ref, gains_ref, *refs):
    parts, (n_mine, n_send, turned, ordered) = refs[:4], refs[4:]
    normed = rms(x_ref[...].astype(F32), gains_ref[0:1, :]).astype(BF16)
    turned[...] = normed.T

    def rows_of(device):
        return turned[pl.ds(pl.multiple_of(device * QKV_ROWS, 16), QKV_ROWS)]

    position = pos_ref[0]
    for slot, (dx, dy) in enumerate(SLOTS):
        for dc in range(2):
            to = SLOT_ROWS * slot + QKV_ROWS * dc
            ordered[to : to + QKV_ROWS] = rows_of(device_index(position, dx, dy, dc))
    for split, early, late in ((OWN_EARLY, *parts[:2]), (PEER_EARLY, *parts[2:])):
        early[...] = ordered[0 : SLOT_ROWS * split].T
        late[...] = ordered[SLOT_ROWS * split :].T
    core = position % 2
    for chip in range(8):
        to = slice(QKV_ROWS * chip, QKV_ROWS * (chip + 1))
        n_mine[to] = rows_of(2 * chip + core)
        n_send[to] = rows_of(2 * chip + 1 - core)


def early_kernel(slots, normed, *refs):
    pieces, (acc, wqkv, sem) = refs[:-3], refs[-3:]
    load_qkv(slots, pieces, wqkv, sem)
    wait_for(wqkv, sem)

    def one_panel(p, carry):
        acc[p] = nn(normed[...], wqkv[p])
        return carry

    lax.fori_loop(0, QKV_PANELS, one_panel, 0)


def layer(position, early, slots, x_ref, gains_ref, head_ref, normed, acc, pieces, qkv, context, hidden, wqkv, wo, sems):
    load_qkv(slots[early:], pieces, wqkv, sems.at[0])
    load_out(position, SLOTS, slots, pieces, wo, sems.at[1])
    wait_for(wqkv, sems.at[0])

    def one_panel(p, carry):
        qkv[p] = (acc[p] + nn(normed[...], wqkv[p])).astype(BF16)
        return carry

    lax.fori_loop(0, QKV_PANELS, one_panel, 0)
    causal = causal_mask()
    for h in range(HQ):
        group = h // (HQ // HK)
        probs, _ = probabilities(qkv[h], qkv[HQ + group], causal)
        context[:, HEAD * h : HEAD * (h + 1)] = nn(
            probs.astype(BF16), qkv[HQ + HK + group]
        ).astype(BF16)
    wait_for(wo, sems.at[1])

    def one_out(p, carry):
        cols = pl.ds(pl.multiple_of(p * HEAD, HEAD), HEAD)
        hidden[:, cols] = x_ref[:, cols].astype(F32) + nn(context[...], wo[:, cols])
        return carry

    lax.fori_loop(0, O_PANELS, one_out, 0)
    final = rms(hidden[...], gains_ref[1:2, :]).astype(BF16)
    logits = LABEL_CAP * jnp.tanh(nn(final, head_ref[...]) * (1.0 / LABEL_CAP))
    return logits, logits - jnp.log(jnp.sum(jnp.exp(logits), -1, keepdims=True))


def own_kernel(slots, pos_ref, x_ref, gains_ref, head_ref, normed, acc, *refs):
    pieces, refs = refs[:-10], refs[-10:]
    c_mine, c_send, qkv, hidden, logits, wo, context, turned, wqkv, sems = refs
    position = pos_ref[0]
    logits[...], _ = layer(
        position, OWN_EARLY, slots, x_ref, gains_ref, head_ref, normed, acc, pieces, qkv, context, hidden, wqkv, wo, sems
    )
    turned[...] = context[...].T
    core = position % 2
    for chip in range(8):
        to = slice(O_ROWS * chip, O_ROWS * (chip + 1))
        at = pl.multiple_of((2 * chip + core) * O_ROWS, 16)
        c_mine[to] = turned[pl.ds(at, O_ROWS)]
        at = pl.multiple_of((2 * chip + 1 - core) * O_ROWS, 16)
        c_send[to] = turned[pl.ds(at, O_ROWS)]


def peer_kernel(
    slots, pos_ref, x_ref, gains_ref, head_ref, normed, acc, labels_ref, own_logits, own_hidden, *refs
):
    pieces, refs = refs[:-8], refs[-8:]
    loss, dhidden, qkv, context, hidden, wqkv, wo, sems = refs
    _, peer_lp = layer(
        pos_ref[0], PEER_EARLY, slots, x_ref, gains_ref, head_ref, normed, acc, pieces, qkv, context, hidden, wqkv, wo, sems
    )
    logits = own_logits[...]
    own_lp = logits - jnp.log(jnp.sum(jnp.exp(logits), -1, keepdims=True))
    peer = jnp.exp(peer_lp)
    hot = labels_ref[...] == lax.broadcasted_iota(jnp.int32, (SEQ, LABELS), 1)
    picked = jnp.sum(jnp.where(hot, own_lp, 0.0), -1, keepdims=True)
    loss[...] = jnp.sum(peer * (peer_lp - own_lp), -1, keepdims=True) - picked
    d_lp = (jnp.where(hot, 1.0, 0.0) + peer) * (-1.0 / SEQ)
    d_logits = d_lp - jnp.exp(own_lp) * jnp.sum(d_lp, -1, keepdims=True)
    capped = logits * (1.0 / LABEL_CAP)
    d_raw = (d_logits * (1.0 - capped * capped)).astype(BF16)
    d_final = nt(d_raw, head_ref[...]).astype(BF16).astype(F32) * gains_ref[1:2, :]
    own = own_hidden[...]
    scale = lax.rsqrt(jnp.sum(own * own, -1, keepdims=True) * (1.0 / D) + EPSILON)
    along = jnp.sum(d_final * own, -1, keepdims=True) * (1.0 / D)
    dhidden[...] = (d_final * scale - own * (scale * scale * scale * along)).astype(BF16)


def attention_back_kernel(dhidden, wo, qkv, dqkv):
    causal = causal_mask()
    for group in range(HK):
        key, value = qkv[HQ + group], qkv[HQ + HK + group]
        d_key = jnp.zeros((SEQ, HEAD), F32)
        d_value = jnp.zeros((SEQ, HEAD), F32)
        for h in range(group * (HQ // HK), (group + 1) * (HQ // HK)):
            query = qkv[h]
            probs, capped = probabilities(query, key, causal)
            d_out = nt(dhidden[...], wo[HEAD * h : HEAD * (h + 1), :]).astype(BF16)
            d_value += tn(probs.astype(BF16), d_out)
            d_probs = nt(d_out, value).astype(BF16).astype(F32)
            d_scores = probs * (d_probs - jnp.sum(d_probs * probs, -1, keepdims=True))
            d_raw = (d_scores * (1.0 - capped * capped) * (1.0 / math.sqrt(HEAD))).astype(BF16)
            dqkv[h] = nn(d_raw, key).astype(BF16)
            d_key += tn(d_raw, query)
        dqkv[HQ + group] = d_key.astype(BF16)
        dqkv[HQ + HK + group] = d_value.astype(BF16)


CHIPS = [(0, 0), (1, 0), (2, 0), (3, 0), (0, 1), (1, 1), (2, 1), (3, 1)]


def block_outs(outs):
    return [[o] for o in outs[:6]] + [list(outs[6:9])] + [[outs[9]]]


def hand_out(position, outs, whole_blocks):
    for parts, (dx, dy) in zip(block_outs(outs), CHIPS):
        at = chip_index(position, dx, dy)
        row = 0
        for part in parts:
            part[...] = whole_blocks[at, row : row + part.shape[0]]
            row += part.shape[0]


def out_grad_kernel(pos_ref, mine, other, d_mine, d_other, *refs):
    outs, (lhs, rhs, blocks) = refs[:10], refs[10:]
    lhs[:, 0:SEQ], lhs[:, SEQ : 2 * SEQ] = mine[...], other[...]
    rhs[0:SEQ], rhs[SEQ : 2 * SEQ] = d_mine[...], d_other[...]

    def one_panel(p, carry):
        cols = pl.ds(pl.multiple_of(p * HEAD, HEAD), HEAD)
        rows = pl.ds(pl.multiple_of(p * O_ROWS, 16), O_ROWS)
        total = nn(lhs[...], rhs[:, cols]).astype(BF16)
        for chip in range(8):
            blocks[chip, rows] = total[O_ROWS * chip : O_ROWS * (chip + 1)]
        return carry

    lax.fori_loop(0, O_PANELS, one_panel, 0)
    hand_out(pos_ref[0], outs, blocks)


def qkv_grad_kernel(pos_ref, mine, other, d_mine, d_other, *refs):
    outs, (lhs, rhs, blocks) = refs[:10], refs[10:]
    lhs[:, 0:SEQ], lhs[:, SEQ : 2 * SEQ] = mine[...], other[...]
    rhs[:, 0:SEQ], rhs[:, SEQ : 2 * SEQ] = d_mine[...], d_other[...]

    def one_panel(p, carry):
        rows = pl.ds(pl.multiple_of(p * QKV_ROWS, 16), QKV_ROWS)
        total = nn(lhs[...], rhs[p]).astype(BF16)
        for chip in range(8):
            blocks[chip, rows] = total[QKV_ROWS * chip : QKV_ROWS * (chip + 1)]
        return carry

    lax.fori_loop(0, QKV_PANELS, one_panel, 0)
    hand_out(pos_ref[0], outs, blocks)


def prepare(position, x, gains):
    return pl.pallas_call(
        prepare_kernel,
        out_shape=[
            shape((SEQ, SLOT_ROWS * count))
            for count in (OWN_EARLY, 8 - OWN_EARLY, PEER_EARLY, 8 - PEER_EARLY)
        ]
        + [shape((D // 2, SEQ))] * 2,
        in_specs=[SMEM, VMEM, VMEM],
        out_specs=[VMEM] * 6,
        scratch_shapes=[pltpu.VMEM((D, SEQ), BF16)] * 2,
        compiler_params=limit(20),
        cost_estimate=cost(10_000_000, 10_000_000),
        name="prepare",
    )(position, x, gains)


def some_wqkv(count):
    return pltpu.VMEM((QKV_PANELS, SLOT_ROWS * count, HEAD), BF16)


def early_pass(normed, arrays, slots):
    return pl.pallas_call(
        functools.partial(early_kernel, slots),
        out_shape=shape((QKV_PANELS, SEQ, HEAD), F32),
        in_specs=[VMEM] + [ANY] * len(arrays),
        out_specs=VMEM,
        scratch_shapes=[some_wqkv(len(slots)), pltpu.SemaphoreType.DMA],
        compiler_params=limit(14),
        cost_estimate=cost(1_200_000_000, 20_000_000),
        name="early_pass",
    )(normed, *arrays)


def own_pass(position, x, gains, head, normed, acc, arrays, slots):
    return pl.pallas_call(
        functools.partial(own_kernel, slots),
        out_shape=[
            shape((HQ * HEAD // 2, SEQ)),
            shape((HQ * HEAD // 2, SEQ)),
            shape((QKV_PANELS, SEQ, HEAD)),
            shape((SEQ, D), F32),
            shape((SEQ, LABELS), F32),
            shape((HQ * HEAD, D)),
        ],
        in_specs=[SMEM] + [VMEM] * 5 + [ANY] * len(arrays),
        out_specs=[VMEM] * 6,
        scratch_shapes=[
            pltpu.VMEM((SEQ, HQ * HEAD), BF16),
            pltpu.VMEM((HQ * HEAD, SEQ), BF16),
            some_wqkv(8 - OWN_EARLY),
            pltpu.SemaphoreType.DMA((2,)),
        ],
        compiler_params=limit(32),
        cost_estimate=cost(3_000_000_000, 30_000_000),
        name="own_pass",
    )(position, x, gains, head, normed, acc, *arrays)


def peer_pass(position, x, gains, head, normed, acc, labels, own_logits, own_hidden, arrays, slots):
    return pl.pallas_call(
        functools.partial(peer_kernel, slots),
        out_shape=[shape((SEQ, 1), F32), shape((SEQ, D))],
        in_specs=[SMEM] + [VMEM] * 8 + [ANY] * len(arrays),
        out_specs=[VMEM] * 2,
        scratch_shapes=[
            pltpu.VMEM((QKV_PANELS, SEQ, HEAD), BF16),
            pltpu.VMEM((SEQ, HQ * HEAD), BF16),
            pltpu.VMEM((SEQ, D), F32),
            some_wqkv(8 - PEER_EARLY),
            pltpu.VMEM((HQ * HEAD, D), BF16),
            pltpu.SemaphoreType.DMA((2,)),
        ],
        compiler_params=limit(38),
        cost_estimate=cost(3_000_000_000, 30_000_000),
        name="peer_pass",
    )(position, x, gains, head, normed, acc, labels, own_logits, own_hidden, *arrays)


def attention_back(dhidden, wo, qkv):
    return pl.pallas_call(
        attention_back_kernel,
        out_shape=shape((QKV_PANELS, SEQ, HEAD)),
        in_specs=[VMEM] * 3,
        out_specs=VMEM,
        compiler_params=limit(20),
        cost_estimate=cost(2_000_000_000, 16_000_000),
        name="attention_back",
    )(dhidden, wo, qkv)


def weight_grads(kernel, rows, panels, rhs, position, mine, other, d_mine, d_other, name):
    block = rows * panels
    return pl.pallas_call(
        kernel,
        out_shape=[shape((block, HEAD))] * 6 + [shape((block // 3, HEAD))] * 3 + [shape((block, HEAD))],
        in_specs=[SMEM] + [VMEM] * 4,
        out_specs=[VMEM] * 10,
        scratch_shapes=[
            pltpu.VMEM((8 * rows, 2 * SEQ), BF16),
            pltpu.VMEM(rhs, BF16),
            pltpu.VMEM((8, block, HEAD), BF16),
        ],
        compiler_params=limit(28),
        cost_estimate=cost(2 * 8 * rows * 2 * SEQ * panels * HEAD, 10_000_000),
        name=name,
    )(position, mine, other, d_mine, d_other)


def third_added_kernel(a2, o3, o1, in_a, in_b, in_c, a2_out, o3_out, o1_out):
    t = in_a.shape[0]
    for third, (value, more, out) in enumerate(
        ((a2, in_a, a2_out), (o3, in_b, o3_out), (o1, in_c, o1_out))
    ):
        for part in range(3):
            rows = slice(t * part, t * (part + 1))
            if part == third:
                out[rows] = (value[rows].astype(F32) + more[...].astype(F32)).astype(BF16)
            else:
                out[rows] = value[rows]


def next_added_kernel(a1, o0, in_x, in_y, in_o0, a1_out, o0_out):
    total = a1[...].astype(F32) + in_x[...].astype(F32) + in_y[...].astype(F32)
    a1_out[...] = total.astype(BF16)
    o0_out[...] = (o0[...].astype(F32) + in_o0[...].astype(F32)).astype(BF16)


def summed_kernel(rows, *refs):
    parts, outs = refs[:4], refs[4:]
    row = 0
    for out in outs:
        for p in range(out.shape[1] // HEAD):
            at = slice(row, row + rows)
            total = parts[0][at].astype(F32)
            for part in parts[1:]:
                total += part[at].astype(F32)
            out[:, HEAD * p : HEAD * (p + 1)] = total
            row += rows


def elementwise(kernel, outs, name, *values):
    return pl.pallas_call(
        kernel,
        out_shape=outs,
        in_specs=[VMEM] * len(values),
        out_specs=[VMEM] * len(outs),
        compiler_params=limit(12),
        cost_estimate=cost(1_000_000, 4_000_000),
        name=name,
    )(*values)


def reduce_first(blocks):
    return moved(blocks[6], to_y), moved(blocks[7], to_prev_x), moved(blocks[8], to_next_x)


def add_thirds(blocks, incoming):
    a2, o3, o1 = blocks[2], blocks[9], blocks[5]
    outs = [shape(a2.shape)] * 3
    return elementwise(third_added_kernel, outs, "add_thirds", a2, o3, o1, *incoming)


def reduce_rest(blocks, added, rows, widths):
    s0, a1, _, a3, o0, *_ = blocks
    a2, o3, o1 = added
    one = shape(s0.shape)
    in_x, in_o0, in_y = together((moved(a2, to_next_x), moved(o3, to_prev_x), moved(o1, to_y)))
    a1, o0 = elementwise(next_added_kernel, [one] * 2, "add_next", a1, o0, in_x, in_y, in_o0)
    last = together((moved(a1, to_next_x), moved(a3, to_prev_x), moved(o0, to_y)))
    outs = [shape((rows, width), F32) for width in widths]
    return elementwise(functools.partial(summed_kernel, rows), outs, "add_last", s0, *last)


def body(
    activations,
    labels,
    own_q,
    own_k,
    own_v,
    own_o,
    peer_q,
    peer_k,
    peer_v,
    peer_o,
    norm_gains,
    label_head,
):
    me = lax.axis_index("fsdp")
    position = me.astype(jnp.int32).reshape(1)
    x = activations[0, 0]
    replicas = lax.axis_size("replica")

    own = pack(own_q[0], own_k[0], own_v[0], own_o[0])
    peer = pack(peer_q[0], peer_k[0], peer_v[0], peer_o[0])

    a1, a3 = moved(own, to_prev_x), moved(own, to_next_x)
    peer = lax.ppermute(peer, "replica", [(i, (i + 1) % replicas) for i in range(replicas)])
    prepared = prepare(position, x, norm_gains)
    a1, a3, peer, own, prepared = together((a1, a3, peer, own, prepared))
    n_early, n_late, n_peer_early, n_peer_late, n_mine, n_send = prepared

    y0, a2, p_a3 = moved(own, to_y), moved(a1, to_prev_x), moved(peer, to_next_x)
    n_other = moved(n_send, to_core)
    joined = jnp.concatenate([own, a3, a1], 0)
    y0, a2, p_a3, joined, n_other = together((y0, a2, p_a3, joined, n_other))

    p_y0, o3, o1 = moved(peer, to_y), moved(y0, to_next_x), moved(y0, to_prev_x)
    swap_first, swap_a2 = moved(joined, to_core), moved(a2, to_core)
    p_y0, o3, o1, swap_first, swap_a2 = together((p_y0, o3, o1, swap_first, swap_a2))

    o2, p_a1, p_o3 = moved(a2, to_y), moved(peer, to_prev_x), moved(p_y0, to_next_x)
    swap_y0, swap_o3 = moved(y0, to_core), moved(o3, to_core)

    def all_of(piece, at=0):
        return [(piece, at, 0, PACKED)]

    own_slots = [
        (all_of(0), all_of(4, 0)),
        (all_of(1), all_of(4, PACKED)),
        (all_of(2), all_of(5)),
        (all_of(3), all_of(4, 2 * PACKED)),
        (all_of(6), all_of(10)),
        (all_of(7), all_of(11)),
        (all_of(8), all_of(12)),
        (all_of(9), all_of(13)),
    ]
    acc = early_pass(n_early, [own, a3, y0, a1, swap_first, swap_y0], own_slots[:OWN_EARLY])
    joined = jnp.concatenate([peer, p_a3, p_y0], 0)
    o2, p_a1, p_o3, swap_o3, joined, acc = together((o2, p_a1, p_o3, swap_o3, joined, acc))

    p_o1, p_a2, p_o2 = moved(p_a1, to_y), moved(p_a1, to_prev_x), moved(p_o3, to_next_x)
    swap_o1, swap_o2 = moved(o1, to_core), moved(o2, to_core)
    p_swap_first = moved(joined, to_core)
    c_mine, c_send, qkv, hidden, logits, wo = own_pass(
        position,
        x,
        norm_gains,
        label_head,
        n_late,
        acc,
        [own, a3, y0, a1, swap_first, swap_y0, a2, o3, o1, o2, swap_a2, swap_o3, swap_o1, swap_o2],
        own_slots,
    )
    p_o1, p_a2, p_o2, p_swap_first, c_send, hidden = together(
        (p_o1, p_a2, p_o2, p_swap_first, c_send, hidden)
    )

    late = [p_a1, p_a2, p_o3, p_o1, p_o2]
    swap_late = [moved(piece, to_core) for piece in late]
    c_other = moved(c_send, to_core)
    peer_slots = [(all_of(i), all_of(3, PACKED * i)) for i in range(PEER_EARLY)]
    p_acc = early_pass(n_peer_early, [peer, p_a3, p_y0, p_swap_first], peer_slots)
    peer_slots = peer_slots + [(all_of(4 + i), all_of(9 + i)) for i in range(8 - PEER_EARLY)]
    loss, dhidden = peer_pass(
        position,
        x,
        norm_gains,
        label_head,
        n_peer_late,
        p_acc,
        labels[0, 0].reshape(SEQ, 1),
        logits,
        hidden,
        [peer, p_a3, p_y0, p_swap_first, *late, *swap_late],
        peer_slots,
    )
    d_other = moved(dhidden, to_core)
    dqkv = attention_back(dhidden, wo, qkv)
    dqkv_other = moved(dqkv, to_core)
    out_blocks = weight_grads(
        out_grad_kernel,
        *(O_ROWS, O_PANELS, (2 * SEQ, D)),
        *(position, c_mine, c_other, dhidden, d_other, "out_grads"),
    )
    dqkv, dqkv_other, *out_blocks = together((dqkv, dqkv_other, *out_blocks))
    qkv_blocks = weight_grads(
        qkv_grad_kernel,
        *(QKV_ROWS, QKV_PANELS, (QKV_PANELS, 2 * SEQ, HEAD)),
        *(position, n_mine, n_other, dqkv, dqkv_other, "qkv_grads"),
    )
    in_a, in_b, in_c, *qkv_blocks = together((*reduce_first(out_blocks), *qkv_blocks))
    added, qkv_blocks = together((add_thirds(out_blocks, (in_a, in_b, in_c)), qkv_blocks))
    (grad_out,) = reduce_rest(out_blocks, added, O_ROWS, [D])
    added = add_thirds(qkv_blocks, together(reduce_first(qkv_blocks)))
    grads = reduce_rest(qkv_blocks, added, QKV_ROWS, [HQ * HEAD, HK * HEAD, HK * HEAD])
    return (loss.reshape(1, 1, SEQ), *[grad[None] for grad in grads], grad_out[None])


def solution(mesh):
    weights = P("replica", "fsdp", None)
    return jax.shard_map(
        body,
        mesh=mesh,
        in_specs=(P("replica", "fsdp", None, None), weights, *([weights] * 8), P(), P()),
        out_specs=(weights,) * 5,
        check_vma=False,
    )
```

time: 328 us -> 250 us (0.76)
  waiting for transfers between devices: 125 us -> 99.2 us
  local copies, waits for them, and re-layouts: 44.7 us -> 22.2 us
  other arithmetic: 17.8 us -> 4.35 us
  Pallas kernels: 78.7 us -> 65.8 us
  starting transfers between devices: 57.4 us -> 53.5 us
    ppermute x44 -> x48, waiting for transfers between devices: 125 us -> 95.5 us  [moved(): return lax.ppermute(value, 'fsdp', [(i, target(i)) for i in range(N_FSDP)])]
    convert_element_type x10 -> x0, other arithmetic: 9.72 us -> none  [the longest x2 2.77 us: reduce_scattered(): a1 = added(a1, in_a1, in_a1y).astype(BF16)]
    pallas_call x4 -> x15, Pallas kernels: 69.7 us -> 60.9 us  [the longest x1 16.6 us: own_pass(): pl.pallas_call(functools.partial(own_kernel, slots), out_shape=[shape((HQ...]
    slice x15 -> x0, local copies, waits for them, and re-layouts: 8.29 us -> none  [the longest x2 2.17 us: reduce_scattered(): o2[2 * t:]]
    unnamed x115 -> x84, local copies, waits for them, and re-layouts: 30.2 us -> 22.1 us
    ppermute x44 -> x48, starting transfers between devices: 57.4 us -> 53.3 us  [moved(): return lax.ppermute(value, 'fsdp', [(i, target(i)) for i in range(N_FSDP)])]
    pallas_call x1, Pallas kernels: 8.97 us -> 4.89 us  [attention_back(): pl.pallas_call(attention_back_kernel, out_shape=shape((QKV_PANELS, SEQ, H...]
    squeeze x2 -> x0, local copies, waits for them, and re-layouts: 3.91 us -> none  [the longest x1 2.16 us: body(): n_mine = lax.dynamic_index_in_dim(nsel, core, 0, keepdims=False)]
  transfers between devices with their start and end apart: 45 -> 49, of which waited for: 20 -> 23; matrix products, arithmetic and copies ran while one was open for 12% -> 2% of each run, Pallas kernels for 16% -> 20%
where the time goes in v2:
time: 250 us; the launch traced here: 246 us
  waiting for transfers between devices  99.2 us (40%)
  Pallas kernels  65.8 us (26%)
  starting transfers between devices  53.5 us (21%)
  local copies, waits for them, and re-layouts  22.2 us (9%)
  other arithmetic  4.35 us (2%)
    ppermute x48, waiting for transfers between devices, moved(): return lax.ppermute(value, 'fsdp', [(i, target(i)) for i in range(N_FSDP)])  95.5 us
    ppermute x48, starting transfers between devices, moved(): return lax.ppermute(value, 'fsdp', [(i, target(i)) for i in range(N_FSDP)])  53.3 us
    unnamed x84, local copies, waits for them, and re-layouts  22.1 us
    pallas_call x1, Pallas kernels, own_pass(): pl.pallas_call(functools.partial(own_kernel, slots), out_shape=[shape((HQ...  16.6 us
    pallas_call x1, Pallas kernels, peer_pass(): pl.pallas_call(functools.partial(peer_kernel, slots), out_shape=[shape((S...  14.8 us
    pallas_call x2, Pallas kernels, early_pass(): pl.pallas_call(functools.partial(early_kernel, slots), out_shape=shape((Q...  14.3 us
    pallas_call x2, Pallas kernels, weight_grads(): pl.pallas_call(kernel, out_shape=[shape((block, HEAD))] * 6 + [shape((blo...  8.13 us
  transfers between devices with their start and end apart: 49, of which 23 were waited for; matrix products, arithmetic and copies ran while one was open for 2% of the time, Pallas kernels for 20%

profile of v2, /device:TPU:96, one launch (start us, length us, event | category | flops | bytes accessed | tf_op | source)
XLA Modules:
  0.0 246.2 jit_solution(4248793810136864235)
XLA Ops:
  4.5 2.8 %collective-permute-start = (bf16[1728,256]{1,0:T(8,128)(2,1)S(1)}, bf16[1728,256]{1,0:T(8,128)(2,1)S(1)}, u32[]{:S(2)}, u32[]{:S(2)}) collective-permute-start(bf16[1728,256]{1,0:T(8,128)(2,1)S(1)} %pack.2.refs_0_), channel_id=1, source_target_pairs={{0,12},{1,13},{2,14},{3,15},{4,0},{5,1},{6,2},{7,3},{8,4},{9,5},{1... | collective-permute-start | bytes 2654216 | tf_op jit(solution)/shard_map/ppermute | solution.py:43
  12.3 1.4 prepare.1
  15.4 10.8 %collective-permute-done.refs_3_ = bf16[1728,256]{1,0:T(8,128)(2,1)S(1)} collective-permute-done((bf16[1728,256]{1,0:T(8,128)(2,1)S(1)}, bf16[1728,256]{1,0:T(8,128)(2,1)S(1)}, u32[]{:S(2)}, u32[]{:S(2)}) %collective-permute-start) | collective-permute-done | bytes 884768 | tf_op jit(solution)/shard_map/ppermute | solution.py:43
  26.3 3.5 %collective-permute-done.1.refs_1_ = bf16[1728,256]{1,0:T(8,128)(2,1)} collective-permute-done((bf16[1728,256]{1,0:T(8,128)(2,1)S(1)}, bf16[1728,256]{1,0:T(8,128)(2,1)}, u32[]{:S(2)}, u32[]{:S(2)}) %collective-permute-start.1) | collective-permute-done | bytes 884768 | tf_op jit(solution)/shard_map/ppermute | solution.py:43
  29.8 3.7 %collective-permute-done.2.refs_0_ = bf16[1728,256]{1,0:T(8,128)(2,1)} collective-permute-done((bf16[1728,256]{1,0:T(8,128)(2,1)}, bf16[1728,256]{1,0:T(8,128)(2,1)}, u32[]{:S(2)}, u32[]{:S(2)}) %collective-permute-start.2) | collective-permute-done | bytes 884768 | tf_op jit(solution)/shard_map/ppermute | solution.py:550
  34.0 3.2 %collective-permute-start.3 = (bf16[1728,256]{1,0:T(8,128)(2,1)S(1)}, bf16[1728,256]{1,0:T(8,128)(2,1)S(1)}, u32[]{:S(2)}, u32[]{:S(2)}) collective-permute-start(bf16[1728,256]{1,0:T(8,128)(2,1)S(1)} %pack.2.refs_0_), channel_id=1, source_target_pairs={{0,2},{1,3},{2,0},{3,1},{4,6},{5,7},{6,4},{7,5},{8,10},{9,11},{10,... | collective-permute-start | bytes 2654216 | tf_op jit(solution)/shard_map/ppermute | solution.py:43
  37.2 2.8 %collective-permute-start.4 = (bf16[1728,256]{1,0:T(8,128)(2,1)S(1)}, bf16[1728,256]{1,0:T(8,128)(2,1)S(1)}, u32[]{:S(2)}, u32[]{:S(2)}) collective-permute-start(bf16[1728,256]{1,0:T(8,128)(2,1)S(1)} %collective-permute-done.refs_3_), channel_id=1, source_target_pairs={{0,12},{1,13},{2,14},{3,15},{4,0},{5,1},{6,2},{7,3},{8,4},{9,5},{1... | collective-permute-start | bytes 2654216 | tf_op jit(solution)/shard_map/ppermute | solution.py:43
  42.0 13.2 %collective-permute-done.5.refs_1_ = bf16[1728,256]{1,0:T(8,128)(2,1)S(1)} collective-permute-done((bf16[1728,256]{1,0:T(8,128)(2,1)}, bf16[1728,256]{1,0:T(8,128)(2,1)S(1)}, u32[]{:S(2)}, u32[]{:S(2)}) %collective-permute-start.5) | collective-permute-done | bytes 884768 | tf_op jit(solution)/shard_map/ppermute | solution.py:43
  55.2 1.9 collective-permute-done.4.refs_6_
  57.1 1.4 collective-permute-start.7
  58.7 1.4 collective-permute-start.8
  60.1 1.9 collective-permute-start.9
  61.9 19.0 %collective-permute-done.7.refs_2_ = bf16[1728,256]{1,0:T(8,128)(2,1)S(1)} collective-permute-done((bf16[1728,256]{1,0:T(8,128)(2,1)}, bf16[1728,256]{1,0:T(8,128)(2,1)S(1)}, u32[]{:S(2)}, u32[]{:S(2)}) %collective-permute-start.7) | collective-permute-done | bytes 884768 | tf_op jit(solution)/shard_map/ppermute | solution.py:43
  80.9 3.8 %collective-permute-start.13 = (bf16[1728,256]{1,0:T(8,128)(2,1)}, bf16[1728,256]{1,0:T(8,128)(2,1)}, u32[]{:S(2)}, u32[]{:S(2)}) collective-permute-start(bf16[1728,256]{1,0:T(8,128)(2,1)} %collective-permute-done.2.refs_0_), channel_id=1, source_target_pairs={{0,12},{1,13},{2,14},{3,15},{4,0},{5,1},{6,2},{7,3},{8,4},{9,5},{1... | collective-permute-start | bytes 2654216 | tf_op jit(solution)/shard_map/ppermute | solution.py:43
  85.5 8.1 %early_pass.2.acc = f32[8,256,256]{2,1,0:T(8,128)S(1)} custom-call(bf16[256,1152]{1,0:T(8,128)(2,1)S(1)} %get-tuple-element.156.normed, bf16[1728,256]{1,0:T(8,128)(2,1)S(1)} %pack.2.refs_0_, bf16[1728,256]{1,0:T(8,128)(2,1)} %collective-permute-done.1.refs_1_, bf16[1728,256]{1,0:T(8,128)(2,1)S(1)} %collective-permute-done.3.refs_2_, ...), custom_call_target="tpu_custom_call" | custom-call | flops 1200000000 | bytes 20000000 | tf_op jit(solution)/shard_map/early_pass/pallas_call | solution.py:375
  93.6 1.4 pad_maximum_fusion.1
  95.0 9.5 %collective-permute-done.13.refs_4_ = bf16[1728,256]{1,0:T(8,128)(2,1)} collective-permute-done((bf16[1728,256]{1,0:T(8,128)(2,1)}, bf16[1728,256]{1,0:T(8,128)(2,1)}, u32[]{:S(2)}, u32[]{:S(2)}) %collective-permute-start.13) | collective-permute-done | bytes 884768 | tf_op jit(solution)/shard_map/ppermute | solution.py:43
  104.5 3.4 %collective-permute-done.12.refs_9_ = bf16[1728,256]{1,0:T(8,128)(2,1)S(1)} collective-permute-done((bf16[1728,256]{1,0:T(8,128)(2,1)S(1)}, bf16[1728,256]{1,0:T(8,128)(2,1)S(1)}, u32[]{:S(2)}, u32[]{:S(2)}) %collective-permute-start.12) | collective-permute-done | bytes 884768 | tf_op jit(solution)/shard_map/ppermute | solution.py:43
  108.6 3.0 %collective-permute-start.17 = (bf16[1728,256]{1,0:T(8,128)(2,1)}, bf16[1728,256]{1,0:T(8,128)(2,1)}, u32[]{:S(2)}, u32[]{:S(2)}) collective-permute-start(bf16[1728,256]{1,0:T(8,128)(2,1)} %collective-permute-done.13.refs_4_), channel_id=1, source_target_pairs={{0,2},{1,3},{2,0},{3,1},{4,6},{5,7},{6,4},{7,5},{8,10},{9,11},{10,... | collective-permute-start | bytes 2654216 | tf_op jit(solution)/shard_map/ppermute | solution.py:43
  111.6 2.8 %collective-permute-done.21.refs_12_ = bf16[1728,256]{1,0:T(8,128)(2,1)S(1)} collective-permute-done((bf16[1728,256]{1,0:T(8,128)(2,1)S(1)}, bf16[1728,256]{1,0:T(8,128)(2,1)S(1)}, u32[]{:S(2)}, u32[]{:S(2)}) %collective-permute-start.21) | collective-permute-done | bytes 884768 | tf_op jit(solution)/shard_map/ppermute | solution.py:43
  115.7 16.6 %own_pass.1 = (bf16[512,256]{1,0:T(8,128)(2,1)S(1)}, bf16[512,256]{1,0:T(8,128)(2,1)S(1)}, bf16[8,256,256]{2,1,0:T(8,128)(2,1)S(1)}, f32[256,2304]{1,0:T(8,128)S...) custom-call(s32[1]{0:T(128)} %bitcast.pos_ref, bf16[256,2304]{1,0:T(8,128)(2,1)S(1)} %bitcast.17, ...), custom_call_target="tpu_custom_call" | custom-call | flops 3000000000 | bytes 30000000 | tf_op jit(solution)/shard_map/own_pass/pallas_call | solution.py:388
  132.3 1.5 copy-done.13
  137.5 1.6 copy-done.2
  139.8 1.7 copy-done.3
  143.9 6.3 %early_pass.3.acc = f32[8,256,256]{2,1,0:T(8,128)S(1)} custom-call(bf16[256,864]{1,0:T(8,128)(2,1)S(1)} %get-tuple-element.144.normed, bf16[1728,256]{1,0:T(8,128)(2,1)} %collective-permute-done.2.refs_0_, bf16[1728,256]{1,0:T(8,128)(2,1)S(1)} %copy-done.6, bf16[1728,256]{1,0:T(8,128)(2,1)S(1)} %copy-done.9, bf16[5184,256]{1,0:T(8,128)(2,1)S(1)} %copy-done.3), custom_call_target="tpu_custom_call" | custom-call | flops 1200000000 | bytes 20000000 | tf_op jit(solution)/shard_map/early_pass/pallas_call | solution.py:375
  150.2 1.4 copy-done.4
  152.8 14.8 %peer_pass.1 = (f32[256,1]{1,0:T(8,128)S(1)}, bf16[256,2304]{1,0:T(8,128)(2,1)S(1)}) custom-call(s32[1]{0:T(128)} %bitcast.pos_ref, bf16[256,2304]{1,0:T(8,128)(2,1)S(1)} %bitcast.18, f32[2,2304]{1,0:T(2,128)S(1)} %copy-done.25, bf16[2304,256]{1,0:T(8,128)(2,1)S(1)} %copy-done.12, bf16[256,1440]{1,0:T(8,128)(2,1)S(1)} %copy-done.17, ...), custom_call_target="tpu_custom_call" | custom-call | flops 3000000000 | bytes 30000000 | tf_op jit(solution)/shard_map/peer_pass/pallas_call | solution.py:413
  168.5 4.9 %attention_back.1.d_mine = bf16[8,256,256]{2,1,0:T(8,128)(2,1)S(1)} custom-call(bf16[256,2304]{1,0:T(8,128)(2,1)S(1)} %get-tuple-element.176.dhidden.d_mine, bf16[1024,2304]{1,0:T(8,128)(2,1)S(1)} %bitcast.20, bf16[8,256,256]{2,1,0:T(8,128)(2,1)S(1)} %copy-done.15), custom_call_target="tpu_custom_call" | custom-call | flops 2000000000 | bytes 16000000 | tf_op jit(solution)/shard_map/attention_back/pallas_call | solution.py:433
  174.0 2.5 %collective-permute-done.29.other = bf16[512,256]{1,0:T(8,128)(2,1)S(1)} collective-permute-done((bf16[512,256]{1,0:T(8,128)(2,1)S(1)}, bf16[512,256]{1,0:T(8,128)(2,1)S(1)}, u32[]{:S(2)}, u32[]{:S(2)}) %collective-permute-start.29) | collective-permute-done | bytes 262176 | tf_op jit(solution)/shard_map/ppermute | solution.py:43
  176.5 3.0 %out_grads.1 = (bf16[576,256]{1,0:T(8,128)(2,1)S(1)}, bf16[576,256]{1,0:T(8,128)(2,1)S(1)}, bf16[576,256]{1,0:T(8,128)(2,1)S(1)}, bf16[576,256]{1,0:T(8,128)(2,1...) custom-call(s32[1]{0:T(128)} %bitcast.pos_ref, ...), custom_call_target="tpu_custom_call" | custom-call | flops 1207959552 | bytes 10000000 | tf_op jit(solution)/shard_map/out_grads/pallas_call | solution.py:446
  179.5 3.0 %collective-permute-start.31 = (bf16[192,256]{1,0:T(8,128)(2,1)S(1)}, bf16[192,256]{1,0:T(8,128)(2,1)S(1)}, u32[]{:S(2)}, u32[]{:S(2)}) collective-permute-start(bf16[192,256]{1,0:T(8,128)(2,1)S(1)} %get-tuple-element.194), channel_id=1, source_target_pairs={{0,2},{1,3},{2,0},{3,1},{4,6},{5,7},{6,4},{7,5},{8,10},{9,11},{10,... | collective-permute-start | bytes 294920 | tf_op jit(solution)/shard_map/ppermute | solution.py:43
  182.6 1.7 collective-permute-start.32
  184.6 5.1 %qkv_grads.1 = (bf16[1152,256]{1,0:T(8,128)(2,1)S(1)}, bf16[1152,256]{1,0:T(8,128)(2,1)S(1)}, bf16[1152,256]{1,0:T(8,128)(2,1)S(1)}, bf16[1152,256]{1,0:T(8,128)...) custom-call(s32[1]{0:T(128)} %bitcast.pos_ref, ...), custom_call_target="tpu_custom_call" | custom-call | flops 2415919104 | bytes 10000000 | tf_op jit(solution)/shard_map/qkv_grads/pallas_call | solution.py:446
  190.9 2.6 %collective-permute-start.35 = (bf16[384,256]{1,0:T(8,128)(2,1)S(1)}, bf16[384,256]{1,0:T(8,128)(2,1)S(1)}, u32[]{:S(2)}, u32[]{:S(2)}) collective-permute-start(bf16[384,256]{1,0:T(8,128)(2,1)S(1)} %get-tuple-element.234), channel_id=1, source_target_pairs={{0,12},{1,13},{2,14},{3,15},{4,0},{5,1},{6,2},{7,3},{8,4},{9,5},{1... | collective-permute-start | bytes 589832 | tf_op jit(solution)/shard_map/ppermute | solution.py:43
  193.4 4.1 %collective-permute-done.34.in_a = bf16[384,256]{1,0:T(8,128)(2,1)S(1)} collective-permute-done((bf16[384,256]{1,0:T(8,128)(2,1)S(1)}, bf16[384,256]{1,0:T(8,128)(2,1)S(1)}, u32[]{:S(2)}, u32[]{:S(2)}) %collective-permute-start.34) | collective-permute-done | bytes 196640 | tf_op jit(solution)/shard_map/ppermute | solution.py:43
  197.6 2.7 %collective-permute-done.36.in_c = bf16[384,256]{1,0:T(8,128)(2,1)S(1)} collective-permute-done((bf16[384,256]{1,0:T(8,128)(2,1)S(1)}, bf16[384,256]{1,0:T(8,128)(2,1)S(1)}, u32[]{:S(2)}, u32[]{:S(2)}) %collective-permute-start.36) | collective-permute-done | bytes 196640 | tf_op jit(solution)/shard_map/ppermute | solution.py:43
  200.6 3.2 %collective-permute-start.38 = (bf16[1152,256]{1,0:T(8,128)(2,1)S(1)}, bf16[1152,256]{1,0:T(8,128)(2,1)S(1)}, u32[]{:S(2)}, u32[]{:S(2)}) collective-permute-start(bf16[1152,256]{1,0:T(8,128)(2,1)S(1)} %get-tuple-element.240), channel_id=1, source_target_pairs={{0,12},{1,13},{2,14},{3,15},{4,0},{5,1},{6,2},{7,3},{8,4},{9,5},{1... | collective-permute-start | bytes 1769480 | tf_op jit(solution)/shard_map/ppermute | solution.py:43
  203.8 3.0 %collective-permute-start.39 = (bf16[1152,256]{1,0:T(8,128)(2,1)S(1)}, bf16[1152,256]{1,0:T(8,128)(2,1)S(1)}, u32[]{:S(2)}, u32[]{:S(2)}) collective-permute-start(bf16[1152,256]{1,0:T(8,128)(2,1)S(1)} %get-tuple-element.241), channel_id=1, source_target_pairs={{0,2},{1,3},{2,0},{3,1},{4,6},{5,7},{6,4},{7,5},{8,10},{9,11},{10,... | collective-permute-start | bytes 1769480 | tf_op jit(solution)/shard_map/ppermute | solution.py:43
  206.8 3.2 %collective-permute-start.44 = (bf16[576,256]{1,0:T(8,128)(2,1)S(1)}, bf16[576,256]{1,0:T(8,128)(2,1)S(1)}, u32[]{:S(2)}, u32[]{:S(2)}) collective-permute-start(bf16[576,256]{1,0:T(8,128)(2,1)S(1)} %get-tuple-element.258), channel_id=1, source_target_pairs={{0,12},{1,13},{2,14},{3,15},{4,0},{5,1},{6,2},{7,3},{8,4},{9,5},{1... | collective-permute-start | bytes 884744 | tf_op jit(solution)/shard_map/ppermute | solution.py:43
  210.0 7.8 %collective-permute-done.37.in_x = bf16[1152,256]{1,0:T(8,128)(2,1)S(1)} collective-permute-done((bf16[1152,256]{1,0:T(8,128)(2,1)S(1)}, bf16[1152,256]{1,0:T(8,128)(2,1)S(1)}, u32[]{:S(2)}, u32[]{:S(2)}) %collective-permute-start.37) | collective-permute-done | bytes 589856 | tf_op jit(solution)/shard_map/ppermute | solution.py:43
  217.7 3.0 %collective-permute-start.45 = (bf16[576,256]{1,0:T(8,128)(2,1)S(1)}, bf16[576,256]{1,0:T(8,128)(2,1)S(1)}, u32[]{:S(2)}, u32[]{:S(2)}) collective-permute-start(bf16[576,256]{1,0:T(8,128)(2,1)S(1)} %get-tuple-element.259), channel_id=1, source_target_pairs={{0,2},{1,3},{2,0},{3,1},{4,6},{5,7},{6,4},{7,5},{8,10},{9,11},{10,... | collective-permute-start | bytes 884744 | tf_op jit(solution)/shard_map/ppermute | solution.py:43
  222.6 2.0 collective-permute-start.40
  224.6 3.0 %collective-permute-start.42 = (bf16[1152,256]{1,0:T(8,128)(2,1)}, bf16[1152,256]{1,0:T(8,128)(2,1)S(1)}, u32[]{:S(2)}, u32[]{:S(2)}) collective-permute-start(bf16[1152,256]{1,0:T(8,128)(2,1)} %get-tuple-element.247), channel_id=1, source_target_pairs={{0,2},{1,3},{2,0},{3,1},{4,6},{5,7},{6,4},{7,5},{8,10},{9,11},{10,... | collective-permute-start | bytes 1769480 | tf_op jit(solution)/shard_map/ppermute | solution.py:43
  227.5 1.6 collective-permute-done.45.in_y
  230.7 2.5 %collective-permute-start.48 = (bf16[576,256]{1,0:T(8,128)(2,1)}, bf16[576,256]{1,0:T(8,128)(2,1)S(1)}, u32[]{:S(2)}, u32[]{:S(2)}) collective-permute-start(bf16[576,256]{1,0:T(8,128)(2,1)} %get-tuple-element.265), channel_id=1, source_target_pairs={{0,2},{1,3},{2,0},{3,1},{4,6},{5,7},{6,4},{7,5},{8,10},{9,11},{10,... | collective-permute-start | bytes 884744 | tf_op jit(solution)/shard_map/ppermute | solution.py:43
  233.2 1.6 reduce
  234.8 5.8 %collective-permute-done.46.refs_1_ = bf16[576,256]{1,0:T(8,128)(2,1)S(1)} collective-permute-done((bf16[576,256]{1,0:T(8,128)(2,1)}, bf16[576,256]{1,0:T(8,128)(2,1)S(1)}, u32[]{:S(2)}, u32[]{:S(2)}) %collective-permute-start.46) | collective-permute-done | bytes 294944 | tf_op jit(solution)/shard_map/ppermute | solution.py:43
  240.5 3.5 %collective-permute-done.48.refs_3_ = bf16[576,256]{1,0:T(8,128)(2,1)S(1)} collective-permute-done((bf16[576,256]{1,0:T(8,128)(2,1)}, bf16[576,256]{1,0:T(8,128)(2,1)S(1)}, u32[]{:S(2)}, u32[]{:S(2)}) %collective-permute-start.48) | collective-permute-done | bytes 294944 | tf_op jit(solution)/shard_map/ppermute | solution.py:43
  (155 shorter events, 32.7 us)
Async XLA Ops:
  4.5 21.7 %collective-permute-start = (bf16[1728,256]{1,0:T(8,128)(2,1)S(1)}, bf16[1728,256]{1,0:T(8,128)(2,1)S(1)}, u32[]{:S(2)}, u32[]{:S(2)}) collective-permute-start(bf16[1728,256]{1,0:T(8,128)(2,1)S(1)} %pack.2.refs_0_), channel_id=1, source_target_pairs={{0,12},{1,13},{2,14},{3,15},{4,0},{5,1},{6,2},{7,3},{8,4},{9,5},{1... | collective-permute-start | bytes 2654216 | tf_op jit(solution)/shard_map/ppermute | solution.py:43
  7.4 22.4 %collective-permute-start.1 = (bf16[1728,256]{1,0:T(8,128)(2,1)S(1)}, bf16[1728,256]{1,0:T(8,128)(2,1)}, u32[]{:S(2)}, u32[]{:S(2)}) collective-permute-start(bf16[1728,256]{1,0:T(8,128)(2,1)S(1)} %pack.2.refs_0_), channel_id=1, source_target_pairs={{0,4},{1,5},{2,6},{3,7},{4,8},{5,9},{6,10},{7,11},{8,12},{9,13},{1... | collective-permute-start | bytes 2654216 | tf_op jit(solution)/shard_map/ppermute | solution.py:43
  12.1 21.4 %collective-permute-start.2 = (bf16[1728,256]{1,0:T(8,128)(2,1)}, bf16[1728,256]{1,0:T(8,128)(2,1)}, u32[]{:S(2)}, u32[]{:S(2)}) collective-permute-start(bf16[1728,256]{1,0:T(8,128)(2,1)} %pack.3), channel_id=1, source_target_pairs={{0,16},{16,32},{32,48},{48,64},{64,80},{80,96},{96,112},{112,0},{1... | collective-permute-start | bytes 2654216 | tf_op jit(solution)/shard_map/ppermute | solution.py:550
  33.5 21.6 %collective-permute-start.5 = (bf16[1728,256]{1,0:T(8,128)(2,1)}, bf16[1728,256]{1,0:T(8,128)(2,1)S(1)}, u32[]{:S(2)}, u32[]{:S(2)}) collective-permute-start(bf16[1728,256]{1,0:T(8,128)(2,1)} %collective-permute-done.2.refs_0_), channel_id=1, source_target_pairs={{0,4},{1,5},{2,6},{3,7},{4,8},{5,9},{6,10},{7,11},{8,12},{9,13},{1... | collective-permute-start | bytes 2654216 | tf_op jit(solution)/shard_map/ppermute | solution.py:43
  34.0 21.2 %collective-permute-start.3 = (bf16[1728,256]{1,0:T(8,128)(2,1)S(1)}, bf16[1728,256]{1,0:T(8,128)(2,1)S(1)}, u32[]{:S(2)}, u32[]{:S(2)}) collective-permute-start(bf16[1728,256]{1,0:T(8,128)(2,1)S(1)} %pack.2.refs_0_), channel_id=1, source_target_pairs={{0,2},{1,3},{2,0},{3,1},{4,6},{5,7},{6,4},{7,5},{8,10},{9,11},{10,... | collective-permute-start | bytes 2654216 | tf_op jit(solution)/shard_map/ppermute | solution.py:43
  37.2 19.9 %collective-permute-start.4 = (bf16[1728,256]{1,0:T(8,128)(2,1)S(1)}, bf16[1728,256]{1,0:T(8,128)(2,1)S(1)}, u32[]{:S(2)}, u32[]{:S(2)}) collective-permute-start(bf16[1728,256]{1,0:T(8,128)(2,1)S(1)} %collective-permute-done.refs_3_), channel_id=1, source_target_pairs={{0,12},{1,13},{2,14},{3,15},{4,0},{5,1},{6,2},{7,3},{8,4},{9,5},{1... | collective-permute-start | bytes 2654216 | tf_op jit(solution)/shard_map/ppermute | solution.py:43
  57.1 28.1 %collective-permute-start.10 = (bf16[5184,256]{1,0:T(8,128)(2,1)S(1)}, bf16[5184,256]{1,0:T(8,128)(2,1)S(1)}, u32[]{:S(2)}, u32[]{:S(2)}) collective-permute-start(bf16[5184,256]{1,0:T(8,128)(2,1)S(1)} %pad_maximum_fusion), channel_id=1, source_target_pairs={{0,1},{1,0},{2,3},{3,2},{4,5},{5,4},{6,7},{7,6},{8,9},{9,8},{10,11... | collective-permute-start | bytes 7962632 | tf_op jit(solution)/shard_map/ppermute | solution.py:43
  57.1 23.8 %collective-permute-start.7 = (bf16[1728,256]{1,0:T(8,128)(2,1)}, bf16[1728,256]{1,0:T(8,128)(2,1)S(1)}, u32[]{:S(2)}, u32[]{:S(2)}) collective-permute-start(bf16[1728,256]{1,0:T(8,128)(2,1)} %collective-permute-done.2.refs_0_), channel_id=1, source_target_pairs={{0,2},{1,3},{2,0},{3,1},{4,6},{5,7},{6,4},{7,5},{8,10},{9,11},{10,... | collective-permute-start | bytes 2654216 | tf_op jit(solution)/shard_map/ppermute | solution.py:43
  58.5 22.4 %collective-permute-start.11 = (bf16[1728,256]{1,0:T(8,128)(2,1)S(1)}, bf16[1728,256]{1,0:T(8,128)(2,1)S(1)}, u32[]{:S(2)}, u32[]{:S(2)}) collective-permute-start(bf16[1728,256]{1,0:T(8,128)(2,1)S(1)} %collective-permute-done.4.refs_6_), channel_id=1, source_target_pairs={{0,1},{1,0},{2,3},{3,2},{4,5},{5,4},{6,7},{7,6},{8,9},{9,8},{10,11... | collective-permute-start | bytes 2654216 | tf_op jit(solution)/shard_map/ppermute | solution.py:43
  58.7 26.0 %collective-permute-start.8 = (bf16[1728,256]{1,0:T(8,128)(2,1)S(1)}, bf16[1728,256]{1,0:T(8,128)(2,1)S(1)}, u32[]{:S(2)}, u32[]{:S(2)}) collective-permute-start(bf16[1728,256]{1,0:T(8,128)(2,1)S(1)} %collective-permute-done.3.refs_2_), channel_id=1, source_target_pairs={{0,4},{1,5},{2,6},{3,7},{4,8},{5,9},{6,10},{7,11},{8,12},{9,13},{1... | collective-permute-start | bytes 2654216 | tf_op jit(solution)/shard_map/ppermute | solution.py:43
  60.1 25.2 %collective-permute-start.9 = (bf16[1728,256]{1,0:T(8,128)(2,1)S(1)}, bf16[1728,256]{1,0:T(8,128)(2,1)S(1)}, u32[]{:S(2)}, u32[]{:S(2)}) collective-permute-start(bf16[1728,256]{1,0:T(8,128)(2,1)S(1)} %collective-permute-done.3.refs_2_), channel_id=1, source_target_pairs={{0,12},{1,13},{2,14},{3,15},{4,0},{5,1},{6,2},{7,3},{8,4},{9,5},{1... | collective-permute-start | bytes 2654216 | tf_op jit(solution)/shard_map/ppermute | solution.py:43
  80.9 4.5 %collective-permute-start.16 = (bf16[1728,256]{1,0:T(8,128)(2,1)S(1)}, bf16[1728,256]{1,0:T(8,128)(2,1)S(1)}, u32[]{:S(2)}, u32[]{:S(2)}) collective-permute-start(bf16[1728,256]{1,0:T(8,128)(2,1)S(1)} %collective-permute-done.3.refs_2_), channel_id=1, source_target_pairs={{0,1},{1,0},{2,3},{3,2},{4,5},{5,4},{6,7},{7,6},{8,9},{9,8},{10,11... | collective-permute-start | bytes 2654216 | tf_op jit(solution)/shard_map/ppermute | solution.py:43
  80.9 23.6 %collective-permute-start.13 = (bf16[1728,256]{1,0:T(8,128)(2,1)}, bf16[1728,256]{1,0:T(8,128)(2,1)}, u32[]{:S(2)}, u32[]{:S(2)}) collective-permute-start(bf16[1728,256]{1,0:T(8,128)(2,1)} %collective-permute-done.2.refs_0_), channel_id=1, source_target_pairs={{0,12},{1,13},{2,14},{3,15},{4,0},{5,1},{6,2},{7,3},{8,4},{9,5},{1... | collective-permute-start | bytes 2654216 | tf_op jit(solution)/shard_map/ppermute | solution.py:43
  84.7 23.2 %collective-permute-start.12 = (bf16[1728,256]{1,0:T(8,128)(2,1)S(1)}, bf16[1728,256]{1,0:T(8,128)(2,1)S(1)}, u32[]{:S(2)}, u32[]{:S(2)}) collective-permute-start(bf16[1728,256]{1,0:T(8,128)(2,1)S(1)} %collective-permute-done.4.refs_6_), channel_id=1, source_target_pairs={{0,2},{1,3},{2,0},{3,1},{4,6},{5,7},{6,4},{7,5},{8,10},{9,11},{10,... | collective-permute-start | bytes 2654216 | tf_op jit(solution)/shard_map/ppermute | solution.py:43
  85.3 22.8 %collective-permute-start.14 = (bf16[1728,256]{1,0:T(8,128)(2,1)S(1)}, bf16[1728,256]{1,0:T(8,128)(2,1)}, u32[]{:S(2)}, u32[]{:S(2)}) collective-permute-start(bf16[1728,256]{1,0:T(8,128)(2,1)S(1)} %collective-permute-done.7.refs_2_), channel_id=1, source_target_pairs={{0,4},{1,5},{2,6},{3,7},{4,8},{5,9},{6,10},{7,11},{8,12},{9,13},{1... | collective-permute-start | bytes 2654216 | tf_op jit(solution)/shard_map/ppermute | solution.py:43
  85.3 22.7 %collective-permute-start.15 = (bf16[1728,256]{1,0:T(8,128)(2,1)S(1)}, bf16[1728,256]{1,0:T(8,128)(2,1)S(1)}, u32[]{:S(2)}, u32[]{:S(2)}) collective-permute-start(bf16[1728,256]{1,0:T(8,128)(2,1)S(1)} %collective-permute-done.8.refs_7_), channel_id=1, source_target_pairs={{0,1},{1,0},{2,3},{3,2},{4,5},{5,4},{6,7},{7,6},{8,9},{9,8},{10,11... | collective-permute-start | bytes 2654216 | tf_op jit(solution)/shard_map/ppermute | solution.py:43
  108.1 29.4 %collective-permute-start.20 = (bf16[5184,256]{1,0:T(8,128)(2,1)S(1)}, bf16[5184,256]{1,0:T(8,128)(2,1)S(1)}, u32[]{:S(2)}, u32[]{:S(2)}) collective-permute-start(bf16[5184,256]{1,0:T(8,128)(2,1)S(1)} %pad_maximum_fusion.1), channel_id=1, source_target_pairs={{0,1},{1,0},{2,3},{3,2},{4,5},{5,4},{6,7},{7,6},{8,9},{9,8},{10,11... | collective-permute-start | bytes 7962632 | tf_op jit(solution)/shard_map/ppermute | solution.py:43
  108.1 6.2 %collective-permute-start.21 = (bf16[1728,256]{1,0:T(8,128)(2,1)S(1)}, bf16[1728,256]{1,0:T(8,128)(2,1)S(1)}, u32[]{:S(2)}, u32[]{:S(2)}) collective-permute-start(bf16[1728,256]{1,0:T(8,128)(2,1)S(1)} %collective-permute-done.9.refs_8_), channel_id=1, source_target_pairs={{0,1},{1,0},{2,3},{3,2},{4,5},{5,4},{6,7},{7,6},{8,9},{9,8},{10,11... | collective-permute-start | bytes 2654216 | tf_op jit(solution)/shard_map/ppermute | solution.py:43
  108.6 7.0 %collective-permute-start.22 = (bf16[1728,256]{1,0:T(8,128)(2,1)S(1)}, bf16[1728,256]{1,0:T(8,128)(2,1)S(1)}, u32[]{:S(2)}, u32[]{:S(2)}) collective-permute-start(bf16[1728,256]{1,0:T(8,128)(2,1)S(1)} %collective-permute-done.12.refs_9_), channel_id=1, source_target_pairs={{0,1},{1,0},{2,3},{3,2},{4,5},{5,4},{6,7},{7,6},{8,9},{9,8},{10,11... | collective-permute-start | bytes 2654216 | tf_op jit(solution)/shard_map/ppermute | solution.py:43
  108.6 28.3 %collective-permute-start.17 = (bf16[1728,256]{1,0:T(8,128)(2,1)}, bf16[1728,256]{1,0:T(8,128)(2,1)}, u32[]{:S(2)}, u32[]{:S(2)}) collective-permute-start(bf16[1728,256]{1,0:T(8,128)(2,1)} %collective-permute-done.13.refs_4_), channel_id=1, source_target_pairs={{0,2},{1,3},{2,0},{3,1},{4,6},{5,7},{6,4},{7,5},{8,10},{9,11},{10,... | collective-permute-start | bytes 2654216 | tf_op jit(solution)/shard_map/ppermute | solution.py:43
  111.6 25.7 %collective-permute-start.18 = (bf16[1728,256]{1,0:T(8,128)(2,1)}, bf16[1728,256]{1,0:T(8,128)(2,1)}, u32[]{:S(2)}, u32[]{:S(2)}) collective-permute-start(bf16[1728,256]{1,0:T(8,128)(2,1)} %collective-permute-done.13.refs_4_), channel_id=1, source_target_pairs={{0,12},{1,13},{2,14},{3,15},{4,0},{5,1},{6,2},{7,3},{8,4},{9,5},{1... | collective-permute-start | bytes 2654216 | tf_op jit(solution)/shard_map/ppermute | solution.py:43
  114.3 23.2 %collective-permute-start.19 = (bf16[1728,256]{1,0:T(8,128)(2,1)}, bf16[1728,256]{1,0:T(8,128)(2,1)}, u32[]{:S(2)}, u32[]{:S(2)}) collective-permute-start(bf16[1728,256]{1,0:T(8,128)(2,1)} %collective-permute-done.14.refs_6_), channel_id=1, source_target_pairs={{0,4},{1,5},{2,6},{3,7},{4,8},{5,9},{6,10},{7,11},{8,12},{9,13},{1... | collective-permute-start | bytes 2654216 | tf_op jit(solution)/shard_map/ppermute | solution.py:43
  115.6 36.0 %collective-permute-start.23 = (bf16[1728,256]{1,0:T(8,128)(2,1)}, bf16[1728,256]{1,0:T(8,128)(2,1)}, u32[]{:S(2)}, u32[]{:S(2)}) collective-permute-start(bf16[1728,256]{1,0:T(8,128)(2,1)} %collective-permute-done.13.refs_4_), channel_id=1, source_target_pairs={{0,1},{1,0},{2,3},{3,2},{4,5},{5,4},{6,7},{7,6},{8,9},{9,8},{10,11... | collective-permute-start | bytes 2654216 | tf_op jit(solution)/shard_map/ppermute | solution.py:43
  136.9 14.7 %collective-permute-start.25 = (bf16[1728,256]{1,0:T(8,128)(2,1)}, bf16[1728,256]{1,0:T(8,128)(2,1)S(1)}, u32[]{:S(2)}, u32[]{:S(2)}) collective-permute-start(bf16[1728,256]{1,0:T(8,128)(2,1)} %collective-permute-done.14.refs_6_), channel_id=1, source_target_pairs={{0,1},{1,0},{2,3},{3,2},{4,5},{5,4},{6,7},{7,6},{8,9},{9,8},{10,11... | collective-permute-start | bytes 2654216 | tf_op jit(solution)/shard_map/ppermute | solution.py:43
  139.1 12.5 %collective-permute-start.24 = (bf16[1728,256]{1,0:T(8,128)(2,1)}, bf16[1728,256]{1,0:T(8,128)(2,1)S(1)}, u32[]{:S(2)}, u32[]{:S(2)}) collective-permute-start(bf16[1728,256]{1,0:T(8,128)(2,1)} %collective-permute-done.18.refs_5_), channel_id=1, source_target_pairs={{0,1},{1,0},{2,3},{3,2},{4,5},{5,4},{6,7},{7,6},{8,9},{9,8},{10,11... | collective-permute-start | bytes 2654216 | tf_op jit(solution)/shard_map/ppermute | solution.py:43
  139.1 12.5 %collective-permute-start.26 = (bf16[1728,256]{1,0:T(8,128)(2,1)}, bf16[1728,256]{1,0:T(8,128)(2,1)}, u32[]{:S(2)}, u32[]{:S(2)}) collective-permute-start(bf16[1728,256]{1,0:T(8,128)(2,1)} %collective-permute-done.17.refs_7_), channel_id=1, source_target_pairs={{0,1},{1,0},{2,3},{3,2},{4,5},{5,4},{6,7},{7,6},{8,9},{9,8},{10,11... | collective-permute-start | bytes 2654216 | tf_op jit(solution)/shard_map/ppermute | solution.py:43
  139.6 12.0 %collective-permute-start.27 = (bf16[1728,256]{1,0:T(8,128)(2,1)}, bf16[1728,256]{1,0:T(8,128)(2,1)}, u32[]{:S(2)}, u32[]{:S(2)}) collective-permute-start(bf16[1728,256]{1,0:T(8,128)(2,1)} %collective-permute-done.19.refs_8_), channel_id=1, source_target_pairs={{0,1},{1,0},{2,3},{3,2},{4,5},{5,4},{6,7},{7,6},{8,9},{9,8},{10,11... | collective-permute-start | bytes 2654216 | tf_op jit(solution)/shard_map/ppermute | solution.py:43
  167.6 8.9 %collective-permute-start.30 = (bf16[256,2304]{1,0:T(8,128)(2,1)S(1)}, bf16[256,2304]{1,0:T(8,128)(2,1)S(1)}, u32[]{:S(2)}, u32[]{:S(2)}) collective-permute-start(bf16[256,2304]{1,0:T(8,128)(2,1)S(1)} %get-tuple-element.176.dhidden.d_mine), channel_id=1, source_target_pairs={{0,1},{1,0},{2,3},{3,2},{4,5},{5,4},{6,7},{7,6},{8,9},{9,8},{10,11... | collective-permute-start | bytes 3538952 | tf_op jit(solution)/shard_map/ppermute | solution.py:43
  173.4 6.1 %collective-permute-start.28 = (bf16[8,256,256]{2,1,0:T(8,128)(2,1)S(1)}, bf16[8,256,256]{2,1,0:T(8,128)(2,1)S(1)}, u32[]{:S(2)}, u32[]{:S(2)}) collective-permute-start(bf16[8,256,256]{2,1,0:T(8,128)(2,1)S(1)} %attention_back.1.d_mine), channel_id=1, source_target_pairs={{0,1},{1,0},{2,3},{3,2},{4,5},{5,4},{6,7},{7,6},{8,9},{9,8},{10,11... | collective-permute-start | bytes 3145736 | tf_op jit(solution)/shard_map/ppermute | solution.py:43
  173.5 3.0 %collective-permute-start.29 = (bf16[512,256]{1,0:T(8,128)(2,1)S(1)}, bf16[512,256]{1,0:T(8,128)(2,1)S(1)}, u32[]{:S(2)}, u32[]{:S(2)}) collective-permute-start(bf16[512,256]{1,0:T(8,128)(2,1)S(1)} %copy-done.38), channel_id=1, source_target_pairs={{0,1},{1,0},{2,3},{3,2},{4,5},{5,4},{6,7},{7,6},{8,9},{9,8},{10,11... | collective-permute-start | bytes 786440 | tf_op jit(solution)/shard_map/ppermute | solution.py:43
  179.5 10.2 %collective-permute-start.31 = (bf16[192,256]{1,0:T(8,128)(2,1)S(1)}, bf16[192,256]{1,0:T(8,128)(2,1)S(1)}, u32[]{:S(2)}, u32[]{:S(2)}) collective-permute-start(bf16[192,256]{1,0:T(8,128)(2,1)S(1)} %get-tuple-element.194), channel_id=1, source_target_pairs={{0,2},{1,3},{2,0},{3,1},{4,6},{5,7},{6,4},{7,5},{8,10},{9,11},{10,... | collective-permute-start | bytes 294920 | tf_op jit(solution)/shard_map/ppermute | solution.py:43
  182.6 7.2 %collective-permute-start.32 = (bf16[192,256]{1,0:T(8,128)(2,1)S(1)}, bf16[192,256]{1,0:T(8,128)(2,1)S(1)}, u32[]{:S(2)}, u32[]{:S(2)}) collective-permute-start(bf16[192,256]{1,0:T(8,128)(2,1)S(1)} %get-tuple-element.195), channel_id=1, source_target_pairs={{0,12},{1,13},{2,14},{3,15},{4,0},{5,1},{6,2},{7,3},{8,4},{9,5},{1... | collective-permute-start | bytes 294920 | tf_op jit(solution)/shard_map/ppermute | solution.py:43
  184.3 5.8 %collective-permute-start.33 = (bf16[192,256]{1,0:T(8,128)(2,1)S(1)}, bf16[192,256]{1,0:T(8,128)(2,1)S(1)}, u32[]{:S(2)}, u32[]{:S(2)}) collective-permute-start(bf16[192,256]{1,0:T(8,128)(2,1)S(1)} %get-tuple-element.196), channel_id=1, source_target_pairs={{0,4},{1,5},{2,6},{3,7},{4,8},{5,9},{6,10},{7,11},{8,12},{9,13},{1... | collective-permute-start | bytes 294920 | tf_op jit(solution)/shard_map/ppermute | solution.py:43
  190.2 7.4 %collective-permute-start.34 = (bf16[384,256]{1,0:T(8,128)(2,1)S(1)}, bf16[384,256]{1,0:T(8,128)(2,1)S(1)}, u32[]{:S(2)}, u32[]{:S(2)}) collective-permute-start(bf16[384,256]{1,0:T(8,128)(2,1)S(1)} %get-tuple-element.233), channel_id=1, source_target_pairs={{0,2},{1,3},{2,0},{3,1},{4,6},{5,7},{6,4},{7,5},{8,10},{9,11},{10,... | collective-permute-start | bytes 589832 | tf_op jit(solution)/shard_map/ppermute | solution.py:43
  190.9 6.7 %collective-permute-start.35 = (bf16[384,256]{1,0:T(8,128)(2,1)S(1)}, bf16[384,256]{1,0:T(8,128)(2,1)S(1)}, u32[]{:S(2)}, u32[]{:S(2)}) collective-permute-start(bf16[384,256]{1,0:T(8,128)(2,1)S(1)} %get-tuple-element.234), channel_id=1, source_target_pairs={{0,12},{1,13},{2,14},{3,15},{4,0},{5,1},{6,2},{7,3},{8,4},{9,5},{1... | collective-permute-start | bytes 589832 | tf_op jit(solution)/shard_map/ppermute | solution.py:43
  193.4 6.9 %collective-permute-start.36 = (bf16[384,256]{1,0:T(8,128)(2,1)S(1)}, bf16[384,256]{1,0:T(8,128)(2,1)S(1)}, u32[]{:S(2)}, u32[]{:S(2)}) collective-permute-start(bf16[384,256]{1,0:T(8,128)(2,1)S(1)} %get-tuple-element.235), channel_id=1, source_target_pairs={{0,4},{1,5},{2,6},{3,7},{4,8},{5,9},{6,10},{7,11},{8,12},{9,13},{1... | collective-permute-start | bytes 589832 | tf_op jit(solution)/shard_map/ppermute | solution.py:43
  200.5 17.3 %collective-permute-start.37 = (bf16[1152,256]{1,0:T(8,128)(2,1)S(1)}, bf16[1152,256]{1,0:T(8,128)(2,1)S(1)}, u32[]{:S(2)}, u32[]{:S(2)}) collective-permute-start(bf16[1152,256]{1,0:T(8,128)(2,1)S(1)} %get-tuple-element.239), channel_id=1, source_target_pairs={{0,4},{1,5},{2,6},{3,7},{4,8},{5,9},{6,10},{7,11},{8,12},{9,13},{1... | collective-permute-start | bytes 1769480 | tf_op jit(solution)/shard_map/ppermute | solution.py:43
  200.6 20.1 %collective-permute-start.38 = (bf16[1152,256]{1,0:T(8,128)(2,1)S(1)}, bf16[1152,256]{1,0:T(8,128)(2,1)S(1)}, u32[]{:S(2)}, u32[]{:S(2)}) collective-permute-start(bf16[1152,256]{1,0:T(8,128)(2,1)S(1)} %get-tuple-element.240), channel_id=1, source_target_pairs={{0,12},{1,13},{2,14},{3,15},{4,0},{5,1},{6,2},{7,3},{8,4},{9,5},{1... | collective-permute-start | bytes 1769480 | tf_op jit(solution)/shard_map/ppermute | solution.py:43
  203.8 17.5 %collective-permute-start.39 = (bf16[1152,256]{1,0:T(8,128)(2,1)S(1)}, bf16[1152,256]{1,0:T(8,128)(2,1)S(1)}, u32[]{:S(2)}, u32[]{:S(2)}) collective-permute-start(bf16[1152,256]{1,0:T(8,128)(2,1)S(1)} %get-tuple-element.241), channel_id=1, source_target_pairs={{0,2},{1,3},{2,0},{3,1},{4,6},{5,7},{6,4},{7,5},{8,10},{9,11},{10,... | collective-permute-start | bytes 1769480 | tf_op jit(solution)/shard_map/ppermute | solution.py:43
  206.8 15.8 %collective-permute-start.43 = (bf16[576,256]{1,0:T(8,128)(2,1)S(1)}, bf16[576,256]{1,0:T(8,128)(2,1)S(1)}, u32[]{:S(2)}, u32[]{:S(2)}) collective-permute-start(bf16[576,256]{1,0:T(8,128)(2,1)S(1)} %get-tuple-element.257), channel_id=1, source_target_pairs={{0,4},{1,5},{2,6},{3,7},{4,8},{5,9},{6,10},{7,11},{8,12},{9,13},{1... | collective-permute-start | bytes 884744 | tf_op jit(solution)/shard_map/ppermute | solution.py:43
  206.8 17.8 %collective-permute-start.44 = (bf16[576,256]{1,0:T(8,128)(2,1)S(1)}, bf16[576,256]{1,0:T(8,128)(2,1)S(1)}, u32[]{:S(2)}, u32[]{:S(2)}) collective-permute-start(bf16[576,256]{1,0:T(8,128)(2,1)S(1)} %get-tuple-element.258), channel_id=1, source_target_pairs={{0,12},{1,13},{2,14},{3,15},{4,0},{5,1},{6,2},{7,3},{8,4},{9,5},{1... | collective-permute-start | bytes 884744 | tf_op jit(solution)/shard_map/ppermute | solution.py:43
  217.7 11.4 %collective-permute-start.45 = (bf16[576,256]{1,0:T(8,128)(2,1)S(1)}, bf16[576,256]{1,0:T(8,128)(2,1)S(1)}, u32[]{:S(2)}, u32[]{:S(2)}) collective-permute-start(bf16[576,256]{1,0:T(8,128)(2,1)S(1)} %get-tuple-element.259), channel_id=1, source_target_pairs={{0,2},{1,3},{2,0},{3,1},{4,6},{5,7},{6,4},{7,5},{8,10},{9,11},{10,... | collective-permute-start | bytes 884744 | tf_op jit(solution)/shard_map/ppermute | solution.py:43
  220.7 9.9 %collective-permute-start.47 = (bf16[576,256]{1,0:T(8,128)(2,1)S(1)}, bf16[576,256]{1,0:T(8,128)(2,1)S(1)}, u32[]{:S(2)}, u32[]{:S(2)}) collective-permute-start(bf16[576,256]{1,0:T(8,128)(2,1)S(1)} %get-tuple-element.264), channel_id=1, source_target_pairs={{0,12},{1,13},{2,14},{3,15},{4,0},{5,1},{6,2},{7,3},{8,4},{9,5},{1... | collective-permute-start | bytes 884744 | tf_op jit(solution)/shard_map/ppermute | solution.py:43
  221.3 23.7 %collective-permute-start.41 = (bf16[1152,256]{1,0:T(8,128)(2,1)}, bf16[1152,256]{1,0:T(8,128)(2,1)S(1)}, u32[]{:S(2)}, u32[]{:S(2)}) collective-permute-start(bf16[1152,256]{1,0:T(8,128)(2,1)} %get-tuple-element.246), channel_id=1, source_target_pairs={{0,12},{1,13},{2,14},{3,15},{4,0},{5,1},{6,2},{7,3},{8,4},{9,5},{1... | collective-permute-start | bytes 1769480 | tf_op jit(solution)/shard_map/ppermute | solution.py:43
  222.6 22.4 %collective-permute-start.40 = (bf16[1152,256]{1,0:T(8,128)(2,1)}, bf16[1152,256]{1,0:T(8,128)(2,1)S(1)}, u32[]{:S(2)}, u32[]{:S(2)}) collective-permute-start(bf16[1152,256]{1,0:T(8,128)(2,1)} %get-tuple-element.245), channel_id=1, source_target_pairs={{0,4},{1,5},{2,6},{3,7},{4,8},{5,9},{6,10},{7,11},{8,12},{9,13},{1... | collective-permute-start | bytes 1769480 | tf_op jit(solution)/shard_map/ppermute | solution.py:43
  224.6 20.4 %collective-permute-start.42 = (bf16[1152,256]{1,0:T(8,128)(2,1)}, bf16[1152,256]{1,0:T(8,128)(2,1)S(1)}, u32[]{:S(2)}, u32[]{:S(2)}) collective-permute-start(bf16[1152,256]{1,0:T(8,128)(2,1)} %get-tuple-element.247), channel_id=1, source_target_pairs={{0,2},{1,3},{2,0},{3,1},{4,6},{5,7},{6,4},{7,5},{8,10},{9,11},{10,... | collective-permute-start | bytes 1769480 | tf_op jit(solution)/shard_map/ppermute | solution.py:43
  230.0 10.5 %collective-permute-start.46 = (bf16[576,256]{1,0:T(8,128)(2,1)}, bf16[576,256]{1,0:T(8,128)(2,1)S(1)}, u32[]{:S(2)}, u32[]{:S(2)}) collective-permute-start(bf16[576,256]{1,0:T(8,128)(2,1)} %get-tuple-element.263), channel_id=1, source_target_pairs={{0,4},{1,5},{2,6},{3,7},{4,8},{5,9},{6,10},{7,11},{8,12},{9,13},{1... | collective-permute-start | bytes 884744 | tf_op jit(solution)/shard_map/ppermute | solution.py:43
  230.7 13.3 %collective-permute-start.48 = (bf16[576,256]{1,0:T(8,128)(2,1)}, bf16[576,256]{1,0:T(8,128)(2,1)S(1)}, u32[]{:S(2)}, u32[]{:S(2)}) collective-permute-start(bf16[576,256]{1,0:T(8,128)(2,1)} %get-tuple-element.265), channel_id=1, source_target_pairs={{0,2},{1,3},{2,0},{3,1},{4,6},{5,7},{6,4},{7,5},{8,10},{9,11},{10,... | collective-permute-start | bytes 884744 | tf_op jit(solution)/shard_map/ppermute | solution.py:43
  (43 other events, 373.8 us)

commit v3 on v2

--- a/solution.py
+++ b/solution.py
@@ -25,6 +25,7 @@
 SMEM = pl.BlockSpec(memory_space=pltpu.SMEM)
 VMEM = pl.BlockSpec(memory_space=pltpu.VMEM)
 ANY = pl.BlockSpec(memory_space=pl.ANY)
+HBM = pl.BlockSpec(memory_space=pltpu.HBM)
 
 
 def cost(flops, moved_bytes):
@@ -62,25 +63,31 @@
 together = lax.optimization_barrier
 
 
-def pack_kernel(w_q, w_k, w_v, w_o, out):
+def pack_kernel(*refs):
+    given, out, held, sems = refs[:4], refs[4], refs[5:9], refs[9]
+    copies = [pltpu.make_async_copy(w, h, sems.at[i]) for i, (w, h) in enumerate(zip(given, held))]
+    for copy in copies:
+        copy.start()
     row = 0
-    for ref in (w_q, w_k, w_v, w_o):
+    for copy, ref in zip(copies, held):
+        copy.wait()
         rows, cols = ref.shape
         for p in range(cols // HEAD):
             out[row : row + rows] = ref[:, HEAD * p : HEAD * (p + 1)]
             row += rows
 
 
-def pack(w_q, w_k, w_v, w_o):
+def pack(*weights):
     return pl.pallas_call(
         pack_kernel,
         out_shape=shape((PACKED, HEAD)),
-        in_specs=[VMEM] * 4,
+        in_specs=[HBM] * 4,
         out_specs=VMEM,
-        compiler_params=limit(8),
+        scratch_shapes=[pltpu.VMEM(w.shape, BF16) for w in weights] + [pltpu.SemaphoreType.DMA((4,))],
+        compiler_params=limit(60),
         cost_estimate=cost(0, 4_000_000),
         name="pack",
-    )(w_q, w_k, w_v, w_o)
+    )(*weights)
 
 
 QKV_PART = QKV_PANELS * QKV_ROWS
@@ -106,42 +113,22 @@
     return chip_index(position, dx, dy) * 2 + (core if dc == 0 else 1 - core)
 
 
-def panel_copies(sources, refs, height, rows, target, sem):
-    for panel, row in enumerate(rows):
-        for piece, at, first, last in sources:
-            if first <= row < last:
-                pltpu.make_async_copy(
-                    refs[piece].at[pl.ds(at + row - first, height)], target(panel), sem
-                ).start()
-
-
 def load_qkv(slots, refs, wqkv, sem):
-    for slot, cores in enumerate(slots):
-        for dc, sources in enumerate(cores):
-            to = 2 * QKV_ROWS * slot + QKV_ROWS * dc
-            panel_copies(
-                sources,
-                refs,
-                QKV_ROWS,
-                range(0, QKV_PART, QKV_ROWS),
-                lambda p, to=to: wqkv.at[p, pl.ds(to, QKV_ROWS)],
-                sem,
-            )
-
-
-def load_out(position, chips, slots, refs, wo, sem):
-    for (dx, dy), cores in zip(chips, slots):
-        for dc, sources in enumerate(cores):
+    for slot, sources in enumerate(slots):
+        for dc, (piece, row) in enumerate(sources):
+            panels = refs[piece].at[pl.ds(row, QKV_PART)].reshape(QKV_PANELS, QKV_ROWS, HEAD)
+            to = pl.ds(SLOT_ROWS * slot + QKV_ROWS * dc, QKV_ROWS)
+            pltpu.make_async_copy(panels, wqkv.at[:, to], sem).start()
+
+
+def load_out(position, slots, refs, wo, sem):
+    for (dx, dy), sources in zip(SLOTS, slots):
+        for dc, (piece, row) in enumerate(sources):
+            rows = pl.ds(row + QKV_PART, O_PANELS * O_ROWS)
+            panels = refs[piece].at[rows].reshape(O_PANELS, O_ROWS, HEAD)
             owner = device_index(position, dx, dy, dc)
             to = pl.ds(pl.multiple_of(owner * O_ROWS, 16), O_ROWS)
-            panel_copies(
-                sources,
-                refs,
-                O_ROWS,
-                range(QKV_PART, PACKED, O_ROWS),
-                lambda p, to=to: wo.at[to, pl.ds(HEAD * p, HEAD)],
-                sem,
-            )
+            pltpu.make_async_copy(panels, wo.at[:, to], sem).start()
 
 
 def wait_for(ref, sem):
@@ -211,7 +198,7 @@
 
 def layer(position, early, slots, x_ref, gains_ref, head_ref, normed, acc, pieces, qkv, context, hidden, wqkv, wo, sems):
     load_qkv(slots[early:], pieces, wqkv, sems.at[0])
-    load_out(position, SLOTS, slots, pieces, wo, sems.at[1])
+    load_out(position, slots, pieces, wo, sems.at[1])
     wait_for(wqkv, sems.at[0])
 
     def one_panel(p, carry):
@@ -230,7 +217,7 @@
 
     def one_out(p, carry):
         cols = pl.ds(pl.multiple_of(p * HEAD, HEAD), HEAD)
-        hidden[:, cols] = x_ref[:, cols].astype(F32) + nn(context[...], wo[:, cols])
+        hidden[:, cols] = x_ref[:, cols].astype(F32) + nn(context[...], wo[p])
         return carry
 
     lax.fori_loop(0, O_PANELS, one_out, 0)
@@ -240,12 +227,20 @@
 
 
 def own_kernel(slots, pos_ref, x_ref, gains_ref, head_ref, normed, acc, *refs):
-    pieces, refs = refs[:-10], refs[-10:]
-    c_mine, c_send, qkv, hidden, logits, wo, context, turned, wqkv, sems = refs
+    pieces, refs = refs[:-14], refs[-14:]
+    c_mine, c_send, qkv_out, hidden_out, logits, wo_out, qkv, hidden, context, turned, wqkv, wo, sems, out_sems = refs
     position = pos_ref[0]
     logits[...], _ = layer(
-        position, OWN_EARLY, slots, x_ref, gains_ref, head_ref, normed, acc, pieces, qkv, context, hidden, wqkv, wo, sems
-    )
+        *(position, OWN_EARLY, slots, x_ref, gains_ref, head_ref, normed, acc, pieces),
+        *(qkv, context, hidden, wqkv, wo, sems),
+    )
+    copies = [
+        pltpu.make_async_copy(wo, wo_out, out_sems.at[0]),
+        pltpu.make_async_copy(hidden, hidden_out, out_sems.at[1]),
+        pltpu.make_async_copy(qkv, qkv_out, out_sems.at[2]),
+    ]
+    for copy in copies:
+        copy.start()
     turned[...] = context[...].T
     core = position % 2
     for chip in range(8):
@@ -254,6 +249,8 @@
         c_mine[to] = turned[pl.ds(at, O_ROWS)]
         at = pl.multiple_of((2 * chip + 1 - core) * O_ROWS, 16)
         c_send[to] = turned[pl.ds(at, O_ROWS)]
+    for copy in copies:
+        copy.wait()
 
 
 def peer_kernel(
@@ -281,7 +278,10 @@
     dhidden[...] = (d_final * scale - own * (scale * scale * scale * along)).astype(BF16)
 
 
-def attention_back_kernel(dhidden, wo, qkv, dqkv):
+def attention_back_kernel(dhidden, wo_panels, qkv, dqkv, wo, sem):
+    for p in range(O_PANELS):
+        pltpu.make_async_copy(wo_panels.at[p], wo.at[:, pl.ds(HEAD * p, HEAD)], sem).start()
+    wait_for(wo, sem)
     causal = causal_mask()
     for group in range(HK):
         key, value = qkv[HQ + group], qkv[HQ + HK + group]
@@ -393,17 +393,21 @@
             shape((QKV_PANELS, SEQ, HEAD)),
             shape((SEQ, D), F32),
             shape((SEQ, LABELS), F32),
-            shape((HQ * HEAD, D)),
+            shape((O_PANELS, HQ * HEAD, HEAD)),
         ],
         in_specs=[SMEM] + [VMEM] * 5 + [ANY] * len(arrays),
-        out_specs=[VMEM] * 6,
+        out_specs=[VMEM, VMEM, HBM, HBM, VMEM, HBM],
         scratch_shapes=[
+            pltpu.VMEM((QKV_PANELS, SEQ, HEAD), BF16),
+            pltpu.VMEM((SEQ, D), F32),
             pltpu.VMEM((SEQ, HQ * HEAD), BF16),
             pltpu.VMEM((HQ * HEAD, SEQ), BF16),
             some_wqkv(8 - OWN_EARLY),
+            pltpu.VMEM((O_PANELS, HQ * HEAD, HEAD), BF16),
             pltpu.SemaphoreType.DMA((2,)),
+            pltpu.SemaphoreType.DMA((3,)),
         ],
-        compiler_params=limit(32),
+        compiler_params=limit(60),
         cost_estimate=cost(3_000_000_000, 30_000_000),
         name="own_pass",
     )(position, x, gains, head, normed, acc, *arrays)
@@ -420,10 +424,10 @@
             pltpu.VMEM((SEQ, HQ * HEAD), BF16),
             pltpu.VMEM((SEQ, D), F32),
             some_wqkv(8 - PEER_EARLY),
-            pltpu.VMEM((HQ * HEAD, D), BF16),
+            pltpu.VMEM((O_PANELS, HQ * HEAD, HEAD), BF16),
             pltpu.SemaphoreType.DMA((2,)),
         ],
-        compiler_params=limit(38),
+        compiler_params=limit(26),
         cost_estimate=cost(3_000_000_000, 30_000_000),
         name="peer_pass",
     )(position, x, gains, head, normed, acc, labels, own_logits, own_hidden, *arrays)
@@ -433,8 +437,9 @@
     return pl.pallas_call(
         attention_back_kernel,
         out_shape=shape((QKV_PANELS, SEQ, HEAD)),
-        in_specs=[VMEM] * 3,
+        in_specs=[VMEM, HBM, VMEM],
         out_specs=VMEM,
+        scratch_shapes=[pltpu.VMEM((HQ * HEAD, D), BF16), pltpu.SemaphoreType.DMA],
         compiler_params=limit(20),
         cost_estimate=cost(2_000_000_000, 16_000_000),
         name="attention_back",
@@ -565,7 +570,7 @@
     swap_y0, swap_o3 = moved(y0, to_core), moved(o3, to_core)
 
     def all_of(piece, at=0):
-        return [(piece, at, 0, PACKED)]
+        return (piece, at)
 
     own_slots = [
         (all_of(0), all_of(4, 0)),
@@ -617,6 +622,7 @@
         [peer, p_a3, p_y0, p_swap_first, *late, *swap_late],
         peer_slots,
     )
+    dhidden, c_other = together((dhidden, c_other))
     d_other = moved(dhidden, to_core)
     dqkv = attention_back(dhidden, wo, qkv)
     dqkv_other = moved(dqkv, to_core)

time: 250 us -> 235 us (0.940)
  local copies, waits for them, and re-layouts: 22.2 us -> 15 us
  Pallas kernels: 65.8 us -> 58.9 us
    unnamed x84 -> x86, local copies, waits for them, and re-layouts: 22.1 us -> 14.2 us
    pallas_call x2, Pallas kernels: 14.3 us -> 7.55 us  [early_pass(): pl.pallas_call(functools.partial(early_kernel, slots), out_shape=shape((Q...]
    pallas_call x2, Pallas kernels: 1.04 us -> 4.52 us  [pack(): pl.pallas_call(pack_kernel, out_shape=shape((PACKED, HEAD)), in_specs=[HB...]
    pallas_call x1, Pallas kernels: 14.8 us -> 12 us  [peer_pass(): pl.pallas_call(functools.partial(peer_kernel, slots), out_shape=[shape((S...]
    ppermute x1, waiting for transfers between devices: 3.74 us -> 1.07 us  [body(): lax.ppermute(peer, 'replica', [(i, (i + 1) % replicas) for i in range(rep...]
  transfers between devices with their start and end apart: 49 -> 49, of which waited for: 23 -> 23; matrix products, arithmetic and copies ran while one was open for 2% -> 3% of each run, Pallas kernels for 20% -> 24%
where the time goes in v3:
time: 235 us; the launch traced here: 231 us
  waiting for transfers between devices  97.9 us (42%)
  Pallas kernels  58.9 us (25%)
  starting transfers between devices  52.4 us (22%)
  local copies, waits for them, and re-layouts  15 us (6%)
  other arithmetic  5.83 us (2%)
    ppermute x48, waiting for transfers between devices, moved(): return lax.ppermute(value, 'fsdp', [(i, target(i)) for i in range(N_FSDP)])  96.8 us
    ppermute x48, starting transfers between devices, moved(): return lax.ppermute(value, 'fsdp', [(i, target(i)) for i in range(N_FSDP)])  52.2 us
    pallas_call x1, Pallas kernels, own_pass(): pl.pallas_call(functools.partial(own_kernel, slots), out_shape=[shape((HQ...  15.6 us
    unnamed x86, local copies, waits for them, and re-layouts  14.2 us
    pallas_call x1, Pallas kernels, peer_pass(): pl.pallas_call(functools.partial(peer_kernel, slots), out_shape=[shape((S...  12 us
    pallas_call x2, Pallas kernels, weight_grads(): pl.pallas_call(kernel, out_shape=[shape((block, HEAD))] * 6 + [shape((blo...  8.17 us
    pallas_call x2, Pallas kernels, early_pass(): pl.pallas_call(functools.partial(early_kernel, slots), out_shape=shape((Q...  7.55 us
    pallas_call x1, Pallas kernels, attention_back(): pl.pallas_call(attention_back_kernel, out_shape=shape((QKV_PANELS, SEQ, H...  5.17 us
  transfers between devices with their start and end apart: 49, of which 23 were waited for; matrix products, arithmetic and copies ran while one was open for 3% of the time, Pallas kernels for 24%

profile of v3, /device:TPU:96, one launch (start us, length us, event | category | flops | bytes accessed | tf_op | source)
XLA Modules:
  0.0 231.2 jit_solution(6720290476890008403)
XLA Ops:
  0.7 2.3 %pack.2.refs_0_ = bf16[1728,256]{1,0:T(8,128)(2,1)} custom-call(bf16[144,1024]{1,0:T(8,128)(2,1)} %bitcast.22, bf16[144,512]{1,0:T(8,128)(2,1)} %bitcast.26, bf16[144,512]{1,0:T(8,128)(2,1)} %bitcast.27, bf16[64,2304]{1,0:T(8,128)(2,1)} %bitcast.23), custom_call_target="tpu_custom_call" | custom-call | bytes 4000000 | tf_op jit(solution)/shard_map/pack/pallas_call | solution.py:81
  3.0 2.8 %collective-permute-start = (bf16[1728,256]{1,0:T(8,128)(2,1)}, bf16[1728,256]{1,0:T(8,128)(2,1)S(1)}, u32[]{:S(2)}, u32[]{:S(2)}) collective-permute-start(bf16[1728,256]{1,0:T(8,128)(2,1)} %pack.2.refs_0_), channel_id=1, source_target_pairs={{0,12},{1,13},{2,14},{3,15},{4,0},{5,1},{6,2},{7,3},{8,4},{9,5},{1... | collective-permute-start | bytes 2654216 | tf_op jit(solution)/shard_map/ppermute | solution.py:44
  5.8 2.2 pack.3
  8.3 1.4 prepare.1
  13.0 12.0 %collective-permute-done.refs_3_ = bf16[1728,256]{1,0:T(8,128)(2,1)S(1)} collective-permute-done((bf16[1728,256]{1,0:T(8,128)(2,1)}, bf16[1728,256]{1,0:T(8,128)(2,1)S(1)}, u32[]{:S(2)}, u32[]{:S(2)}) %collective-permute-start) | collective-permute-done | bytes 884768 | tf_op jit(solution)/shard_map/ppermute | solution.py:44
  25.0 3.4 %collective-permute-done.1.refs_1_ = bf16[1728,256]{1,0:T(8,128)(2,1)} collective-permute-done((bf16[1728,256]{1,0:T(8,128)(2,1)}, bf16[1728,256]{1,0:T(8,128)(2,1)}, u32[]{:S(2)}, u32[]{:S(2)}) %collective-permute-start.1) | collective-permute-done | bytes 884768 | tf_op jit(solution)/shard_map/ppermute | solution.py:44
  30.0 3.2 %collective-permute-start.3 = (bf16[1728,256]{1,0:T(8,128)(2,1)S(1)}, bf16[1728,256]{1,0:T(8,128)(2,1)S(1)}, u32[]{:S(2)}, u32[]{:S(2)}) collective-permute-start(bf16[1728,256]{1,0:T(8,128)(2,1)S(1)} %copy-done), channel_id=1, source_target_pairs={{0,2},{1,3},{2,0},{3,1},{4,6},{5,7},{6,4},{7,5},{8,10},{9,11},{10,... | collective-permute-start | bytes 2654216 | tf_op jit(solution)/shard_map/ppermute | solution.py:44
  33.2 2.8 %collective-permute-start.4 = (bf16[1728,256]{1,0:T(8,128)(2,1)S(1)}, bf16[1728,256]{1,0:T(8,128)(2,1)S(1)}, u32[]{:S(2)}, u32[]{:S(2)}) collective-permute-start(bf16[1728,256]{1,0:T(8,128)(2,1)S(1)} %collective-permute-done.refs_3_), channel_id=1, source_target_pairs={{0,12},{1,13},{2,14},{3,15},{4,0},{5,1},{6,2},{7,3},{8,4},{9,5},{1... | collective-permute-start | bytes 2654216 | tf_op jit(solution)/shard_map/ppermute | solution.py:44
  36.0 1.3 pad_maximum_fusion
  38.8 12.3 %collective-permute-done.5.refs_1_ = bf16[1728,256]{1,0:T(8,128)(2,1)S(1)} collective-permute-done((bf16[1728,256]{1,0:T(8,128)(2,1)}, bf16[1728,256]{1,0:T(8,128)(2,1)S(1)}, u32[]{:S(2)}, u32[]{:S(2)}) %collective-permute-start.5) | collective-permute-done | bytes 884768 | tf_op jit(solution)/shard_map/ppermute | solution.py:44
  51.2 1.9 collective-permute-done.4.refs_6_
  53.1 1.5 collective-permute-start.7
  54.8 1.4 collective-permute-start.8
  56.2 1.8 collective-permute-start.9
  58.0 18.9 %collective-permute-done.7.refs_2_ = bf16[1728,256]{1,0:T(8,128)(2,1)S(1)} collective-permute-done((bf16[1728,256]{1,0:T(8,128)(2,1)}, bf16[1728,256]{1,0:T(8,128)(2,1)S(1)}, u32[]{:S(2)}, u32[]{:S(2)}) %collective-permute-start.7) | collective-permute-done | bytes 884768 | tf_op jit(solution)/shard_map/ppermute | solution.py:44
  76.9 3.8 %collective-permute-start.13 = (bf16[1728,256]{1,0:T(8,128)(2,1)}, bf16[1728,256]{1,0:T(8,128)(2,1)}, u32[]{:S(2)}, u32[]{:S(2)}) collective-permute-start(bf16[1728,256]{1,0:T(8,128)(2,1)} %collective-permute-done.2.refs_0_), channel_id=1, source_target_pairs={{0,12},{1,13},{2,14},{3,15},{4,0},{5,1},{6,2},{7,3},{8,4},{9,5},{1... | collective-permute-start | bytes 2654216 | tf_op jit(solution)/shard_map/ppermute | solution.py:44
  81.6 1.8 copy-done.6
  83.4 3.9 %early_pass.2.acc = f32[8,256,256]{2,1,0:T(8,128)S(1)} custom-call(bf16[256,1152]{1,0:T(8,128)(2,1)S(1)} %get-tuple-element.158.normed, bf16[1728,256]{1,0:T(8,128)(2,1)S(1)} %copy-done, bf16[1728,256]{1,0:T(8,128)(2,1)} %collective-permute-done.1.refs_1_, bf16[1728,256]{1,0:T(8,128)(2,1)S(1)} %collective-permute-done.3.refs_2_, ...), custom_call_target="tpu_custom_call" | custom-call | flops 1200000000 | bytes 20000000 | tf_op jit(solution)/shard_map/early_pass/pallas_call | solution.py:375
  87.4 1.3 copy-done.4
  89.6 2.9 %pad_maximum_fusion.1 = bf16[5184,256]{1,0:T(8,128)(2,1)} fusion(bf16[1728,256]{1,0:T(8,128)(2,1)S(1)} %collective-permute-done.7.refs_2_, bf16[1728,256]{1,0:T(8,128)(2,1)S(1)} %collective-permute-done.5.refs_1_, bf16[1728,256]{1,0:T(8,128)(2,1)} %collective-permute-done.2.refs_0_), kind=kLoop, calls=%fused_computation.1 | loop fusion | flops 7962624 | bytes 5308416 | tf_op jit(solution)/shard_map/concatenate | solution.py:586
  92.5 8.0 %collective-permute-done.13.refs_4_ = bf16[1728,256]{1,0:T(8,128)(2,1)} collective-permute-done((bf16[1728,256]{1,0:T(8,128)(2,1)}, bf16[1728,256]{1,0:T(8,128)(2,1)}, u32[]{:S(2)}, u32[]{:S(2)}) %collective-permute-start.13) | collective-permute-done | bytes 884768 | tf_op jit(solution)/shard_map/ppermute | solution.py:44
  100.5 3.4 %collective-permute-done.12.refs_9_ = bf16[1728,256]{1,0:T(8,128)(2,1)S(1)} collective-permute-done((bf16[1728,256]{1,0:T(8,128)(2,1)S(1)}, bf16[1728,256]{1,0:T(8,128)(2,1)S(1)}, u32[]{:S(2)}, u32[]{:S(2)}) %collective-permute-start.12) | collective-permute-done | bytes 884768 | tf_op jit(solution)/shard_map/ppermute | solution.py:44
  104.8 2.9 %collective-permute-start.17 = (bf16[1728,256]{1,0:T(8,128)(2,1)}, bf16[1728,256]{1,0:T(8,128)(2,1)}, u32[]{:S(2)}, u32[]{:S(2)}) collective-permute-start(bf16[1728,256]{1,0:T(8,128)(2,1)} %collective-permute-done.13.refs_4_), channel_id=1, source_target_pairs={{0,2},{1,3},{2,0},{3,1},{4,6},{5,7},{6,4},{7,5},{8,10},{9,11},{10,... | collective-permute-start | bytes 2654216 | tf_op jit(solution)/shard_map/ppermute | solution.py:44
  107.7 2.4 %collective-permute-done.21.refs_12_ = bf16[1728,256]{1,0:T(8,128)(2,1)S(1)} collective-permute-done((bf16[1728,256]{1,0:T(8,128)(2,1)S(1)}, bf16[1728,256]{1,0:T(8,128)(2,1)S(1)}, u32[]{:S(2)}, u32[]{:S(2)}) %collective-permute-start.21) | collective-permute-done | bytes 884768 | tf_op jit(solution)/shard_map/ppermute | solution.py:44
  112.6 15.6 %own_pass.1 = (bf16[512,256]{1,0:T(8,128)(2,1)}, bf16[512,256]{1,0:T(8,128)(2,1)}, bf16[8,256,256]{2,1,0:T(8,128)(2,1)}, f32[256,2304]{1,0:T(8,128)}, f32[256,256]{1,0:T(8,128)}, /*index=5*/bf16[9,1024,256]{2,1,0:T(8,128)(2,1)}) custom-call(s32[1]{0:T(128)} %bitcast.pos_ref, bf16[256,2304]{1,0:T(8,128)(2,1)} %bitcast.16, f32[2,2304]{1,0:T(2,128)} %gains_ref.5, ...), custom_call_target="tpu_custom_call" | custom-call | flops 3000000000 | bytes 30000000 | tf_op jit(solution)/shard_map/own_pass/pallas_call | solution.py:388
  129.7 3.8 %collective-permute-done.19.refs_8_ = bf16[1728,256]{1,0:T(8,128)(2,1)} collective-permute-done((bf16[1728,256]{1,0:T(8,128)(2,1)}, bf16[1728,256]{1,0:T(8,128)(2,1)}, u32[]{:S(2)}, u32[]{:S(2)}) %collective-permute-start.19) | collective-permute-done | bytes 884768 | tf_op jit(solution)/shard_map/ppermute | solution.py:44
  137.1 3.7 %early_pass.3.acc = f32[8,256,256]{2,1,0:T(8,128)S(1)} custom-call(bf16[256,864]{1,0:T(8,128)(2,1)S(1)} %copy-done.22, bf16[1728,256]{1,0:T(8,128)(2,1)} %collective-permute-done.2.refs_0_, bf16[1728,256]{1,0:T(8,128)(2,1)S(1)} %copy-done.8, bf16[1728,256]{1,0:T(8,128)(2,1)S(1)} %copy-done.10, bf16[5184,256]{1,0:T(8,128)(2,1)S(1)} %collective-permute-done.20.refs_3_), custom_call_target="tpu_custom_call" | custom-call | flops 1200000000 | bytes 20000000 | tf_op jit(solution)/shard_map/early_pass/pallas_call | solution.py:375
  141.4 1.7 copy-done.15
  144.2 12.0 %peer_pass.1 = (f32[256,1]{1,0:T(8,128)S(1)}, bf16[256,2304]{1,0:T(8,128)(2,1)S(1)}) custom-call(s32[1]{0:T(128)} %bitcast.pos_ref, bf16[256,2304]{1,0:T(8,128)(2,1)S(1)} %bitcast.18, f32[2,2304]{1,0:T(2,128)S(1)} %copy-done.25, bf16[2304,256]{1,0:T(8,128)(2,1)S(1)} %copy-done.12, bf16[256,1440]{1,0:T(8,128)(2,1)S(1)} %copy-done.18, ...), custom_call_target="tpu_custom_call" | custom-call | flops 3000000000 | bytes 30000000 | tf_op jit(solution)/shard_map/peer_pass/pallas_call | solution.py:417
  156.4 5.2 %attention_back.1.d_mine = bf16[8,256,256]{2,1,0:T(8,128)(2,1)S(1)} custom-call(bf16[256,2304]{1,0:T(8,128)(2,1)S(1)} %get-tuple-element.180.dhidden.d_mine, bf16[9,1024,256]{2,1,0:T(8,128)(2,1)S(1)} %bitcast.20, bf16[8,256,256]{2,1,0:T(8,128)(2,1)S(1)} %copy-done.16), custom_call_target="tpu_custom_call" | custom-call | flops 2000000000 | bytes 16000000 | tf_op jit(solution)/shard_map/attention_back/pallas_call | solution.py:437
  162.4 3.0 %out_grads.1 = (bf16[576,256]{1,0:T(8,128)(2,1)S(1)}, bf16[576,256]{1,0:T(8,128)(2,1)S(1)}, bf16[576,256]{1,0:T(8,128)(2,1)S(1)}, bf16[576,256]{1,0:T(8,128)(2,1...) custom-call(s32[1]{0:T(128)} %bitcast.pos_ref, ...), custom_call_target="tpu_custom_call" | custom-call | flops 1207959552 | bytes 10000000 | tf_op jit(solution)/shard_map/out_grads/pallas_call | solution.py:451
  165.4 2.9 %collective-permute-start.31 = (bf16[192,256]{1,0:T(8,128)(2,1)S(1)}, bf16[192,256]{1,0:T(8,128)(2,1)S(1)}, u32[]{:S(2)}, u32[]{:S(2)}) collective-permute-start(bf16[192,256]{1,0:T(8,128)(2,1)S(1)} %get-tuple-element.198), channel_id=1, source_target_pairs={{0,2},{1,3},{2,0},{3,1},{4,6},{5,7},{6,4},{7,5},{8,10},{9,11},{10,... | collective-permute-start | bytes 294920 | tf_op jit(solution)/shard_map/ppermute | solution.py:44
  168.4 2.0 collective-permute-start.33
  170.4 5.1 %qkv_grads.1 = (bf16[1152,256]{1,0:T(8,128)(2,1)S(1)}, bf16[1152,256]{1,0:T(8,128)(2,1)S(1)}, bf16[1152,256]{1,0:T(8,128)(2,1)S(1)}, bf16[1152,256]{1,0:T(8,128)...) custom-call(s32[1]{0:T(128)} %bitcast.pos_ref, ...), custom_call_target="tpu_custom_call" | custom-call | flops 2415919104 | bytes 10000000 | tf_op jit(solution)/shard_map/qkv_grads/pallas_call | solution.py:451
  178.4 4.8 %collective-permute-done.34.in_a = bf16[384,256]{1,0:T(8,128)(2,1)S(1)} collective-permute-done((bf16[384,256]{1,0:T(8,128)(2,1)S(1)}, bf16[384,256]{1,0:T(8,128)(2,1)S(1)}, u32[]{:S(2)}, u32[]{:S(2)}) %collective-permute-start.34) | collective-permute-done | bytes 196640 | tf_op jit(solution)/shard_map/ppermute | solution.py:44
  183.2 1.3 collective-permute-done.36.in_c
  184.8 3.2 %collective-permute-start.38 = (bf16[1152,256]{1,0:T(8,128)(2,1)S(1)}, bf16[1152,256]{1,0:T(8,128)(2,1)S(1)}, u32[]{:S(2)}, u32[]{:S(2)}) collective-permute-start(bf16[1152,256]{1,0:T(8,128)(2,1)S(1)} %get-tuple-element.244), channel_id=1, source_target_pairs={{0,12},{1,13},{2,14},{3,15},{4,0},{5,1},{6,2},{7,3},{8,4},{9,5},{1... | collective-permute-start | bytes 1769480 | tf_op jit(solution)/shard_map/ppermute | solution.py:44
  188.0 2.9 %collective-permute-start.39 = (bf16[1152,256]{1,0:T(8,128)(2,1)S(1)}, bf16[1152,256]{1,0:T(8,128)(2,1)S(1)}, u32[]{:S(2)}, u32[]{:S(2)}) collective-permute-start(bf16[1152,256]{1,0:T(8,128)(2,1)S(1)} %get-tuple-element.245), channel_id=1, source_target_pairs={{0,2},{1,3},{2,0},{3,1},{4,6},{5,7},{6,4},{7,5},{8,10},{9,11},{10,... | collective-permute-start | bytes 1769480 | tf_op jit(solution)/shard_map/ppermute | solution.py:44
  190.9 3.2 %collective-permute-start.44 = (bf16[576,256]{1,0:T(8,128)(2,1)S(1)}, bf16[576,256]{1,0:T(8,128)(2,1)S(1)}, u32[]{:S(2)}, u32[]{:S(2)}) collective-permute-start(bf16[576,256]{1,0:T(8,128)(2,1)S(1)} %get-tuple-element.262), channel_id=1, source_target_pairs={{0,12},{1,13},{2,14},{3,15},{4,0},{5,1},{6,2},{7,3},{8,4},{9,5},{1... | collective-permute-start | bytes 884744 | tf_op jit(solution)/shard_map/ppermute | solution.py:44
  194.1 8.1 %collective-permute-done.37.in_x = bf16[1152,256]{1,0:T(8,128)(2,1)S(1)} collective-permute-done((bf16[1152,256]{1,0:T(8,128)(2,1)S(1)}, bf16[1152,256]{1,0:T(8,128)(2,1)S(1)}, u32[]{:S(2)}, u32[]{:S(2)}) %collective-permute-start.37) | collective-permute-done | bytes 589856 | tf_op jit(solution)/shard_map/ppermute | solution.py:44
  202.2 2.7 %collective-permute-start.45 = (bf16[576,256]{1,0:T(8,128)(2,1)S(1)}, bf16[576,256]{1,0:T(8,128)(2,1)S(1)}, u32[]{:S(2)}, u32[]{:S(2)}) collective-permute-start(bf16[576,256]{1,0:T(8,128)(2,1)S(1)} %get-tuple-element.263), channel_id=1, source_target_pairs={{0,2},{1,3},{2,0},{3,1},{4,6},{5,7},{6,4},{7,5},{8,10},{9,11},{10,... | collective-permute-start | bytes 884744 | tf_op jit(solution)/shard_map/ppermute | solution.py:44
  206.7 2.0 collective-permute-start.40
  208.7 2.9 %collective-permute-start.42 = (bf16[1152,256]{1,0:T(8,128)(2,1)}, bf16[1152,256]{1,0:T(8,128)(2,1)S(1)}, u32[]{:S(2)}, u32[]{:S(2)}) collective-permute-start(bf16[1152,256]{1,0:T(8,128)(2,1)} %get-tuple-element.251), channel_id=1, source_target_pairs={{0,2},{1,3},{2,0},{3,1},{4,6},{5,7},{6,4},{7,5},{8,10},{9,11},{10,... | collective-permute-start | bytes 1769480 | tf_op jit(solution)/shard_map/ppermute | solution.py:44
  211.6 2.0 collective-permute-done.45.in_y
  214.9 2.4 %collective-permute-start.48 = (bf16[576,256]{1,0:T(8,128)(2,1)}, bf16[576,256]{1,0:T(8,128)(2,1)S(1)}, u32[]{:S(2)}, u32[]{:S(2)}) collective-permute-start(bf16[576,256]{1,0:T(8,128)(2,1)} %get-tuple-element.269), channel_id=1, source_target_pairs={{0,2},{1,3},{2,0},{3,1},{4,6},{5,7},{6,4},{7,5},{8,10},{9,11},{10,... | collective-permute-start | bytes 884744 | tf_op jit(solution)/shard_map/ppermute | solution.py:44
  217.3 1.6 reduce
  218.9 6.7 %collective-permute-done.46.refs_1_ = bf16[576,256]{1,0:T(8,128)(2,1)S(1)} collective-permute-done((bf16[576,256]{1,0:T(8,128)(2,1)}, bf16[576,256]{1,0:T(8,128)(2,1)S(1)}, u32[]{:S(2)}, u32[]{:S(2)}) %collective-permute-start.46) | collective-permute-done | bytes 294944 | tf_op jit(solution)/shard_map/ppermute | solution.py:44
  225.6 3.5 %collective-permute-done.48.refs_3_ = bf16[576,256]{1,0:T(8,128)(2,1)S(1)} collective-permute-done((bf16[576,256]{1,0:T(8,128)(2,1)}, bf16[576,256]{1,0:T(8,128)(2,1)S(1)}, u32[]{:S(2)}, u32[]{:S(2)}) %collective-permute-start.48) | collective-permute-done | bytes 294944 | tf_op jit(solution)/shard_map/ppermute | solution.py:44
  (157 shorter events, 28.2 us)
Async XLA Ops:
  3.0 22.1 %collective-permute-start = (bf16[1728,256]{1,0:T(8,128)(2,1)}, bf16[1728,256]{1,0:T(8,128)(2,1)S(1)}, u32[]{:S(2)}, u32[]{:S(2)}) collective-permute-start(bf16[1728,256]{1,0:T(8,128)(2,1)} %pack.2.refs_0_), channel_id=1, source_target_pairs={{0,12},{1,13},{2,14},{3,15},{4,0},{5,1},{6,2},{7,3},{8,4},{9,5},{1... | collective-permute-start | bytes 2654216 | tf_op jit(solution)/shard_map/ppermute | solution.py:44
  5.8 22.6 %collective-permute-start.1 = (bf16[1728,256]{1,0:T(8,128)(2,1)}, bf16[1728,256]{1,0:T(8,128)(2,1)}, u32[]{:S(2)}, u32[]{:S(2)}) collective-permute-start(bf16[1728,256]{1,0:T(8,128)(2,1)} %pack.2.refs_0_), channel_id=1, source_target_pairs={{0,4},{1,5},{2,6},{3,7},{4,8},{5,9},{6,10},{7,11},{8,12},{9,13},{1... | collective-permute-start | bytes 2654216 | tf_op jit(solution)/shard_map/ppermute | solution.py:44
  8.0 21.5 %collective-permute-start.2 = (bf16[1728,256]{1,0:T(8,128)(2,1)}, bf16[1728,256]{1,0:T(8,128)(2,1)}, u32[]{:S(2)}, u32[]{:S(2)}) collective-permute-start(bf16[1728,256]{1,0:T(8,128)(2,1)} %pack.3), channel_id=1, source_target_pairs={{0,16},{16,32},{32,48},{48,64},{64,80},{80,96},{96,112},{112,0},{1... | collective-permute-start | bytes 2654216 | tf_op jit(solution)/shard_map/ppermute | solution.py:555
  29.5 21.6 %collective-permute-start.5 = (bf16[1728,256]{1,0:T(8,128)(2,1)}, bf16[1728,256]{1,0:T(8,128)(2,1)S(1)}, u32[]{:S(2)}, u32[]{:S(2)}) collective-permute-start(bf16[1728,256]{1,0:T(8,128)(2,1)} %collective-permute-done.2.refs_0_), channel_id=1, source_target_pairs={{0,4},{1,5},{2,6},{3,7},{4,8},{5,9},{6,10},{7,11},{8,12},{9,13},{1... | collective-permute-start | bytes 2654216 | tf_op jit(solution)/shard_map/ppermute | solution.py:44
  30.0 21.2 %collective-permute-start.3 = (bf16[1728,256]{1,0:T(8,128)(2,1)S(1)}, bf16[1728,256]{1,0:T(8,128)(2,1)S(1)}, u32[]{:S(2)}, u32[]{:S(2)}) collective-permute-start(bf16[1728,256]{1,0:T(8,128)(2,1)S(1)} %copy-done), channel_id=1, source_target_pairs={{0,2},{1,3},{2,0},{3,1},{4,6},{5,7},{6,4},{7,5},{8,10},{9,11},{10,... | collective-permute-start | bytes 2654216 | tf_op jit(solution)/shard_map/ppermute | solution.py:44
  33.2 19.9 %collective-permute-start.4 = (bf16[1728,256]{1,0:T(8,128)(2,1)S(1)}, bf16[1728,256]{1,0:T(8,128)(2,1)S(1)}, u32[]{:S(2)}, u32[]{:S(2)}) collective-permute-start(bf16[1728,256]{1,0:T(8,128)(2,1)S(1)} %collective-permute-done.refs_3_), channel_id=1, source_target_pairs={{0,12},{1,13},{2,14},{3,15},{4,0},{5,1},{6,2},{7,3},{8,4},{9,5},{1... | collective-permute-start | bytes 2654216 | tf_op jit(solution)/shard_map/ppermute | solution.py:44
  53.1 28.2 %collective-permute-start.10 = (bf16[5184,256]{1,0:T(8,128)(2,1)S(1)}, bf16[5184,256]{1,0:T(8,128)(2,1)S(1)}, u32[]{:S(2)}, u32[]{:S(2)}) collective-permute-start(bf16[5184,256]{1,0:T(8,128)(2,1)S(1)} %pad_maximum_fusion), channel_id=1, source_target_pairs={{0,1},{1,0},{2,3},{3,2},{4,5},{5,4},{6,7},{7,6},{8,9},{9,8},{10,11... | collective-permute-start | bytes 7962632 | tf_op jit(solution)/shard_map/ppermute | solution.py:44
  53.1 23.8 %collective-permute-start.7 = (bf16[1728,256]{1,0:T(8,128)(2,1)}, bf16[1728,256]{1,0:T(8,128)(2,1)S(1)}, u32[]{:S(2)}, u32[]{:S(2)}) collective-permute-start(bf16[1728,256]{1,0:T(8,128)(2,1)} %collective-permute-done.2.refs_0_), channel_id=1, source_target_pairs={{0,2},{1,3},{2,0},{3,1},{4,6},{5,7},{6,4},{7,5},{8,10},{9,11},{10,... | collective-permute-start | bytes 2654216 | tf_op jit(solution)/shard_map/ppermute | solution.py:44
  54.6 22.3 %collective-permute-start.11 = (bf16[1728,256]{1,0:T(8,128)(2,1)S(1)}, bf16[1728,256]{1,0:T(8,128)(2,1)S(1)}, u32[]{:S(2)}, u32[]{:S(2)}) collective-permute-start(bf16[1728,256]{1,0:T(8,128)(2,1)S(1)} %collective-permute-done.4.refs_6_), channel_id=1, source_target_pairs={{0,1},{1,0},{2,3},{3,2},{4,5},{5,4},{6,7},{7,6},{8,9},{9,8},{10,11... | collective-permute-start | bytes 2654216 | tf_op jit(solution)/shard_map/ppermute | solution.py:44
  54.8 25.9 %collective-permute-start.8 = (bf16[1728,256]{1,0:T(8,128)(2,1)S(1)}, bf16[1728,256]{1,0:T(8,128)(2,1)S(1)}, u32[]{:S(2)}, u32[]{:S(2)}) collective-permute-start(bf16[1728,256]{1,0:T(8,128)(2,1)S(1)} %collective-permute-done.3.refs_2_), channel_id=1, source_target_pairs={{0,4},{1,5},{2,6},{3,7},{4,8},{5,9},{6,10},{7,11},{8,12},{9,13},{1... | collective-permute-start | bytes 2654216 | tf_op jit(solution)/shard_map/ppermute | solution.py:44
  56.2 25.2 %collective-permute-start.9 = (bf16[1728,256]{1,0:T(8,128)(2,1)S(1)}, bf16[1728,256]{1,0:T(8,128)(2,1)S(1)}, u32[]{:S(2)}, u32[]{:S(2)}) collective-permute-start(bf16[1728,256]{1,0:T(8,128)(2,1)S(1)} %collective-permute-done.3.refs_2_), channel_id=1, source_target_pairs={{0,12},{1,13},{2,14},{3,15},{4,0},{5,1},{6,2},{7,3},{8,4},{9,5},{1... | collective-permute-start | bytes 2654216 | tf_op jit(solution)/shard_map/ppermute | solution.py:44
  76.9 4.7 %collective-permute-start.16 = (bf16[1728,256]{1,0:T(8,128)(2,1)S(1)}, bf16[1728,256]{1,0:T(8,128)(2,1)S(1)}, u32[]{:S(2)}, u32[]{:S(2)}) collective-permute-start(bf16[1728,256]{1,0:T(8,128)(2,1)S(1)} %collective-permute-done.3.refs_2_), channel_id=1, source_target_pairs={{0,1},{1,0},{2,3},{3,2},{4,5},{5,4},{6,7},{7,6},{8,9},{9,8},{10,11... | collective-permute-start | bytes 2654216 | tf_op jit(solution)/shard_map/ppermute | solution.py:44
  76.9 23.6 %collective-permute-start.13 = (bf16[1728,256]{1,0:T(8,128)(2,1)}, bf16[1728,256]{1,0:T(8,128)(2,1)}, u32[]{:S(2)}, u32[]{:S(2)}) collective-permute-start(bf16[1728,256]{1,0:T(8,128)(2,1)} %collective-permute-done.2.refs_0_), channel_id=1, source_target_pairs={{0,12},{1,13},{2,14},{3,15},{4,0},{5,1},{6,2},{7,3},{8,4},{9,5},{1... | collective-permute-start | bytes 2654216 | tf_op jit(solution)/shard_map/ppermute | solution.py:44
  80.7 23.2 %collective-permute-start.12 = (bf16[1728,256]{1,0:T(8,128)(2,1)S(1)}, bf16[1728,256]{1,0:T(8,128)(2,1)S(1)}, u32[]{:S(2)}, u32[]{:S(2)}) collective-permute-start(bf16[1728,256]{1,0:T(8,128)(2,1)S(1)} %collective-permute-done.4.refs_6_), channel_id=1, source_target_pairs={{0,2},{1,3},{2,0},{3,1},{4,6},{5,7},{6,4},{7,5},{8,10},{9,11},{10,... | collective-permute-start | bytes 2654216 | tf_op jit(solution)/shard_map/ppermute | solution.py:44
  81.4 22.8 %collective-permute-start.14 = (bf16[1728,256]{1,0:T(8,128)(2,1)S(1)}, bf16[1728,256]{1,0:T(8,128)(2,1)}, u32[]{:S(2)}, u32[]{:S(2)}) collective-permute-start(bf16[1728,256]{1,0:T(8,128)(2,1)S(1)} %collective-permute-done.7.refs_2_), channel_id=1, source_target_pairs={{0,4},{1,5},{2,6},{3,7},{4,8},{5,9},{6,10},{7,11},{8,12},{9,13},{1... | collective-permute-start | bytes 2654216 | tf_op jit(solution)/shard_map/ppermute | solution.py:44
  81.5 22.7 %collective-permute-start.15 = (bf16[1728,256]{1,0:T(8,128)(2,1)S(1)}, bf16[1728,256]{1,0:T(8,128)(2,1)S(1)}, u32[]{:S(2)}, u32[]{:S(2)}) collective-permute-start(bf16[1728,256]{1,0:T(8,128)(2,1)S(1)} %collective-permute-done.8.refs_7_), channel_id=1, source_target_pairs={{0,1},{1,0},{2,3},{3,2},{4,5},{5,4},{6,7},{7,6},{8,9},{9,8},{10,11... | collective-permute-start | bytes 2654216 | tf_op jit(solution)/shard_map/ppermute | solution.py:44
  104.2 29.3 %collective-permute-start.20 = (bf16[5184,256]{1,0:T(8,128)(2,1)}, bf16[5184,256]{1,0:T(8,128)(2,1)S(1)}, u32[]{:S(2)}, u32[]{:S(2)}) collective-permute-start(bf16[5184,256]{1,0:T(8,128)(2,1)} %pad_maximum_fusion.1), channel_id=1, source_target_pairs={{0,1},{1,0},{2,3},{3,2},{4,5},{5,4},{6,7},{7,6},{8,9},{9,8},{10,11... | collective-permute-start | bytes 7962632 | tf_op jit(solution)/shard_map/ppermute | solution.py:44
  104.2 5.8 %collective-permute-start.21 = (bf16[1728,256]{1,0:T(8,128)(2,1)S(1)}, bf16[1728,256]{1,0:T(8,128)(2,1)S(1)}, u32[]{:S(2)}, u32[]{:S(2)}) collective-permute-start(bf16[1728,256]{1,0:T(8,128)(2,1)S(1)} %collective-permute-done.9.refs_8_), channel_id=1, source_target_pairs={{0,1},{1,0},{2,3},{3,2},{4,5},{5,4},{6,7},{7,6},{8,9},{9,8},{10,11... | collective-permute-start | bytes 2654216 | tf_op jit(solution)/shard_map/ppermute | solution.py:44
  104.7 6.7 %collective-permute-start.22 = (bf16[1728,256]{1,0:T(8,128)(2,1)S(1)}, bf16[1728,256]{1,0:T(8,128)(2,1)S(1)}, u32[]{:S(2)}, u32[]{:S(2)}) collective-permute-start(bf16[1728,256]{1,0:T(8,128)(2,1)S(1)} %collective-permute-done.12.refs_9_), channel_id=1, source_target_pairs={{0,1},{1,0},{2,3},{3,2},{4,5},{5,4},{6,7},{7,6},{8,9},{9,8},{10,11... | collective-permute-start | bytes 2654216 | tf_op jit(solution)/shard_map/ppermute | solution.py:44
  104.8 23.8 %collective-permute-start.17 = (bf16[1728,256]{1,0:T(8,128)(2,1)}, bf16[1728,256]{1,0:T(8,128)(2,1)}, u32[]{:S(2)}, u32[]{:S(2)}) collective-permute-start(bf16[1728,256]{1,0:T(8,128)(2,1)} %collective-permute-done.13.refs_4_), channel_id=1, source_target_pairs={{0,2},{1,3},{2,0},{3,1},{4,6},{5,7},{6,4},{7,5},{8,10},{9,11},{10,... | collective-permute-start | bytes 2654216 | tf_op jit(solution)/shard_map/ppermute | solution.py:44
  107.7 22.0 %collective-permute-start.18 = (bf16[1728,256]{1,0:T(8,128)(2,1)}, bf16[1728,256]{1,0:T(8,128)(2,1)}, u32[]{:S(2)}, u32[]{:S(2)}) collective-permute-start(bf16[1728,256]{1,0:T(8,128)(2,1)} %collective-permute-done.13.refs_4_), channel_id=1, source_target_pairs={{0,12},{1,13},{2,14},{3,15},{4,0},{5,1},{6,2},{7,3},{8,4},{9,5},{1... | collective-permute-start | bytes 2654216 | tf_op jit(solution)/shard_map/ppermute | solution.py:44
  110.1 23.5 %collective-permute-start.19 = (bf16[1728,256]{1,0:T(8,128)(2,1)}, bf16[1728,256]{1,0:T(8,128)(2,1)}, u32[]{:S(2)}, u32[]{:S(2)}) collective-permute-start(bf16[1728,256]{1,0:T(8,128)(2,1)} %collective-permute-done.14.refs_6_), channel_id=1, source_target_pairs={{0,4},{1,5},{2,6},{3,7},{4,8},{5,9},{6,10},{7,11},{8,12},{9,13},{1... | collective-permute-start | bytes 2654216 | tf_op jit(solution)/shard_map/ppermute | solution.py:44
  112.3 28.5 %collective-permute-start.23 = (bf16[1728,256]{1,0:T(8,128)(2,1)}, bf16[1728,256]{1,0:T(8,128)(2,1)}, u32[]{:S(2)}, u32[]{:S(2)}) collective-permute-start(bf16[1728,256]{1,0:T(8,128)(2,1)} %collective-permute-done.13.refs_4_), channel_id=1, source_target_pairs={{0,1},{1,0},{2,3},{3,2},{4,5},{5,4},{6,7},{7,6},{8,9},{9,8},{10,11... | collective-permute-start | bytes 2654216 | tf_op jit(solution)/shard_map/ppermute | solution.py:44
  128.6 12.7 %collective-permute-start.25 = (bf16[1728,256]{1,0:T(8,128)(2,1)}, bf16[1728,256]{1,0:T(8,128)(2,1)}, u32[]{:S(2)}, u32[]{:S(2)}) collective-permute-start(bf16[1728,256]{1,0:T(8,128)(2,1)} %collective-permute-done.14.refs_6_), channel_id=1, source_target_pairs={{0,1},{1,0},{2,3},{3,2},{4,5},{5,4},{6,7},{7,6},{8,9},{9,8},{10,11... | collective-permute-start | bytes 2654216 | tf_op jit(solution)/shard_map/ppermute | solution.py:44
  133.5 7.8 %collective-permute-start.24 = (bf16[1728,256]{1,0:T(8,128)(2,1)}, bf16[1728,256]{1,0:T(8,128)(2,1)}, u32[]{:S(2)}, u32[]{:S(2)}) collective-permute-start(bf16[1728,256]{1,0:T(8,128)(2,1)} %collective-permute-done.18.refs_5_), channel_id=1, source_target_pairs={{0,1},{1,0},{2,3},{3,2},{4,5},{5,4},{6,7},{7,6},{8,9},{9,8},{10,11... | collective-permute-start | bytes 2654216 | tf_op jit(solution)/shard_map/ppermute | solution.py:44
  133.5 7.8 %collective-permute-start.26 = (bf16[1728,256]{1,0:T(8,128)(2,1)}, bf16[1728,256]{1,0:T(8,128)(2,1)}, u32[]{:S(2)}, u32[]{:S(2)}) collective-permute-start(bf16[1728,256]{1,0:T(8,128)(2,1)} %collective-permute-done.17.refs_7_), channel_id=1, source_target_pairs={{0,1},{1,0},{2,3},{3,2},{4,5},{5,4},{6,7},{7,6},{8,9},{9,8},{10,11... | collective-permute-start | bytes 2654216 | tf_op jit(solution)/shard_map/ppermute | solution.py:44
  134.0 7.3 %collective-permute-start.27 = (bf16[1728,256]{1,0:T(8,128)(2,1)}, bf16[1728,256]{1,0:T(8,128)(2,1)}, u32[]{:S(2)}, u32[]{:S(2)}) collective-permute-start(bf16[1728,256]{1,0:T(8,128)(2,1)} %collective-permute-done.19.refs_8_), channel_id=1, source_target_pairs={{0,1},{1,0},{2,3},{3,2},{4,5},{5,4},{6,7},{7,6},{8,9},{9,8},{10,11... | collective-permute-start | bytes 2654216 | tf_op jit(solution)/shard_map/ppermute | solution.py:44
  140.8 15.5 %collective-permute-start.28 = (bf16[512,256]{1,0:T(8,128)(2,1)}, bf16[512,256]{1,0:T(8,128)(2,1)S(1)}, u32[]{:S(2)}, u32[]{:S(2)}) collective-permute-start(bf16[512,256]{1,0:T(8,128)(2,1)} %get-tuple-element.179), channel_id=1, source_target_pairs={{0,1},{1,0},{2,3},{3,2},{4,5},{5,4},{6,7},{7,6},{8,9},{9,8},{10,11... | collective-permute-start | bytes 786440 | tf_op jit(solution)/shard_map/ppermute | solution.py:44
  156.2 6.1 %collective-permute-start.30 = (bf16[256,2304]{1,0:T(8,128)(2,1)S(1)}, bf16[256,2304]{1,0:T(8,128)(2,1)S(1)}, u32[]{:S(2)}, u32[]{:S(2)}) collective-permute-start(bf16[256,2304]{1,0:T(8,128)(2,1)S(1)} %get-tuple-element.180.dhidden.d_mine), channel_id=1, source_target_pairs={{0,1},{1,0},{2,3},{3,2},{4,5},{5,4},{6,7},{7,6},{8,9},{9,8},{10,11... | collective-permute-start | bytes 3538952 | tf_op jit(solution)/shard_map/ppermute | solution.py:44
  161.6 3.8 %collective-permute-start.29 = (bf16[8,256,256]{2,1,0:T(8,128)(2,1)S(1)}, bf16[8,256,256]{2,1,0:T(8,128)(2,1)S(1)}, u32[]{:S(2)}, u32[]{:S(2)}) collective-permute-start(bf16[8,256,256]{2,1,0:T(8,128)(2,1)S(1)} %attention_back.1.d_mine), channel_id=1, source_target_pairs={{0,1},{1,0},{2,3},{3,2},{4,5},{5,4},{6,7},{7,6},{8,9},{9,8},{10,11... | collective-permute-start | bytes 3145736 | tf_op jit(solution)/shard_map/ppermute | solution.py:44
  165.4 10.1 %collective-permute-start.31 = (bf16[192,256]{1,0:T(8,128)(2,1)S(1)}, bf16[192,256]{1,0:T(8,128)(2,1)S(1)}, u32[]{:S(2)}, u32[]{:S(2)}) collective-permute-start(bf16[192,256]{1,0:T(8,128)(2,1)S(1)} %get-tuple-element.198), channel_id=1, source_target_pairs={{0,2},{1,3},{2,0},{3,1},{4,6},{5,7},{6,4},{7,5},{8,10},{9,11},{10,... | collective-permute-start | bytes 294920 | tf_op jit(solution)/shard_map/ppermute | solution.py:44
  168.4 7.2 %collective-permute-start.32 = (bf16[192,256]{1,0:T(8,128)(2,1)S(1)}, bf16[192,256]{1,0:T(8,128)(2,1)S(1)}, u32[]{:S(2)}, u32[]{:S(2)}) collective-permute-start(bf16[192,256]{1,0:T(8,128)(2,1)S(1)} %get-tuple-element.199), channel_id=1, source_target_pairs={{0,12},{1,13},{2,14},{3,15},{4,0},{5,1},{6,2},{7,3},{8,4},{9,5},{1... | collective-permute-start | bytes 294920 | tf_op jit(solution)/shard_map/ppermute | solution.py:44
  168.4 7.2 %collective-permute-start.33 = (bf16[192,256]{1,0:T(8,128)(2,1)S(1)}, bf16[192,256]{1,0:T(8,128)(2,1)S(1)}, u32[]{:S(2)}, u32[]{:S(2)}) collective-permute-start(bf16[192,256]{1,0:T(8,128)(2,1)S(1)} %get-tuple-element.200), channel_id=1, source_target_pairs={{0,4},{1,5},{2,6},{3,7},{4,8},{5,9},{6,10},{7,11},{8,12},{9,13},{1... | collective-permute-start | bytes 294920 | tf_op jit(solution)/shard_map/ppermute | solution.py:44
  175.6 7.6 %collective-permute-start.34 = (bf16[384,256]{1,0:T(8,128)(2,1)S(1)}, bf16[384,256]{1,0:T(8,128)(2,1)S(1)}, u32[]{:S(2)}, u32[]{:S(2)}) collective-permute-start(bf16[384,256]{1,0:T(8,128)(2,1)S(1)} %get-tuple-element.237), channel_id=1, source_target_pairs={{0,2},{1,3},{2,0},{3,1},{4,6},{5,7},{6,4},{7,5},{8,10},{9,11},{10,... | collective-permute-start | bytes 589832 | tf_op jit(solution)/shard_map/ppermute | solution.py:44
  176.4 6.8 %collective-permute-start.35 = (bf16[384,256]{1,0:T(8,128)(2,1)S(1)}, bf16[384,256]{1,0:T(8,128)(2,1)S(1)}, u32[]{:S(2)}, u32[]{:S(2)}) collective-permute-start(bf16[384,256]{1,0:T(8,128)(2,1)S(1)} %get-tuple-element.238), channel_id=1, source_target_pairs={{0,12},{1,13},{2,14},{3,15},{4,0},{5,1},{6,2},{7,3},{8,4},{9,5},{1... | collective-permute-start | bytes 589832 | tf_op jit(solution)/shard_map/ppermute | solution.py:44
  177.6 6.9 %collective-permute-start.36 = (bf16[384,256]{1,0:T(8,128)(2,1)S(1)}, bf16[384,256]{1,0:T(8,128)(2,1)S(1)}, u32[]{:S(2)}, u32[]{:S(2)}) collective-permute-start(bf16[384,256]{1,0:T(8,128)(2,1)S(1)} %get-tuple-element.239), channel_id=1, source_target_pairs={{0,4},{1,5},{2,6},{3,7},{4,8},{5,9},{6,10},{7,11},{8,12},{9,13},{1... | collective-permute-start | bytes 589832 | tf_op jit(solution)/shard_map/ppermute | solution.py:44
  184.7 17.5 %collective-permute-start.37 = (bf16[1152,256]{1,0:T(8,128)(2,1)S(1)}, bf16[1152,256]{1,0:T(8,128)(2,1)S(1)}, u32[]{:S(2)}, u32[]{:S(2)}) collective-permute-start(bf16[1152,256]{1,0:T(8,128)(2,1)S(1)} %get-tuple-element.243), channel_id=1, source_target_pairs={{0,4},{1,5},{2,6},{3,7},{4,8},{5,9},{6,10},{7,11},{8,12},{9,13},{1... | collective-permute-start | bytes 1769480 | tf_op jit(solution)/shard_map/ppermute | solution.py:44
  184.8 20.2 %collective-permute-start.38 = (bf16[1152,256]{1,0:T(8,128)(2,1)S(1)}, bf16[1152,256]{1,0:T(8,128)(2,1)S(1)}, u32[]{:S(2)}, u32[]{:S(2)}) collective-permute-start(bf16[1152,256]{1,0:T(8,128)(2,1)S(1)} %get-tuple-element.244), channel_id=1, source_target_pairs={{0,12},{1,13},{2,14},{3,15},{4,0},{5,1},{6,2},{7,3},{8,4},{9,5},{1... | collective-permute-start | bytes 1769480 | tf_op jit(solution)/shard_map/ppermute | solution.py:44
  188.0 17.5 %collective-permute-start.39 = (bf16[1152,256]{1,0:T(8,128)(2,1)S(1)}, bf16[1152,256]{1,0:T(8,128)(2,1)S(1)}, u32[]{:S(2)}, u32[]{:S(2)}) collective-permute-start(bf16[1152,256]{1,0:T(8,128)(2,1)S(1)} %get-tuple-element.245), channel_id=1, source_target_pairs={{0,2},{1,3},{2,0},{3,1},{4,6},{5,7},{6,4},{7,5},{8,10},{9,11},{10,... | collective-permute-start | bytes 1769480 | tf_op jit(solution)/shard_map/ppermute | solution.py:44
  190.9 15.9 %collective-permute-start.43 = (bf16[576,256]{1,0:T(8,128)(2,1)S(1)}, bf16[576,256]{1,0:T(8,128)(2,1)S(1)}, u32[]{:S(2)}, u32[]{:S(2)}) collective-permute-start(bf16[576,256]{1,0:T(8,128)(2,1)S(1)} %get-tuple-element.261), channel_id=1, source_target_pairs={{0,4},{1,5},{2,6},{3,7},{4,8},{5,9},{6,10},{7,11},{8,12},{9,13},{1... | collective-permute-start | bytes 884744 | tf_op jit(solution)/shard_map/ppermute | solution.py:44
  190.9 17.9 %collective-permute-start.44 = (bf16[576,256]{1,0:T(8,128)(2,1)S(1)}, bf16[576,256]{1,0:T(8,128)(2,1)S(1)}, u32[]{:S(2)}, u32[]{:S(2)}) collective-permute-start(bf16[576,256]{1,0:T(8,128)(2,1)S(1)} %get-tuple-element.262), channel_id=1, source_target_pairs={{0,12},{1,13},{2,14},{3,15},{4,0},{5,1},{6,2},{7,3},{8,4},{9,5},{1... | collective-permute-start | bytes 884744 | tf_op jit(solution)/shard_map/ppermute | solution.py:44
  202.2 11.3 %collective-permute-start.45 = (bf16[576,256]{1,0:T(8,128)(2,1)S(1)}, bf16[576,256]{1,0:T(8,128)(2,1)S(1)}, u32[]{:S(2)}, u32[]{:S(2)}) collective-permute-start(bf16[576,256]{1,0:T(8,128)(2,1)S(1)} %get-tuple-element.263), channel_id=1, source_target_pairs={{0,2},{1,3},{2,0},{3,1},{4,6},{5,7},{6,4},{7,5},{8,10},{9,11},{10,... | collective-permute-start | bytes 884744 | tf_op jit(solution)/shard_map/ppermute | solution.py:44
  204.9 9.9 %collective-permute-start.47 = (bf16[576,256]{1,0:T(8,128)(2,1)S(1)}, bf16[576,256]{1,0:T(8,128)(2,1)S(1)}, u32[]{:S(2)}, u32[]{:S(2)}) collective-permute-start(bf16[576,256]{1,0:T(8,128)(2,1)S(1)} %get-tuple-element.268), channel_id=1, source_target_pairs={{0,12},{1,13},{2,14},{3,15},{4,0},{5,1},{6,2},{7,3},{8,4},{9,5},{1... | collective-permute-start | bytes 884744 | tf_op jit(solution)/shard_map/ppermute | solution.py:44
  205.5 24.5 %collective-permute-start.41 = (bf16[1152,256]{1,0:T(8,128)(2,1)}, bf16[1152,256]{1,0:T(8,128)(2,1)S(1)}, u32[]{:S(2)}, u32[]{:S(2)}) collective-permute-start(bf16[1152,256]{1,0:T(8,128)(2,1)} %get-tuple-element.250), channel_id=1, source_target_pairs={{0,12},{1,13},{2,14},{3,15},{4,0},{5,1},{6,2},{7,3},{8,4},{9,5},{1... | collective-permute-start | bytes 1769480 | tf_op jit(solution)/shard_map/ppermute | solution.py:44
  206.7 23.3 %collective-permute-start.40 = (bf16[1152,256]{1,0:T(8,128)(2,1)}, bf16[1152,256]{1,0:T(8,128)(2,1)S(1)}, u32[]{:S(2)}, u32[]{:S(2)}) collective-permute-start(bf16[1152,256]{1,0:T(8,128)(2,1)} %get-tuple-element.249), channel_id=1, source_target_pairs={{0,4},{1,5},{2,6},{3,7},{4,8},{5,9},{6,10},{7,11},{8,12},{9,13},{1... | collective-permute-start | bytes 1769480 | tf_op jit(solution)/shard_map/ppermute | solution.py:44
  208.7 21.3 %collective-permute-start.42 = (bf16[1152,256]{1,0:T(8,128)(2,1)}, bf16[1152,256]{1,0:T(8,128)(2,1)S(1)}, u32[]{:S(2)}, u32[]{:S(2)}) collective-permute-start(bf16[1152,256]{1,0:T(8,128)(2,1)} %get-tuple-element.251), channel_id=1, source_target_pairs={{0,2},{1,3},{2,0},{3,1},{4,6},{5,7},{6,4},{7,5},{8,10},{9,11},{10,... | collective-permute-start | bytes 1769480 | tf_op jit(solution)/shard_map/ppermute | solution.py:44
  214.5 11.1 %collective-permute-start.46 = (bf16[576,256]{1,0:T(8,128)(2,1)}, bf16[576,256]{1,0:T(8,128)(2,1)S(1)}, u32[]{:S(2)}, u32[]{:S(2)}) collective-permute-start(bf16[576,256]{1,0:T(8,128)(2,1)} %get-tuple-element.267), channel_id=1, source_target_pairs={{0,4},{1,5},{2,6},{3,7},{4,8},{5,9},{6,10},{7,11},{8,12},{9,13},{1... | collective-permute-start | bytes 884744 | tf_op jit(solution)/shard_map/ppermute | solution.py:44
  214.9 14.2 %collective-permute-start.48 = (bf16[576,256]{1,0:T(8,128)(2,1)}, bf16[576,256]{1,0:T(8,128)(2,1)S(1)}, u32[]{:S(2)}, u32[]{:S(2)}) collective-permute-start(bf16[576,256]{1,0:T(8,128)(2,1)} %get-tuple-element.269), channel_id=1, source_target_pairs={{0,2},{1,3},{2,0},{3,1},{4,6},{5,7},{6,4},{7,5},{8,10},{9,11},{10,... | collective-permute-start | bytes 884744 | tf_op jit(solution)/shard_map/ppermute | solution.py:44
  (44 other events, 424.9 us)

commit v4 on v3

--- a/solution.py
+++ b/solution.py
@@ -64,42 +64,45 @@
 
 
 def pack_kernel(*refs):
-    given, out, held, sems = refs[:4], refs[4], refs[5:9], refs[9]
+    given, outs, held, sems = refs[:8], refs[8:10], refs[10:18], refs[18]
     copies = [pltpu.make_async_copy(w, h, sems.at[i]) for i, (w, h) in enumerate(zip(given, held))]
     for copy in copies:
         copy.start()
-    row = 0
-    for copy, ref in zip(copies, held):
+    for i, (copy, ref) in enumerate(zip(copies, held)):
+        row = 0 if i % 4 == 0 else row
         copy.wait()
         rows, cols = ref.shape
         for p in range(cols // HEAD):
-            out[row : row + rows] = ref[:, HEAD * p : HEAD * (p + 1)]
+            outs[i // 4][row : row + rows] = ref[:, HEAD * p : HEAD * (p + 1)]
             row += rows
 
 
 def pack(*weights):
     return pl.pallas_call(
         pack_kernel,
-        out_shape=shape((PACKED, HEAD)),
-        in_specs=[HBM] * 4,
-        out_specs=VMEM,
-        scratch_shapes=[pltpu.VMEM(w.shape, BF16) for w in weights] + [pltpu.SemaphoreType.DMA((4,))],
+        out_shape=[shape((PACKED, HEAD))] * 2,
+        in_specs=[HBM] * 8,
+        out_specs=[VMEM] * 2,
+        scratch_shapes=[pltpu.VMEM(w.shape, BF16) for w in weights] + [pltpu.SemaphoreType.DMA((8,))],
         compiler_params=limit(60),
-        cost_estimate=cost(0, 4_000_000),
+        cost_estimate=cost(0, 8_000_000),
         name="pack",
     )(*weights)
 
 
 QKV_PART = QKV_PANELS * QKV_ROWS
 
-SLOTS = [(0, 0), (3, 0), (0, 1), (1, 0), (2, 0), (3, 1), (1, 1), (2, 1)]
+SLOTS = [(0, 0), (3, 0), (0, 1), (1, 0), (3, 1), (2, 0), (1, 1), (2, 1)]
 SLOT_ROWS = 2 * QKV_ROWS
-OWN_EARLY, PEER_EARLY = 4, 3
+EARLY = 4
 
 
 def rms(values, gain):
     mean = jnp.sum(values * values, -1, keepdims=True) * (1.0 / D)
     return values * lax.rsqrt(mean + EPSILON) * gain
+
+
+CHIPS = [(0, 0), (1, 0), (2, 0), (3, 0), (0, 1), (1, 1), (2, 1), (3, 1)]
 
 
 def chip_index(position, dx, dy):
@@ -162,7 +165,7 @@
 
 
 def prepare_kernel(pos_ref, x_ref, gains_ref, *refs):
-    parts, (n_mine, n_send, turned, ordered) = refs[:4], refs[4:]
+    early, late, n_mine, n_send, turned, ordered = refs
     normed = rms(x_ref[...].astype(F32), gains_ref[0:1, :]).astype(BF16)
     turned[...] = normed.T
 
@@ -174,14 +177,12 @@
         for dc in range(2):
             to = SLOT_ROWS * slot + QKV_ROWS * dc
             ordered[to : to + QKV_ROWS] = rows_of(device_index(position, dx, dy, dc))
-    for split, early, late in ((OWN_EARLY, *parts[:2]), (PEER_EARLY, *parts[2:])):
-        early[...] = ordered[0 : SLOT_ROWS * split].T
-        late[...] = ordered[SLOT_ROWS * split :].T
-    core = position % 2
-    for chip in range(8):
+    early[...] = ordered[0 : SLOT_ROWS * EARLY].T
+    late[...] = ordered[SLOT_ROWS * EARLY :].T
+    for chip, (dx, dy) in enumerate(CHIPS):
         to = slice(QKV_ROWS * chip, QKV_ROWS * (chip + 1))
-        n_mine[to] = rows_of(2 * chip + core)
-        n_send[to] = rows_of(2 * chip + 1 - core)
+        n_mine[to] = rows_of(device_index(position, dx, dy, 0))
+        n_send[to] = rows_of(device_index(position, dx, dy, 1))
 
 
 def early_kernel(slots, normed, *refs):
@@ -196,9 +197,10 @@
     lax.fori_loop(0, QKV_PANELS, one_panel, 0)
 
 
-def layer(position, early, slots, x_ref, gains_ref, head_ref, normed, acc, pieces, qkv, context, hidden, wqkv, wo, sems):
+def layer(position, early, slots, x_ref, gains_ref, head_ref, normed, acc, pieces, qkv, context, hidden, wqkv, wo, sems, reached=lambda stage: None):
     load_qkv(slots[early:], pieces, wqkv, sems.at[0])
     load_out(position, slots, pieces, wo, sems.at[1])
+    reached("loads")
     wait_for(wqkv, sems.at[0])
 
     def one_panel(p, carry):
@@ -206,6 +208,7 @@
         return carry
 
     lax.fori_loop(0, QKV_PANELS, one_panel, 0)
+    reached("qkv")
     causal = causal_mask()
     for h in range(HQ):
         group = h // (HQ // HK)
@@ -214,6 +217,7 @@
             probs.astype(BF16), qkv[HQ + HK + group]
         ).astype(BF16)
     wait_for(wo, sems.at[1])
+    reached("out")
 
     def one_out(p, carry):
         cols = pl.ds(pl.multiple_of(p * HEAD, HEAD), HEAD)
@@ -221,36 +225,51 @@
         return carry
 
     lax.fori_loop(0, O_PANELS, one_out, 0)
+    reached("hidden")
     final = rms(hidden[...], gains_ref[1:2, :]).astype(BF16)
     logits = LABEL_CAP * jnp.tanh(nn(final, head_ref[...]) * (1.0 / LABEL_CAP))
     return logits, logits - jnp.log(jnp.sum(jnp.exp(logits), -1, keepdims=True))
 
 
 def own_kernel(slots, pos_ref, x_ref, gains_ref, head_ref, normed, acc, *refs):
-    pieces, refs = refs[:-14], refs[-14:]
-    c_mine, c_send, qkv_out, hidden_out, logits, wo_out, qkv, hidden, context, turned, wqkv, wo, sems, out_sems = refs
+    pieces, refs = refs[:-18], refs[-18:]
+    c_mine, c_send, qkv_out, hidden_out, logits, wo_out = refs[:6]
+    x, head, late, sums, qkv, hidden, context, turned, wqkv, wo, sems, more_sems = refs[6:]
     position = pos_ref[0]
+
+    def copy(source, target, i):
+        return pltpu.make_async_copy(source, target, more_sems.at[i])
+
+    reads = [copy(normed, late, 0), copy(acc, sums, 1), copy(x_ref, x, 2), copy(head_ref, head, 3)]
+    writes = [copy(qkv, qkv_out, 4), copy(wo, wo_out, 5), copy(hidden, hidden_out, 6)]
+
+    def reached(stage):
+        if stage == "loads":
+            for read in reads:
+                read.start()
+            reads[0].wait()
+            reads[1].wait()
+        if stage == "qkv":
+            writes[0].start()
+        if stage == "out":
+            writes[1].start()
+            reads[2].wait()
+        if stage == "hidden":
+            writes[2].start()
+            reads[3].wait()
+
     logits[...], _ = layer(
-        *(position, OWN_EARLY, slots, x_ref, gains_ref, head_ref, normed, acc, pieces),
-        *(qkv, context, hidden, wqkv, wo, sems),
-    )
-    copies = [
-        pltpu.make_async_copy(wo, wo_out, out_sems.at[0]),
-        pltpu.make_async_copy(hidden, hidden_out, out_sems.at[1]),
-        pltpu.make_async_copy(qkv, qkv_out, out_sems.at[2]),
-    ]
-    for copy in copies:
-        copy.start()
+        *(position, EARLY, slots, x, gains_ref, head, late, sums, pieces),
+        *(qkv, context, hidden, wqkv, wo, sems, reached),
+    )
     turned[...] = context[...].T
-    core = position % 2
-    for chip in range(8):
+    for chip, (dx, dy) in enumerate(CHIPS):
         to = slice(O_ROWS * chip, O_ROWS * (chip + 1))
-        at = pl.multiple_of((2 * chip + core) * O_ROWS, 16)
-        c_mine[to] = turned[pl.ds(at, O_ROWS)]
-        at = pl.multiple_of((2 * chip + 1 - core) * O_ROWS, 16)
-        c_send[to] = turned[pl.ds(at, O_ROWS)]
-    for copy in copies:
-        copy.wait()
+        for dc, out in ((0, c_mine), (1, c_send)):
+            at = pl.multiple_of(device_index(position, dx, dy, dc) * O_ROWS, 16)
+            out[to] = turned[pl.ds(at, O_ROWS)]
+    for write in writes:
+        write.wait()
 
 
 def peer_kernel(
@@ -259,7 +278,7 @@
     pieces, refs = refs[:-8], refs[-8:]
     loss, dhidden, qkv, context, hidden, wqkv, wo, sems = refs
     _, peer_lp = layer(
-        pos_ref[0], PEER_EARLY, slots, x_ref, gains_ref, head_ref, normed, acc, pieces, qkv, context, hidden, wqkv, wo, sems
+        pos_ref[0], EARLY, slots, x_ref, gains_ref, head_ref, normed, acc, pieces, qkv, context, hidden, wqkv, wo, sems
     )
     logits = own_logits[...]
     own_lp = logits - jnp.log(jnp.sum(jnp.exp(logits), -1, keepdims=True))
@@ -278,76 +297,68 @@
     dhidden[...] = (d_final * scale - own * (scale * scale * scale * along)).astype(BF16)
 
 
-def attention_back_kernel(dhidden, wo_panels, qkv, dqkv, wo, sem):
+def attention_back_kernel(dhidden, wo_panels, qkv, dqkv, wo, probs, capped, sem):
     for p in range(O_PANELS):
         pltpu.make_async_copy(wo_panels.at[p], wo.at[:, pl.ds(HEAD * p, HEAD)], sem).start()
+    causal = causal_mask()
+    for h in range(HQ):
+        probs[h], capped[h] = probabilities(qkv[h], qkv[HQ + h // (HQ // HK)], causal)
     wait_for(wo, sem)
-    causal = causal_mask()
     for group in range(HK):
         key, value = qkv[HQ + group], qkv[HQ + HK + group]
         d_key = jnp.zeros((SEQ, HEAD), F32)
         d_value = jnp.zeros((SEQ, HEAD), F32)
         for h in range(group * (HQ // HK), (group + 1) * (HQ // HK)):
-            query = qkv[h]
-            probs, capped = probabilities(query, key, causal)
             d_out = nt(dhidden[...], wo[HEAD * h : HEAD * (h + 1), :]).astype(BF16)
-            d_value += tn(probs.astype(BF16), d_out)
+            d_value += tn(probs[h].astype(BF16), d_out)
             d_probs = nt(d_out, value).astype(BF16).astype(F32)
-            d_scores = probs * (d_probs - jnp.sum(d_probs * probs, -1, keepdims=True))
-            d_raw = (d_scores * (1.0 - capped * capped) * (1.0 / math.sqrt(HEAD))).astype(BF16)
+            d_scores = probs[h] * (d_probs - jnp.sum(d_probs * probs[h], -1, keepdims=True))
+            slope = (1.0 - capped[h] * capped[h]) * (1.0 / math.sqrt(HEAD))
+            d_raw = (d_scores * slope).astype(BF16)
             dqkv[h] = nn(d_raw, key).astype(BF16)
-            d_key += tn(d_raw, query)
+            d_key += tn(d_raw, qkv[h])
         dqkv[HQ + group] = d_key.astype(BF16)
         dqkv[HQ + HK + group] = d_value.astype(BF16)
 
 
-CHIPS = [(0, 0), (1, 0), (2, 0), (3, 0), (0, 1), (1, 1), (2, 1), (3, 1)]
-
-
-def block_outs(outs):
-    return [[o] for o in outs[:6]] + [list(outs[6:9])] + [[outs[9]]]
-
-
-def hand_out(position, outs, whole_blocks):
-    for parts, (dx, dy) in zip(block_outs(outs), CHIPS):
-        at = chip_index(position, dx, dy)
-        row = 0
-        for part in parts:
-            part[...] = whole_blocks[at, row : row + part.shape[0]]
-            row += part.shape[0]
-
-
-def out_grad_kernel(pos_ref, mine, other, d_mine, d_other, *refs):
-    outs, (lhs, rhs, blocks) = refs[:10], refs[10:]
+def store(outs, split, panel, total):
+    rows = total.shape[0] // 8
+    to = pl.ds(pl.multiple_of(panel * rows, 16), rows)
+    for chip, out in enumerate((*outs[:6], split, outs[9])):
+        out[to] = total[rows * chip : rows * (chip + 1)]
+
+
+def hand_out(outs, split):
+    for third, out in enumerate(outs[6:9]):
+        rows = out.shape[0]
+        out[...] = split[rows * third : rows * (third + 1)]
+
+
+def out_grad_kernel(mine, other, d_mine, d_other, *refs):
+    outs, (lhs, rhs, split) = refs[:10], refs[10:]
     lhs[:, 0:SEQ], lhs[:, SEQ : 2 * SEQ] = mine[...], other[...]
     rhs[0:SEQ], rhs[SEQ : 2 * SEQ] = d_mine[...], d_other[...]
 
     def one_panel(p, carry):
         cols = pl.ds(pl.multiple_of(p * HEAD, HEAD), HEAD)
-        rows = pl.ds(pl.multiple_of(p * O_ROWS, 16), O_ROWS)
-        total = nn(lhs[...], rhs[:, cols]).astype(BF16)
-        for chip in range(8):
-            blocks[chip, rows] = total[O_ROWS * chip : O_ROWS * (chip + 1)]
+        store(outs, split, p, nn(lhs[...], rhs[:, cols]).astype(BF16))
         return carry
 
     lax.fori_loop(0, O_PANELS, one_panel, 0)
-    hand_out(pos_ref[0], outs, blocks)
-
-
-def qkv_grad_kernel(pos_ref, mine, other, d_mine, d_other, *refs):
-    outs, (lhs, rhs, blocks) = refs[:10], refs[10:]
+    hand_out(outs, split)
+
+
+def qkv_grad_kernel(mine, other, d_mine, d_other, *refs):
+    outs, (lhs, rhs, split) = refs[:10], refs[10:]
     lhs[:, 0:SEQ], lhs[:, SEQ : 2 * SEQ] = mine[...], other[...]
     rhs[:, 0:SEQ], rhs[:, SEQ : 2 * SEQ] = d_mine[...], d_other[...]
 
     def one_panel(p, carry):
-        rows = pl.ds(pl.multiple_of(p * QKV_ROWS, 16), QKV_ROWS)
-        total = nn(lhs[...], rhs[p]).astype(BF16)
-        for chip in range(8):
-            blocks[chip, rows] = total[QKV_ROWS * chip : QKV_ROWS * (chip + 1)]
+        store(outs, split, p, nn(lhs[...], rhs[p]).astype(BF16))
         return carry
 
     lax.fori_loop(0, QKV_PANELS, one_panel, 0)
-    hand_out(pos_ref[0], outs, blocks)
+    hand_out(outs, split)
 
 
 def prepare(position, x, gains):
@@ -355,11 +366,11 @@
         prepare_kernel,
         out_shape=[
             shape((SEQ, SLOT_ROWS * count))
-            for count in (OWN_EARLY, 8 - OWN_EARLY, PEER_EARLY, 8 - PEER_EARLY)
+            for count in (EARLY, 8 - EARLY)
         ]
         + [shape((D // 2, SEQ))] * 2,
         in_specs=[SMEM, VMEM, VMEM],
-        out_specs=[VMEM] * 6,
+        out_specs=[VMEM] * 4,
         scratch_shapes=[pltpu.VMEM((D, SEQ), BF16)] * 2,
         compiler_params=limit(20),
         cost_estimate=cost(10_000_000, 10_000_000),
@@ -395,17 +406,21 @@
             shape((SEQ, LABELS), F32),
             shape((O_PANELS, HQ * HEAD, HEAD)),
         ],
-        in_specs=[SMEM] + [VMEM] * 5 + [ANY] * len(arrays),
+        in_specs=[SMEM, ANY, VMEM, ANY, ANY, ANY] + [ANY] * len(arrays),
         out_specs=[VMEM, VMEM, HBM, HBM, VMEM, HBM],
         scratch_shapes=[
+            pltpu.VMEM((SEQ, D), BF16),
+            pltpu.VMEM((D, LABELS), BF16),
+            pltpu.VMEM((SEQ, SLOT_ROWS * (8 - EARLY)), BF16),
+            pltpu.VMEM((QKV_PANELS, SEQ, HEAD), F32),
             pltpu.VMEM((QKV_PANELS, SEQ, HEAD), BF16),
             pltpu.VMEM((SEQ, D), F32),
             pltpu.VMEM((SEQ, HQ * HEAD), BF16),
             pltpu.VMEM((HQ * HEAD, SEQ), BF16),
-            some_wqkv(8 - OWN_EARLY),
+            some_wqkv(8 - EARLY),
             pltpu.VMEM((O_PANELS, HQ * HEAD, HEAD), BF16),
             pltpu.SemaphoreType.DMA((2,)),
-            pltpu.SemaphoreType.DMA((3,)),
+            pltpu.SemaphoreType.DMA((7,)),
         ],
         compiler_params=limit(60),
         cost_estimate=cost(3_000_000_000, 30_000_000),
@@ -423,7 +438,7 @@
             pltpu.VMEM((QKV_PANELS, SEQ, HEAD), BF16),
             pltpu.VMEM((SEQ, HQ * HEAD), BF16),
             pltpu.VMEM((SEQ, D), F32),
-            some_wqkv(8 - PEER_EARLY),
+            some_wqkv(8 - EARLY),
             pltpu.VMEM((O_PANELS, HQ * HEAD, HEAD), BF16),
             pltpu.SemaphoreType.DMA((2,)),
         ],
@@ -439,29 +454,34 @@
         out_shape=shape((QKV_PANELS, SEQ, HEAD)),
         in_specs=[VMEM, HBM, VMEM],
         out_specs=VMEM,
-        scratch_shapes=[pltpu.VMEM((HQ * HEAD, D), BF16), pltpu.SemaphoreType.DMA],
+        scratch_shapes=[
+            pltpu.VMEM((HQ * HEAD, D), BF16),
+            pltpu.VMEM((HQ, SEQ, SEQ), F32),
+            pltpu.VMEM((HQ, SEQ, SEQ), F32),
+            pltpu.SemaphoreType.DMA,
+        ],
         compiler_params=limit(20),
         cost_estimate=cost(2_000_000_000, 16_000_000),
         name="attention_back",
     )(dhidden, wo, qkv)
 
 
-def weight_grads(kernel, rows, panels, rhs, position, mine, other, d_mine, d_other, name):
+def weight_grads(kernel, rows, panels, rhs, mine, other, d_mine, d_other, name):
     block = rows * panels
     return pl.pallas_call(
         kernel,
         out_shape=[shape((block, HEAD))] * 6 + [shape((block // 3, HEAD))] * 3 + [shape((block, HEAD))],
-        in_specs=[SMEM] + [VMEM] * 4,
+        in_specs=[VMEM] * 4,
         out_specs=[VMEM] * 10,
         scratch_shapes=[
             pltpu.VMEM((8 * rows, 2 * SEQ), BF16),
             pltpu.VMEM(rhs, BF16),
-            pltpu.VMEM((8, block, HEAD), BF16),
+            pltpu.VMEM((block, HEAD), BF16),
         ],
         compiler_params=limit(28),
         cost_estimate=cost(2 * 8 * rows * 2 * SEQ * panels * HEAD, 10_000_000),
         name=name,
-    )(position, mine, other, d_mine, d_other)
+    )(mine, other, d_mine, d_other)
 
 
 def third_added_kernel(a2, o3, o1, in_a, in_b, in_c, a2_out, o3_out, o1_out):
@@ -548,47 +568,39 @@
     x = activations[0, 0]
     replicas = lax.axis_size("replica")
 
-    own = pack(own_q[0], own_k[0], own_v[0], own_o[0])
-    peer = pack(peer_q[0], peer_k[0], peer_v[0], peer_o[0])
+    own, peer = pack(
+        *(own_q[0], own_k[0], own_v[0], own_o[0]), *(peer_q[0], peer_k[0], peer_v[0], peer_o[0])
+    )
 
     a1, a3 = moved(own, to_prev_x), moved(own, to_next_x)
     peer = lax.ppermute(peer, "replica", [(i, (i + 1) % replicas) for i in range(replicas)])
-    prepared = prepare(position, x, norm_gains)
-    a1, a3, peer, own, prepared = together((a1, a3, peer, own, prepared))
-    n_early, n_late, n_peer_early, n_peer_late, n_mine, n_send = prepared
+    s_own = moved(own, to_core)
+    *prepared, n_send = prepare(position, x, norm_gains)
+    n_other = moved(n_send, to_core)
+    column = labels[0, 0].reshape(SEQ, 1)
+    a1, a3, own, s_own, n_other, prepared, column = together(
+        (a1, a3, own, s_own, n_other, prepared, column)
+    )
+    n_early, n_late, n_mine = prepared
 
     y0, a2, p_a3 = moved(own, to_y), moved(a1, to_prev_x), moved(peer, to_next_x)
-    n_other = moved(n_send, to_core)
-    joined = jnp.concatenate([own, a3, a1], 0)
-    y0, a2, p_a3, joined, n_other = together((y0, a2, p_a3, joined, n_other))
+    s_a1, s_a3 = moved(a1, to_core), moved(a3, to_core)
+    y0, a2, p_a3, s_a1, s_a3 = together((y0, a2, p_a3, s_a1, s_a3))
 
     p_y0, o3, o1 = moved(peer, to_y), moved(y0, to_next_x), moved(y0, to_prev_x)
-    swap_first, swap_a2 = moved(joined, to_core), moved(a2, to_core)
-    p_y0, o3, o1, swap_first, swap_a2 = together((p_y0, o3, o1, swap_first, swap_a2))
+    s_y0, s_a2 = moved(y0, to_core), moved(a2, to_core)
+    p_y0, o3, o1, s_y0, s_a2 = together((p_y0, o3, o1, s_y0, s_a2))
 
     o2, p_a1, p_o3 = moved(a2, to_y), moved(peer, to_prev_x), moved(p_y0, to_next_x)
-    swap_y0, swap_o3 = moved(y0, to_core), moved(o3, to_core)
-
-    def all_of(piece, at=0):
-        return (piece, at)
-
-    own_slots = [
-        (all_of(0), all_of(4, 0)),
-        (all_of(1), all_of(4, PACKED)),
-        (all_of(2), all_of(5)),
-        (all_of(3), all_of(4, 2 * PACKED)),
-        (all_of(6), all_of(10)),
-        (all_of(7), all_of(11)),
-        (all_of(8), all_of(12)),
-        (all_of(9), all_of(13)),
-    ]
-    acc = early_pass(n_early, [own, a3, y0, a1, swap_first, swap_y0], own_slots[:OWN_EARLY])
+    s_o3, s_o1 = moved(o3, to_core), moved(o1, to_core)
+    early, s_early = [own, a3, y0, a1], [s_own, s_a3, s_y0, s_a1]
+    acc = early_pass(n_early, early + s_early, [((i, 0), (4 + i, 0)) for i in range(4)])
     joined = jnp.concatenate([peer, p_a3, p_y0], 0)
-    o2, p_a1, p_o3, swap_o3, joined, acc = together((o2, p_a1, p_o3, swap_o3, joined, acc))
+    o2, p_a1, p_o3, s_o3, s_o1, joined, acc = together((o2, p_a1, p_o3, s_o3, s_o1, joined, acc))
 
     p_o1, p_a2, p_o2 = moved(p_a1, to_y), moved(p_a1, to_prev_x), moved(p_o3, to_next_x)
-    swap_o1, swap_o2 = moved(o1, to_core), moved(o2, to_core)
-    p_swap_first = moved(joined, to_core)
+    s_o2, s_joined = moved(o2, to_core), moved(joined, to_core)
+    s_p_a1 = moved(p_a1, to_core)
     c_mine, c_send, qkv, hidden, logits, wo = own_pass(
         position,
         x,
@@ -596,31 +608,31 @@
         label_head,
         n_late,
         acc,
-        [own, a3, y0, a1, swap_first, swap_y0, a2, o3, o1, o2, swap_a2, swap_o3, swap_o1, swap_o2],
-        own_slots,
-    )
-    p_o1, p_a2, p_o2, p_swap_first, c_send, hidden = together(
-        (p_o1, p_a2, p_o2, p_swap_first, c_send, hidden)
-    )
-
-    late = [p_a1, p_a2, p_o3, p_o1, p_o2]
-    swap_late = [moved(piece, to_core) for piece in late]
+        early + [o3, a2, o1, o2] + s_early + [s_o3, s_a2, s_o1, s_o2],
+        [((i, 0), (8 + i, 0)) for i in range(8)],
+    )
+    p_o1, p_a2, p_o2, s_joined, s_p_a1, c_send, hidden = together(
+        (p_o1, p_a2, p_o2, s_joined, s_p_a1, c_send, hidden)
+    )
+
+    late = [p_o3, p_a2, p_o1, p_o2]
+    s_late = [moved(piece, to_core) for piece in late]
     c_other = moved(c_send, to_core)
-    peer_slots = [(all_of(i), all_of(3, PACKED * i)) for i in range(PEER_EARLY)]
-    p_acc = early_pass(n_peer_early, [peer, p_a3, p_y0, p_swap_first], peer_slots)
-    peer_slots = peer_slots + [(all_of(4 + i), all_of(9 + i)) for i in range(8 - PEER_EARLY)]
+    arrays = [peer, p_a3, p_y0, p_a1, s_joined, s_p_a1]
+    slots = [((i, 0), (4, PACKED * i)) for i in range(3)] + [((3, 0), (5, 0))]
+    p_acc = early_pass(n_early, arrays, slots)
     loss, dhidden = peer_pass(
         position,
         x,
         norm_gains,
         label_head,
-        n_peer_late,
+        n_late,
         p_acc,
-        labels[0, 0].reshape(SEQ, 1),
+        column,
         logits,
         hidden,
-        [peer, p_a3, p_y0, p_swap_first, *late, *swap_late],
-        peer_slots,
+        arrays + late + s_late,
+        slots + [((6 + i, 0), (10 + i, 0)) for i in range(4)],
     )
     dhidden, c_other = together((dhidden, c_other))
     d_other = moved(dhidden, to_core)
@@ -629,16 +641,16 @@
     out_blocks = weight_grads(
         out_grad_kernel,
         *(O_ROWS, O_PANELS, (2 * SEQ, D)),
-        *(position, c_mine, c_other, dhidden, d_other, "out_grads"),
+        *(c_mine, c_other, dhidden, d_other, "out_grads"),
     )
     dqkv, dqkv_other, *out_blocks = together((dqkv, dqkv_other, *out_blocks))
     qkv_blocks = weight_grads(
         qkv_grad_kernel,
         *(QKV_ROWS, QKV_PANELS, (QKV_PANELS, 2 * SEQ, HEAD)),
-        *(position, n_mine, n_other, dqkv, dqkv_other, "qkv_grads"),
+        *(n_mine, n_other, dqkv, dqkv_other, "qkv_grads"),
     )
     in_a, in_b, in_c, *qkv_blocks = together((*reduce_first(out_blocks), *qkv_blocks))
-    added, qkv_blocks = together((add_thirds(out_blocks, (in_a, in_b, in_c)), qkv_blocks))
+    added = add_thirds(out_blocks, (in_a, in_b, in_c))
     (grad_out,) = reduce_rest(out_blocks, added, O_ROWS, [D])
     added = add_thirds(qkv_blocks, together(reduce_first(qkv_blocks)))
     grads = reduce_rest(qkv_blocks, added, QKV_ROWS, [HQ * HEAD, HK * HEAD, HK * HEAD])

time: 235 us -> 224 us (0.953); the launches traced: 231 us -> 223 us
  Pallas kernels: 58.9 us -> 54.3 us
  local copies, waits for them, and re-layouts: 15 us -> 19.6 us
  starting transfers between devices: 52.4 us -> 48.2 us
  other arithmetic: 5.83 us -> 3.32 us
    unnamed x86 -> x90, local copies, waits for them, and re-layouts: 14.2 us -> 18.8 us
    ppermute x48 -> x50, starting transfers between devices: 52.2 us -> 48 us  [moved(): return lax.ppermute(value, 'fsdp', [(i, target(i)) for i in range(N_FSDP)])]
    ppermute x48 -> x50, waiting for transfers between devices: 96.8 us -> 96.7 us  [moved(): return lax.ppermute(value, 'fsdp', [(i, target(i)) for i in range(N_FSDP)])]
  transfers between devices with their start and end apart: 49 -> 51, of which waited for: 23 -> 24; matrix products, arithmetic and copies ran while one was open for 3% -> 2% of each run, Pallas kernels for 24% -> 22%
where the time goes in v4:
time: 224 us; the launch traced here: 223 us
  waiting for transfers between devices  96.7 us (43%)
  Pallas kernels  54.3 us (24%)
  starting transfers between devices  48.2 us (22%)
  local copies, waits for them, and re-layouts  19.6 us (9%)
  other arithmetic  3.32 us (1%)
    ppermute x50, waiting for transfers between devices, moved(): return lax.ppermute(value, 'fsdp', [(i, target(i)) for i in range(N_FSDP)])  96.7 us
    ppermute x50, starting transfers between devices, moved(): return lax.ppermute(value, 'fsdp', [(i, target(i)) for i in range(N_FSDP)])  48 us
    unnamed x90, local copies, waits for them, and re-layouts  18.8 us
    pallas_call x1, Pallas kernels, own_pass(): pl.pallas_call(functools.partial(own_kernel, slots), out_shape=[shape((HQ...  14.1 us
    pallas_call x1, Pallas kernels, peer_pass(): pl.pallas_call(functools.partial(peer_kernel, slots), out_shape=[shape((S...  11.3 us
    pallas_call x2, Pallas kernels, weight_grads(): pl.pallas_call(kernel, out_shape=[shape((block, HEAD))] * 6 + [shape((blo...  7.52 us
    pallas_call x2, Pallas kernels, early_pass(): pl.pallas_call(functools.partial(early_kernel, slots), out_shape=shape((Q...  7.49 us
    pallas_call x1, Pallas kernels, attention_back(): pl.pallas_call(attention_back_kernel, out_shape=shape((QKV_PANELS, SEQ, H...  5.45 us
  transfers between devices with their start and end apart: 51, of which 24 were waited for; matrix products, arithmetic and copies ran while one was open for 2% of the time, Pallas kernels for 22%

profile of v4, /device:TPU:96, one launch (start us, length us, event | category | flops | bytes accessed | tf_op | source)
XLA Modules:
  0.0 223.2 jit_solution(7190106901738785036)
XLA Ops:
  0.6 2.8 %pack.1 = (bf16[1728,256]{1,0:T(8,128)(2,1)}, bf16[1728,256]{1,0:T(8,128)(2,1)}) custom-call(bf16[144,1024]{1,0:T(8,128)(2,1)} %bitcast.22, bf16[144,512]{1,0:T(8,128)(2,1)} %bitcast.26, bf16[144,512]{1,0:T(8,128)(2,1)} %bitcast.27, bf16[64,2304]{1,0:T(8,128)(2,1)} %bitcast.23, bf16[144,1024]{1,0:T(8,128)(2,1)} %bitcast.24, bf16[144,512]{1,0:T(8,128)(2,1)} %bitcast.28, ...), custom_call_target="tpu_custom_call" | custom-call | bytes 8000000 | tf_op jit(solution)/shard_map/pack/pallas_call | solution.py:81
  3.4 2.8 %collective-permute-start = (bf16[1728,256]{1,0:T(8,128)(2,1)}, bf16[1728,256]{1,0:T(8,128)(2,1)S(1)}, u32[]{:S(2)}, u32[]{:S(2)}) collective-permute-start(bf16[1728,256]{1,0:T(8,128)(2,1)} %get-tuple-element.135.refs_0_), channel_id=1, source_target_pairs={{0,12},{1,13},{2,14},{3,15},{4,0},{5,1},{6,2},{7,3},{8,4},{9,5},{1... | collective-permute-start | bytes 2654216 | tf_op jit(solution)/shard_map/ppermute | solution.py:44
  6.5 1.3 copy-done
  11.4 1.7 collective-permute-done.3.other
  14.0 11.5 %collective-permute-done.refs_3_ = bf16[1728,256]{1,0:T(8,128)(2,1)S(1)} collective-permute-done((bf16[1728,256]{1,0:T(8,128)(2,1)}, bf16[1728,256]{1,0:T(8,128)(2,1)S(1)}, u32[]{:S(2)}, u32[]{:S(2)}) %collective-permute-start) | collective-permute-done | bytes 884768 | tf_op jit(solution)/shard_map/ppermute | solution.py:44
  25.5 3.3 %collective-permute-done.1.refs_1_ = bf16[1728,256]{1,0:T(8,128)(2,1)S(1)} collective-permute-done((bf16[1728,256]{1,0:T(8,128)(2,1)}, bf16[1728,256]{1,0:T(8,128)(2,1)S(1)}, u32[]{:S(2)}, u32[]{:S(2)}) %collective-permute-start.1) | collective-permute-done | bytes 884768 | tf_op jit(solution)/shard_map/ppermute | solution.py:44
  29.1 3.2 %collective-permute-start.5 = (bf16[1728,256]{1,0:T(8,128)(2,1)}, bf16[1728,256]{1,0:T(8,128)(2,1)S(1)}, u32[]{:S(2)}, u32[]{:S(2)}) collective-permute-start(bf16[1728,256]{1,0:T(8,128)(2,1)} %get-tuple-element.135.refs_0_), channel_id=1, source_target_pairs={{0,2},{1,3},{2,0},{3,1},{4,6},{5,7},{6,4},{7,5},{8,10},{9,11},{10,... | collective-permute-start | bytes 2654216 | tf_op jit(solution)/shard_map/ppermute | solution.py:44
  32.6 1.7 collective-permute-start.7
  34.3 14.7 %collective-permute-done.6.refs_5_ = bf16[1728,256]{1,0:T(8,128)(2,1)S(1)} collective-permute-done((bf16[1728,256]{1,0:T(8,128)(2,1)S(1)}, bf16[1728,256]{1,0:T(8,128)(2,1)S(1)}, u32[]{:S(2)}, u32[]{:S(2)}) %collective-permute-start.6) | collective-permute-done | bytes 884768 | tf_op jit(solution)/shard_map/ppermute | solution.py:44
  49.0 3.2 %collective-permute-start.10 = (bf16[1728,256]{1,0:T(8,128)(2,1)S(1)}, bf16[1728,256]{1,0:T(8,128)(2,1)S(1)}, u32[]{:S(2)}, u32[]{:S(2)}) collective-permute-start(bf16[1728,256]{1,0:T(8,128)(2,1)S(1)} %collective-permute-done.4.refs_0_), channel_id=1, source_target_pairs={{0,2},{1,3},{2,0},{3,1},{4,6},{5,7},{6,4},{7,5},{8,10},{9,11},{10,... | collective-permute-start | bytes 2654216 | tf_op jit(solution)/shard_map/ppermute | solution.py:44
  53.3 2.3 %collective-permute-done.7.refs_1_ = bf16[1728,256]{1,0:T(8,128)(2,1)S(1)} collective-permute-done((bf16[1728,256]{1,0:T(8,128)(2,1)S(1)}, bf16[1728,256]{1,0:T(8,128)(2,1)S(1)}, u32[]{:S(2)}, u32[]{:S(2)}) %collective-permute-start.7) | collective-permute-done | bytes 884768 | tf_op jit(solution)/shard_map/ppermute | solution.py:44
  56.1 2.7 %collective-permute-start.12 = (bf16[1728,256]{1,0:T(8,128)(2,1)S(1)}, bf16[1728,256]{1,0:T(8,128)(2,1)S(1)}, u32[]{:S(2)}, u32[]{:S(2)}) collective-permute-start(bf16[1728,256]{1,0:T(8,128)(2,1)S(1)} %collective-permute-done.5.refs_2_), channel_id=1, source_target_pairs={{0,12},{1,13},{2,14},{3,15},{4,0},{5,1},{6,2},{7,3},{8,4},{9,5},{1... | collective-permute-start | bytes 2654216 | tf_op jit(solution)/shard_map/ppermute | solution.py:44
  59.4 12.5 %collective-permute-done.10.refs_2_ = bf16[1728,256]{1,0:T(8,128)(2,1)S(1)} collective-permute-done((bf16[1728,256]{1,0:T(8,128)(2,1)S(1)}, bf16[1728,256]{1,0:T(8,128)(2,1)S(1)}, u32[]{:S(2)}, u32[]{:S(2)}) %collective-permute-start.10) | collective-permute-done | bytes 884768 | tf_op jit(solution)/shard_map/ppermute | solution.py:44
  72.0 5.9 %collective-permute-done.11.refs_4_ = bf16[1728,256]{1,0:T(8,128)(2,1)S(1)} collective-permute-done((bf16[1728,256]{1,0:T(8,128)(2,1)S(1)}, bf16[1728,256]{1,0:T(8,128)(2,1)S(1)}, u32[]{:S(2)}, u32[]{:S(2)}) %collective-permute-start.11) | collective-permute-done | bytes 884768 | tf_op jit(solution)/shard_map/ppermute | solution.py:44
  81.1 3.1 %early_pass.2.acc = f32[8,256,256]{2,1,0:T(8,128)S(1)} custom-call(bf16[256,1152]{1,0:T(8,128)(2,1)S(1)} %get-tuple-element.133.normed, bf16[1728,256]{1,0:T(8,128)(2,1)S(1)} %copy-done.10, bf16[1728,256]{1,0:T(8,128)(2,1)S(1)} %collective-permute-done.1.refs_1_, bf16[1728,256]{1,0:T(8,128)(2,1)S(1)} %collective-permute-done.5.refs_2_, ...), custom_call_target="tpu_custom_call" | custom-call | flops 1200000000 | bytes 20000000 | tf_op jit(solution)/shard_map/early_pass/pallas_call | solution.py:386
  84.3 1.4 copy-done.2
  90.3 1.7 pad_maximum_fusion
  92.0 4.1 %collective-permute-done.16.refs_3_ = bf16[1728,256]{1,0:T(8,128)(2,1)} collective-permute-done((bf16[1728,256]{1,0:T(8,128)(2,1)S(1)}, bf16[1728,256]{1,0:T(8,128)(2,1)}, u32[]{:S(2)}, u32[]{:S(2)}) %collective-permute-start.16) | collective-permute-done | bytes 884768 | tf_op jit(solution)/shard_map/ppermute | solution.py:44
  96.1 3.4 %collective-permute-done.15.refs_7_ = bf16[1728,256]{1,0:T(8,128)(2,1)S(1)} collective-permute-done((bf16[1728,256]{1,0:T(8,128)(2,1)S(1)}, bf16[1728,256]{1,0:T(8,128)(2,1)S(1)}, u32[]{:S(2)}, u32[]{:S(2)}) %collective-permute-start.15) | collective-permute-done | bytes 884768 | tf_op jit(solution)/shard_map/ppermute | solution.py:44
  100.4 2.8 %collective-permute-start.20 = (bf16[1728,256]{1,0:T(8,128)(2,1)}, bf16[1728,256]{1,0:T(8,128)(2,1)}, u32[]{:S(2)}, u32[]{:S(2)}) collective-permute-start(bf16[1728,256]{1,0:T(8,128)(2,1)} %collective-permute-done.16.refs_3_), channel_id=1, source_target_pairs={{0,2},{1,3},{2,0},{3,1},{4,6},{5,7},{6,4},{7,5},{8,10},{9,11},{10,... | collective-permute-start | bytes 2654216 | tf_op jit(solution)/shard_map/ppermute | solution.py:44
  103.2 2.0 collective-permute-start.22
  107.2 14.1 %own_pass.1 = (bf16[512,256]{1,0:T(8,128)(2,1)}, bf16[512,256]{1,0:T(8,128)(2,1)}, bf16[8,256,256]{2,1,0:T(8,128)(2,1)}, f32[256,2304]{1,0:T(8,128)}, f32[256,256]{1,0:T(8,128)}, /*index=5*/bf16[9,1024,256]{2,1,0:T(8,128)(2,1)}) custom-call(s32[1]{0:T(128)} %bitcast.pos_ref, bf16[256,2304]{1,0:T(8,128)(2,1)} %bitcast.16, f32[2,2304]{1,0:T(2,128)} %gains_ref.5, ...), custom_call_target="tpu_custom_call" | custom-call | flops 3000000000 | bytes 30000000 | tf_op jit(solution)/shard_map/own_pass/pallas_call | solution.py:399
  121.3 2.9 %collective-permute-done.20.refs_8_ = bf16[1728,256]{1,0:T(8,128)(2,1)} collective-permute-done((bf16[1728,256]{1,0:T(8,128)(2,1)}, bf16[1728,256]{1,0:T(8,128)(2,1)}, u32[]{:S(2)}, u32[]{:S(2)}) %collective-permute-start.20) | collective-permute-done | bytes 884768 | tf_op jit(solution)/shard_map/ppermute | solution.py:44
  131.4 4.4 %early_pass.3.acc = f32[8,256,256]{2,1,0:T(8,128)S(1)} custom-call(bf16[256,1152]{1,0:T(8,128)(2,1)S(1)} %copy-done.21, bf16[1728,256]{1,0:T(8,128)(2,1)S(1)} %collective-permute-done.4.refs_0_, bf16[1728,256]{1,0:T(8,128)(2,1)S(1)} %copy-done.4, bf16[1728,256]{1,0:T(8,128)(2,1)S(1)} %copy-done.7, bf16[1728,256]{1,0:T(8,128)(2,1)} %collective-permute-done.16.refs_3_, ...), custom_call_target="tpu_custom_call" | custom-call | flops 1200000000 | bytes 20000000 | tf_op jit(solution)/shard_map/early_pass/pallas_call | solution.py:386
  136.0 1.7 copy-done.22
  137.6 11.3 %peer_pass.1 = (f32[256,1]{1,0:T(8,128)S(1)}, bf16[256,2304]{1,0:T(8,128)(2,1)S(1)}) custom-call(s32[1]{0:T(128)} %bitcast.pos_ref, bf16[256,2304]{1,0:T(8,128)(2,1)S(1)} %bitcast.18, f32[2,2304]{1,0:T(2,128)S(1)} %copy-done.27, bf16[2304,256]{1,0:T(8,128)(2,1)S(1)} %copy-done.9, bf16[256,1152]{1,0:T(8,128)(2,1)S(1)} %copy-done.19, ...), custom_call_target="tpu_custom_call" | custom-call | flops 3000000000 | bytes 30000000 | tf_op jit(solution)/shard_map/peer_pass/pallas_call | solution.py:432
  149.3 5.4 %attention_back.1.d_mine = bf16[8,256,256]{2,1,0:T(8,128)(2,1)S(1)} custom-call(bf16[256,2304]{1,0:T(8,128)(2,1)S(1)} %get-tuple-element.169.dhidden.d_mine, bf16[9,1024,256]{2,1,0:T(8,128)(2,1)S(1)} %bitcast.20, bf16[8,256,256]{2,1,0:T(8,128)(2,1)S(1)} %copy-done.23), custom_call_target="tpu_custom_call" | custom-call | flops 2000000000 | bytes 16000000 | tf_op jit(solution)/shard_map/attention_back/pallas_call | solution.py:452
  155.4 2.9 %out_grads.1 = (bf16[576,256]{1,0:T(8,128)(2,1)S(1)}, bf16[576,256]{1,0:T(8,128)(2,1)S(1)}, bf16[576,256]{1,0:T(8,128)(2,1)S(1)}, bf16[576,256]{1,0:T(8,128)(2,1...) custom-call(bf16[512,256]{1,0:T(8,128)(2,1)S(1)} %copy-done.33, ...), custom_call_target="tpu_custom_call" | custom-call | flops 1207959552 | bytes 10000000 | tf_op jit(solution)/shard_map/out_grads/pallas_call | solution.py:471
  158.3 1.5 collective-permute-start.33
  160.2 1.7 collective-permute-start.35
  161.8 4.7 %qkv_grads.1 = (bf16[1152,256]{1,0:T(8,128)(2,1)S(1)}, bf16[1152,256]{1,0:T(8,128)(2,1)S(1)}, bf16[1152,256]{1,0:T(8,128)(2,1)S(1)}, bf16[1152,256]{1,0:T(8,128)...) custom-call(bf16[1152,256]{1,0:T(8,128)(2,1)S(1)} %copy-done.30, ...), custom_call_target="tpu_custom_call" | custom-call | flops 2415919104 | bytes 10000000 | tf_op jit(solution)/shard_map/qkv_grads/pallas_call | solution.py:471
  166.5 2.2 collective-permute-start.36
  168.7 1.6 collective-permute-start.37
  170.7 3.6 %collective-permute-done.36.in_a = bf16[384,256]{1,0:T(8,128)(2,1)S(1)} collective-permute-done((bf16[384,256]{1,0:T(8,128)(2,1)S(1)}, bf16[384,256]{1,0:T(8,128)(2,1)S(1)}, u32[]{:S(2)}, u32[]{:S(2)}) %collective-permute-start.36) | collective-permute-done | bytes 196640 | tf_op jit(solution)/shard_map/ppermute | solution.py:44
  174.6 2.6 %collective-permute-done.38.in_c = bf16[384,256]{1,0:T(8,128)(2,1)S(1)} collective-permute-done((bf16[384,256]{1,0:T(8,128)(2,1)S(1)}, bf16[384,256]{1,0:T(8,128)(2,1)S(1)}, u32[]{:S(2)}, u32[]{:S(2)}) %collective-permute-start.38) | collective-permute-done | bytes 196640 | tf_op jit(solution)/shard_map/ppermute | solution.py:44
  177.4 3.2 %collective-permute-start.40 = (bf16[1152,256]{1,0:T(8,128)(2,1)S(1)}, bf16[1152,256]{1,0:T(8,128)(2,1)S(1)}, u32[]{:S(2)}, u32[]{:S(2)}) collective-permute-start(bf16[1152,256]{1,0:T(8,128)(2,1)S(1)} %get-tuple-element.214), channel_id=1, source_target_pairs={{0,12},{1,13},{2,14},{3,15},{4,0},{5,1},{6,2},{7,3},{8,4},{9,5},{1... | collective-permute-start | bytes 1769480 | tf_op jit(solution)/shard_map/ppermute | solution.py:44
  180.6 1.4 collective-permute-start.41
  182.2 3.2 %collective-permute-start.46 = (bf16[576,256]{1,0:T(8,128)(2,1)S(1)}, bf16[576,256]{1,0:T(8,128)(2,1)S(1)}, u32[]{:S(2)}, u32[]{:S(2)}) collective-permute-start(bf16[576,256]{1,0:T(8,128)(2,1)S(1)} %get-tuple-element.238), channel_id=1, source_target_pairs={{0,12},{1,13},{2,14},{3,15},{4,0},{5,1},{6,2},{7,3},{8,4},{9,5},{1... | collective-permute-start | bytes 884744 | tf_op jit(solution)/shard_map/ppermute | solution.py:44
  185.4 9.2 %collective-permute-done.39.in_x = bf16[1152,256]{1,0:T(8,128)(2,1)S(1)} collective-permute-done((bf16[1152,256]{1,0:T(8,128)(2,1)S(1)}, bf16[1152,256]{1,0:T(8,128)(2,1)S(1)}, u32[]{:S(2)}, u32[]{:S(2)}) %collective-permute-start.39) | collective-permute-done | bytes 589856 | tf_op jit(solution)/shard_map/ppermute | solution.py:44
  194.7 1.6 collective-permute-start.47
  196.2 1.9 collective-permute-start.49
  199.4 2.0 collective-permute-start.42
  201.4 1.4 collective-permute-start.44
  202.8 3.2 %collective-permute-done.47.in_y = bf16[576,256]{1,0:T(8,128)(2,1)S(1)} collective-permute-done((bf16[576,256]{1,0:T(8,128)(2,1)S(1)}, bf16[576,256]{1,0:T(8,128)(2,1)S(1)}, u32[]{:S(2)}, u32[]{:S(2)}) %collective-permute-start.47) | collective-permute-done | bytes 294944 | tf_op jit(solution)/shard_map/ppermute | solution.py:44
  207.0 1.5 collective-permute-start.50
  208.5 1.6 reduce
  210.1 7.4 %collective-permute-done.48.refs_1_ = bf16[576,256]{1,0:T(8,128)(2,1)S(1)} collective-permute-done((bf16[576,256]{1,0:T(8,128)(2,1)}, bf16[576,256]{1,0:T(8,128)(2,1)S(1)}, u32[]{:S(2)}, u32[]{:S(2)}) %collective-permute-start.48) | collective-permute-done | bytes 294944 | tf_op jit(solution)/shard_map/ppermute | solution.py:44
  217.5 3.5 %collective-permute-done.50.refs_3_ = bf16[576,256]{1,0:T(8,128)(2,1)S(1)} collective-permute-done((bf16[576,256]{1,0:T(8,128)(2,1)}, bf16[576,256]{1,0:T(8,128)(2,1)S(1)}, u32[]{:S(2)}, u32[]{:S(2)}) %collective-permute-start.50) | collective-permute-done | bytes 294944 | tf_op jit(solution)/shard_map/ppermute | solution.py:44
  (163 shorter events, 32.3 us)
Async XLA Ops:
  3.4 22.1 %collective-permute-start = (bf16[1728,256]{1,0:T(8,128)(2,1)}, bf16[1728,256]{1,0:T(8,128)(2,1)S(1)}, u32[]{:S(2)}, u32[]{:S(2)}) collective-permute-start(bf16[1728,256]{1,0:T(8,128)(2,1)} %get-tuple-element.135.refs_0_), channel_id=1, source_target_pairs={{0,12},{1,13},{2,14},{3,15},{4,0},{5,1},{6,2},{7,3},{8,4},{9,5},{1... | collective-permute-start | bytes 2654216 | tf_op jit(solution)/shard_map/ppermute | solution.py:44
  6.2 22.5 %collective-permute-start.1 = (bf16[1728,256]{1,0:T(8,128)(2,1)}, bf16[1728,256]{1,0:T(8,128)(2,1)S(1)}, u32[]{:S(2)}, u32[]{:S(2)}) collective-permute-start(bf16[1728,256]{1,0:T(8,128)(2,1)} %get-tuple-element.135.refs_0_), channel_id=1, source_target_pairs={{0,4},{1,5},{2,6},{3,7},{4,8},{5,9},{6,10},{7,11},{8,12},{9,13},{1... | collective-permute-start | bytes 2654216 | tf_op jit(solution)/shard_map/ppermute | solution.py:44
  6.2 22.5 %collective-permute-start.2 = (bf16[1728,256]{1,0:T(8,128)(2,1)}, bf16[1728,256]{1,0:T(8,128)(2,1)S(1)}, u32[]{:S(2)}, u32[]{:S(2)}) collective-permute-start(bf16[1728,256]{1,0:T(8,128)(2,1)} %get-tuple-element.135.refs_0_), channel_id=1, source_target_pairs={{0,1},{1,0},{2,3},{3,2},{4,5},{5,4},{6,7},{7,6},{8,9},{9,8},{10,11... | collective-permute-start | bytes 2654216 | tf_op jit(solution)/shard_map/ppermute | solution.py:44
  6.2 26.3 %collective-permute-start.4 = (bf16[1728,256]{1,0:T(8,128)(2,1)}, bf16[1728,256]{1,0:T(8,128)(2,1)S(1)}, u32[]{:S(2)}, u32[]{:S(2)}) collective-permute-start(bf16[1728,256]{1,0:T(8,128)(2,1)} %get-tuple-element.134), channel_id=1, source_target_pairs={{0,16},{16,32},{32,48},{48,64},{64,80},{80,96},{96,112},{112,0},{1... | collective-permute-start | bytes 2654216 | tf_op jit(solution)/shard_map/ppermute | solution.py:576
  28.8 20.3 %collective-permute-start.6 = (bf16[1728,256]{1,0:T(8,128)(2,1)S(1)}, bf16[1728,256]{1,0:T(8,128)(2,1)S(1)}, u32[]{:S(2)}, u32[]{:S(2)}) collective-permute-start(bf16[1728,256]{1,0:T(8,128)(2,1)S(1)} %collective-permute-done.refs_3_), channel_id=1, source_target_pairs={{0,12},{1,13},{2,14},{3,15},{4,0},{5,1},{6,2},{7,3},{8,4},{9,5},{1... | collective-permute-start | bytes 2654216 | tf_op jit(solution)/shard_map/ppermute | solution.py:44
  29.1 23.1 %collective-permute-start.8 = (bf16[1728,256]{1,0:T(8,128)(2,1)S(1)}, bf16[1728,256]{1,0:T(8,128)(2,1)S(1)}, u32[]{:S(2)}, u32[]{:S(2)}) collective-permute-start(bf16[1728,256]{1,0:T(8,128)(2,1)S(1)} %collective-permute-done.refs_3_), channel_id=1, source_target_pairs={{0,1},{1,0},{2,3},{3,2},{4,5},{5,4},{6,7},{7,6},{8,9},{9,8},{10,11... | collective-permute-start | bytes 2654216 | tf_op jit(solution)/shard_map/ppermute | solution.py:44
  29.1 24.2 %collective-permute-start.5 = (bf16[1728,256]{1,0:T(8,128)(2,1)}, bf16[1728,256]{1,0:T(8,128)(2,1)S(1)}, u32[]{:S(2)}, u32[]{:S(2)}) collective-permute-start(bf16[1728,256]{1,0:T(8,128)(2,1)} %get-tuple-element.135.refs_0_), channel_id=1, source_target_pairs={{0,2},{1,3},{2,0},{3,1},{4,6},{5,7},{6,4},{7,5},{8,10},{9,11},{10,... | collective-permute-start | bytes 2654216 | tf_op jit(solution)/shard_map/ppermute | solution.py:44
  32.3 21.0 %collective-permute-start.9 = (bf16[1728,256]{1,0:T(8,128)(2,1)S(1)}, bf16[1728,256]{1,0:T(8,128)(2,1)S(1)}, u32[]{:S(2)}, u32[]{:S(2)}) collective-permute-start(bf16[1728,256]{1,0:T(8,128)(2,1)S(1)} %collective-permute-done.1.refs_1_), channel_id=1, source_target_pairs={{0,1},{1,0},{2,3},{3,2},{4,5},{5,4},{6,7},{7,6},{8,9},{9,8},{10,11... | collective-permute-start | bytes 2654216 | tf_op jit(solution)/shard_map/ppermute | solution.py:44
  32.6 23.0 %collective-permute-start.7 = (bf16[1728,256]{1,0:T(8,128)(2,1)S(1)}, bf16[1728,256]{1,0:T(8,128)(2,1)S(1)}, u32[]{:S(2)}, u32[]{:S(2)}) collective-permute-start(bf16[1728,256]{1,0:T(8,128)(2,1)S(1)} %collective-permute-done.4.refs_0_), channel_id=1, source_target_pairs={{0,4},{1,5},{2,6},{3,7},{4,8},{5,9},{6,10},{7,11},{8,12},{9,13},{1... | collective-permute-start | bytes 2654216 | tf_op jit(solution)/shard_map/ppermute | solution.py:44
  49.0 22.8 %collective-permute-start.10 = (bf16[1728,256]{1,0:T(8,128)(2,1)S(1)}, bf16[1728,256]{1,0:T(8,128)(2,1)S(1)}, u32[]{:S(2)}, u32[]{:S(2)}) collective-permute-start(bf16[1728,256]{1,0:T(8,128)(2,1)S(1)} %collective-permute-done.4.refs_0_), channel_id=1, source_target_pairs={{0,2},{1,3},{2,0},{3,1},{4,6},{5,7},{6,4},{7,5},{8,10},{9,11},{10,... | collective-permute-start | bytes 2654216 | tf_op jit(solution)/shard_map/ppermute | solution.py:44
  55.6 22.2 %collective-permute-start.11 = (bf16[1728,256]{1,0:T(8,128)(2,1)S(1)}, bf16[1728,256]{1,0:T(8,128)(2,1)S(1)}, u32[]{:S(2)}, u32[]{:S(2)}) collective-permute-start(bf16[1728,256]{1,0:T(8,128)(2,1)S(1)} %collective-permute-done.5.refs_2_), channel_id=1, source_target_pairs={{0,4},{1,5},{2,6},{3,7},{4,8},{5,9},{6,10},{7,11},{8,12},{9,13},{1... | collective-permute-start | bytes 2654216 | tf_op jit(solution)/shard_map/ppermute | solution.py:44
  56.1 22.8 %collective-permute-start.12 = (bf16[1728,256]{1,0:T(8,128)(2,1)S(1)}, bf16[1728,256]{1,0:T(8,128)(2,1)S(1)}, u32[]{:S(2)}, u32[]{:S(2)}) collective-permute-start(bf16[1728,256]{1,0:T(8,128)(2,1)S(1)} %collective-permute-done.5.refs_2_), channel_id=1, source_target_pairs={{0,12},{1,13},{2,14},{3,15},{4,0},{5,1},{6,2},{7,3},{8,4},{9,5},{1... | collective-permute-start | bytes 2654216 | tf_op jit(solution)/shard_map/ppermute | solution.py:44
  58.9 20.1 %collective-permute-start.13 = (bf16[1728,256]{1,0:T(8,128)(2,1)S(1)}, bf16[1728,256]{1,0:T(8,128)(2,1)S(1)}, u32[]{:S(2)}, u32[]{:S(2)}) collective-permute-start(bf16[1728,256]{1,0:T(8,128)(2,1)S(1)} %collective-permute-done.5.refs_2_), channel_id=1, source_target_pairs={{0,1},{1,0},{2,3},{3,2},{4,5},{5,4},{6,7},{7,6},{8,9},{9,8},{10,11... | collective-permute-start | bytes 2654216 | tf_op jit(solution)/shard_map/ppermute | solution.py:44
  58.9 20.1 %collective-permute-start.14 = (bf16[1728,256]{1,0:T(8,128)(2,1)S(1)}, bf16[1728,256]{1,0:T(8,128)(2,1)S(1)}, u32[]{:S(2)}, u32[]{:S(2)}) collective-permute-start(bf16[1728,256]{1,0:T(8,128)(2,1)S(1)} %collective-permute-done.6.refs_5_), channel_id=1, source_target_pairs={{0,1},{1,0},{2,3},{3,2},{4,5},{5,4},{6,7},{7,6},{8,9},{9,8},{10,11... | collective-permute-start | bytes 2654216 | tf_op jit(solution)/shard_map/ppermute | solution.py:44
  71.9 24.2 %collective-permute-start.16 = (bf16[1728,256]{1,0:T(8,128)(2,1)S(1)}, bf16[1728,256]{1,0:T(8,128)(2,1)}, u32[]{:S(2)}, u32[]{:S(2)}) collective-permute-start(bf16[1728,256]{1,0:T(8,128)(2,1)S(1)} %collective-permute-done.4.refs_0_), channel_id=1, source_target_pairs={{0,12},{1,13},{2,14},{3,15},{4,0},{5,1},{6,2},{7,3},{8,4},{9,5},{1... | collective-permute-start | bytes 2654216 | tf_op jit(solution)/shard_map/ppermute | solution.py:44
  77.8 21.6 %collective-permute-start.15 = (bf16[1728,256]{1,0:T(8,128)(2,1)S(1)}, bf16[1728,256]{1,0:T(8,128)(2,1)S(1)}, u32[]{:S(2)}, u32[]{:S(2)}) collective-permute-start(bf16[1728,256]{1,0:T(8,128)(2,1)S(1)} %collective-permute-done.6.refs_5_), channel_id=1, source_target_pairs={{0,2},{1,3},{2,0},{3,1},{4,6},{5,7},{6,4},{7,5},{8,10},{9,11},{10,... | collective-permute-start | bytes 2654216 | tf_op jit(solution)/shard_map/ppermute | solution.py:44
  79.0 20.8 %collective-permute-start.17 = (bf16[1728,256]{1,0:T(8,128)(2,1)S(1)}, bf16[1728,256]{1,0:T(8,128)(2,1)}, u32[]{:S(2)}, u32[]{:S(2)}) collective-permute-start(bf16[1728,256]{1,0:T(8,128)(2,1)S(1)} %collective-permute-done.10.refs_2_), channel_id=1, source_target_pairs={{0,4},{1,5},{2,6},{3,7},{4,8},{5,9},{6,10},{7,11},{8,12},{9,13},{1... | collective-permute-start | bytes 2654216 | tf_op jit(solution)/shard_map/ppermute | solution.py:44
  79.3 20.5 %collective-permute-start.18 = (bf16[1728,256]{1,0:T(8,128)(2,1)S(1)}, bf16[1728,256]{1,0:T(8,128)(2,1)S(1)}, u32[]{:S(2)}, u32[]{:S(2)}) collective-permute-start(bf16[1728,256]{1,0:T(8,128)(2,1)S(1)} %collective-permute-done.11.refs_4_), channel_id=1, source_target_pairs={{0,1},{1,0},{2,3},{3,2},{4,5},{5,4},{6,7},{7,6},{8,9},{9,8},{10,11... | collective-permute-start | bytes 2654216 | tf_op jit(solution)/shard_map/ppermute | solution.py:44
  79.9 19.9 %collective-permute-start.19 = (bf16[1728,256]{1,0:T(8,128)(2,1)S(1)}, bf16[1728,256]{1,0:T(8,128)(2,1)S(1)}, u32[]{:S(2)}, u32[]{:S(2)}) collective-permute-start(bf16[1728,256]{1,0:T(8,128)(2,1)S(1)} %collective-permute-done.12.refs_6_), channel_id=1, source_target_pairs={{0,1},{1,0},{2,3},{3,2},{4,5},{5,4},{6,7},{7,6},{8,9},{9,8},{10,11... | collective-permute-start | bytes 2654216 | tf_op jit(solution)/shard_map/ppermute | solution.py:44
  99.8 26.3 %collective-permute-start.23 = (bf16[5184,256]{1,0:T(8,128)(2,1)}, bf16[5184,256]{1,0:T(8,128)(2,1)S(1)}, u32[]{:S(2)}, u32[]{:S(2)}) collective-permute-start(bf16[5184,256]{1,0:T(8,128)(2,1)} %pad_maximum_fusion), channel_id=1, source_target_pairs={{0,1},{1,0},{2,3},{3,2},{4,5},{5,4},{6,7},{7,6},{8,9},{9,8},{10,11... | collective-permute-start | bytes 7962632 | tf_op jit(solution)/shard_map/ppermute | solution.py:44
  100.4 23.9 %collective-permute-start.20 = (bf16[1728,256]{1,0:T(8,128)(2,1)}, bf16[1728,256]{1,0:T(8,128)(2,1)}, u32[]{:S(2)}, u32[]{:S(2)}) collective-permute-start(bf16[1728,256]{1,0:T(8,128)(2,1)} %collective-permute-done.16.refs_3_), channel_id=1, source_target_pairs={{0,2},{1,3},{2,0},{3,1},{4,6},{5,7},{6,4},{7,5},{8,10},{9,11},{10,... | collective-permute-start | bytes 2654216 | tf_op jit(solution)/shard_map/ppermute | solution.py:44
  103.2 21.7 %collective-permute-start.21 = (bf16[1728,256]{1,0:T(8,128)(2,1)}, bf16[1728,256]{1,0:T(8,128)(2,1)}, u32[]{:S(2)}, u32[]{:S(2)}) collective-permute-start(bf16[1728,256]{1,0:T(8,128)(2,1)} %collective-permute-done.16.refs_3_), channel_id=1, source_target_pairs={{0,12},{1,13},{2,14},{3,15},{4,0},{5,1},{6,2},{7,3},{8,4},{9,5},{1... | collective-permute-start | bytes 2654216 | tf_op jit(solution)/shard_map/ppermute | solution.py:44
  103.2 22.9 %collective-permute-start.22 = (bf16[1728,256]{1,0:T(8,128)(2,1)}, bf16[1728,256]{1,0:T(8,128)(2,1)}, u32[]{:S(2)}, u32[]{:S(2)}) collective-permute-start(bf16[1728,256]{1,0:T(8,128)(2,1)} %collective-permute-done.17.refs_6_), channel_id=1, source_target_pairs={{0,4},{1,5},{2,6},{3,7},{4,8},{5,9},{6,10},{7,11},{8,12},{9,13},{1... | collective-permute-start | bytes 2654216 | tf_op jit(solution)/shard_map/ppermute | solution.py:44
  107.1 19.1 %collective-permute-start.24 = (bf16[1728,256]{1,0:T(8,128)(2,1)}, bf16[1728,256]{1,0:T(8,128)(2,1)}, u32[]{:S(2)}, u32[]{:S(2)}) collective-permute-start(bf16[1728,256]{1,0:T(8,128)(2,1)} %collective-permute-done.16.refs_3_), channel_id=1, source_target_pairs={{0,1},{1,0},{2,3},{3,2},{4,5},{5,4},{6,7},{7,6},{8,9},{9,8},{10,11... | collective-permute-start | bytes 2654216 | tf_op jit(solution)/shard_map/ppermute | solution.py:44
  124.3 11.6 %collective-permute-start.26 = (bf16[1728,256]{1,0:T(8,128)(2,1)}, bf16[1728,256]{1,0:T(8,128)(2,1)}, u32[]{:S(2)}, u32[]{:S(2)}) collective-permute-start(bf16[1728,256]{1,0:T(8,128)(2,1)} %collective-permute-done.17.refs_6_), channel_id=1, source_target_pairs={{0,1},{1,0},{2,3},{3,2},{4,5},{5,4},{6,7},{7,6},{8,9},{9,8},{10,11... | collective-permute-start | bytes 2654216 | tf_op jit(solution)/shard_map/ppermute | solution.py:44
  126.1 9.7 %collective-permute-start.27 = (bf16[1728,256]{1,0:T(8,128)(2,1)}, bf16[1728,256]{1,0:T(8,128)(2,1)}, u32[]{:S(2)}, u32[]{:S(2)}) collective-permute-start(bf16[1728,256]{1,0:T(8,128)(2,1)} %collective-permute-done.21.refs_7_), channel_id=1, source_target_pairs={{0,1},{1,0},{2,3},{3,2},{4,5},{5,4},{6,7},{7,6},{8,9},{9,8},{10,11... | collective-permute-start | bytes 2654216 | tf_op jit(solution)/shard_map/ppermute | solution.py:44
  126.2 9.7 %collective-permute-start.28 = (bf16[1728,256]{1,0:T(8,128)(2,1)}, bf16[1728,256]{1,0:T(8,128)(2,1)}, u32[]{:S(2)}, u32[]{:S(2)}) collective-permute-start(bf16[1728,256]{1,0:T(8,128)(2,1)} %collective-permute-done.20.refs_8_), channel_id=1, source_target_pairs={{0,1},{1,0},{2,3},{3,2},{4,5},{5,4},{6,7},{7,6},{8,9},{9,8},{10,11... | collective-permute-start | bytes 2654216 | tf_op jit(solution)/shard_map/ppermute | solution.py:44
  126.7 9.2 %collective-permute-start.29 = (bf16[1728,256]{1,0:T(8,128)(2,1)}, bf16[1728,256]{1,0:T(8,128)(2,1)}, u32[]{:S(2)}, u32[]{:S(2)}) collective-permute-start(bf16[1728,256]{1,0:T(8,128)(2,1)} %collective-permute-done.22.refs_9_), channel_id=1, source_target_pairs={{0,1},{1,0},{2,3},{3,2},{4,5},{5,4},{6,7},{7,6},{8,9},{9,8},{10,11... | collective-permute-start | bytes 2654216 | tf_op jit(solution)/shard_map/ppermute | solution.py:44
  127.5 21.4 %collective-permute-start.30 = (bf16[512,256]{1,0:T(8,128)(2,1)}, bf16[512,256]{1,0:T(8,128)(2,1)S(1)}, u32[]{:S(2)}, u32[]{:S(2)}) collective-permute-start(bf16[512,256]{1,0:T(8,128)(2,1)} %get-tuple-element.168), channel_id=1, source_target_pairs={{0,1},{1,0},{2,3},{3,2},{4,5},{5,4},{6,7},{7,6},{8,9},{9,8},{10,11... | collective-permute-start | bytes 786440 | tf_op jit(solution)/shard_map/ppermute | solution.py:44
  149.0 6.4 %collective-permute-start.32 = (bf16[256,2304]{1,0:T(8,128)(2,1)S(1)}, bf16[256,2304]{1,0:T(8,128)(2,1)S(1)}, u32[]{:S(2)}, u32[]{:S(2)}) collective-permute-start(bf16[256,2304]{1,0:T(8,128)(2,1)S(1)} %get-tuple-element.169.dhidden.d_mine), channel_id=1, source_target_pairs={{0,1},{1,0},{2,3},{3,2},{4,5},{5,4},{6,7},{7,6},{8,9},{9,8},{10,11... | collective-permute-start | bytes 3538952 | tf_op jit(solution)/shard_map/ppermute | solution.py:44
  158.3 8.2 %collective-permute-start.33 = (bf16[192,256]{1,0:T(8,128)(2,1)S(1)}, bf16[192,256]{1,0:T(8,128)(2,1)S(1)}, u32[]{:S(2)}, u32[]{:S(2)}) collective-permute-start(bf16[192,256]{1,0:T(8,128)(2,1)S(1)} %get-tuple-element.184), channel_id=1, source_target_pairs={{0,2},{1,3},{2,0},{3,1},{4,6},{5,7},{6,4},{7,5},{8,10},{9,11},{10,... | collective-permute-start | bytes 294920 | tf_op jit(solution)/shard_map/ppermute | solution.py:44
  159.8 6.7 %collective-permute-start.34 = (bf16[192,256]{1,0:T(8,128)(2,1)S(1)}, bf16[192,256]{1,0:T(8,128)(2,1)S(1)}, u32[]{:S(2)}, u32[]{:S(2)}) collective-permute-start(bf16[192,256]{1,0:T(8,128)(2,1)S(1)} %get-tuple-element.185), channel_id=1, source_target_pairs={{0,12},{1,13},{2,14},{3,15},{4,0},{5,1},{6,2},{7,3},{8,4},{9,5},{1... | collective-permute-start | bytes 294920 | tf_op jit(solution)/shard_map/ppermute | solution.py:44
  160.2 6.3 %collective-permute-start.35 = (bf16[192,256]{1,0:T(8,128)(2,1)S(1)}, bf16[192,256]{1,0:T(8,128)(2,1)S(1)}, u32[]{:S(2)}, u32[]{:S(2)}) collective-permute-start(bf16[192,256]{1,0:T(8,128)(2,1)S(1)} %get-tuple-element.186), channel_id=1, source_target_pairs={{0,4},{1,5},{2,6},{3,7},{4,8},{5,9},{6,10},{7,11},{8,12},{9,13},{1... | collective-permute-start | bytes 294920 | tf_op jit(solution)/shard_map/ppermute | solution.py:44
  166.5 7.7 %collective-permute-start.36 = (bf16[384,256]{1,0:T(8,128)(2,1)S(1)}, bf16[384,256]{1,0:T(8,128)(2,1)S(1)}, u32[]{:S(2)}, u32[]{:S(2)}) collective-permute-start(bf16[384,256]{1,0:T(8,128)(2,1)S(1)} %get-tuple-element.207), channel_id=1, source_target_pairs={{0,2},{1,3},{2,0},{3,1},{4,6},{5,7},{6,4},{7,5},{8,10},{9,11},{10,... | collective-permute-start | bytes 589832 | tf_op jit(solution)/shard_map/ppermute | solution.py:44
  168.7 5.9 %collective-permute-start.37 = (bf16[384,256]{1,0:T(8,128)(2,1)S(1)}, bf16[384,256]{1,0:T(8,128)(2,1)S(1)}, u32[]{:S(2)}, u32[]{:S(2)}) collective-permute-start(bf16[384,256]{1,0:T(8,128)(2,1)S(1)} %get-tuple-element.208), channel_id=1, source_target_pairs={{0,12},{1,13},{2,14},{3,15},{4,0},{5,1},{6,2},{7,3},{8,4},{9,5},{1... | collective-permute-start | bytes 589832 | tf_op jit(solution)/shard_map/ppermute | solution.py:44
  170.3 6.9 %collective-permute-start.38 = (bf16[384,256]{1,0:T(8,128)(2,1)S(1)}, bf16[384,256]{1,0:T(8,128)(2,1)S(1)}, u32[]{:S(2)}, u32[]{:S(2)}) collective-permute-start(bf16[384,256]{1,0:T(8,128)(2,1)S(1)} %get-tuple-element.209), channel_id=1, source_target_pairs={{0,4},{1,5},{2,6},{3,7},{4,8},{5,9},{6,10},{7,11},{8,12},{9,13},{1... | collective-permute-start | bytes 589832 | tf_op jit(solution)/shard_map/ppermute | solution.py:44
  177.3 17.3 %collective-permute-start.39 = (bf16[1152,256]{1,0:T(8,128)(2,1)S(1)}, bf16[1152,256]{1,0:T(8,128)(2,1)S(1)}, u32[]{:S(2)}, u32[]{:S(2)}) collective-permute-start(bf16[1152,256]{1,0:T(8,128)(2,1)S(1)} %get-tuple-element.213), channel_id=1, source_target_pairs={{0,4},{1,5},{2,6},{3,7},{4,8},{5,9},{6,10},{7,11},{8,12},{9,13},{1... | collective-permute-start | bytes 1769480 | tf_op jit(solution)/shard_map/ppermute | solution.py:44
  177.4 18.8 %collective-permute-start.40 = (bf16[1152,256]{1,0:T(8,128)(2,1)S(1)}, bf16[1152,256]{1,0:T(8,128)(2,1)S(1)}, u32[]{:S(2)}, u32[]{:S(2)}) collective-permute-start(bf16[1152,256]{1,0:T(8,128)(2,1)S(1)} %get-tuple-element.214), channel_id=1, source_target_pairs={{0,12},{1,13},{2,14},{3,15},{4,0},{5,1},{6,2},{7,3},{8,4},{9,5},{1... | collective-permute-start | bytes 1769480 | tf_op jit(solution)/shard_map/ppermute | solution.py:44
  180.6 17.5 %collective-permute-start.41 = (bf16[1152,256]{1,0:T(8,128)(2,1)S(1)}, bf16[1152,256]{1,0:T(8,128)(2,1)S(1)}, u32[]{:S(2)}, u32[]{:S(2)}) collective-permute-start(bf16[1152,256]{1,0:T(8,128)(2,1)S(1)} %get-tuple-element.215), channel_id=1, source_target_pairs={{0,2},{1,3},{2,0},{3,1},{4,6},{5,7},{6,4},{7,5},{8,10},{9,11},{10,... | collective-permute-start | bytes 1769480 | tf_op jit(solution)/shard_map/ppermute | solution.py:44
  182.1 17.2 %collective-permute-start.45 = (bf16[576,256]{1,0:T(8,128)(2,1)S(1)}, bf16[576,256]{1,0:T(8,128)(2,1)S(1)}, u32[]{:S(2)}, u32[]{:S(2)}) collective-permute-start(bf16[576,256]{1,0:T(8,128)(2,1)S(1)} %get-tuple-element.237), channel_id=1, source_target_pairs={{0,4},{1,5},{2,6},{3,7},{4,8},{5,9},{6,10},{7,11},{8,12},{9,13},{1... | collective-permute-start | bytes 884744 | tf_op jit(solution)/shard_map/ppermute | solution.py:44
  182.2 19.2 %collective-permute-start.46 = (bf16[576,256]{1,0:T(8,128)(2,1)S(1)}, bf16[576,256]{1,0:T(8,128)(2,1)S(1)}, u32[]{:S(2)}, u32[]{:S(2)}) collective-permute-start(bf16[576,256]{1,0:T(8,128)(2,1)S(1)} %get-tuple-element.238), channel_id=1, source_target_pairs={{0,12},{1,13},{2,14},{3,15},{4,0},{5,1},{6,2},{7,3},{8,4},{9,5},{1... | collective-permute-start | bytes 884744 | tf_op jit(solution)/shard_map/ppermute | solution.py:44
  194.7 11.4 %collective-permute-start.47 = (bf16[576,256]{1,0:T(8,128)(2,1)S(1)}, bf16[576,256]{1,0:T(8,128)(2,1)S(1)}, u32[]{:S(2)}, u32[]{:S(2)}) collective-permute-start(bf16[576,256]{1,0:T(8,128)(2,1)S(1)} %get-tuple-element.239), channel_id=1, source_target_pairs={{0,2},{1,3},{2,0},{3,1},{4,6},{5,7},{6,4},{7,5},{8,10},{9,11},{10,... | collective-permute-start | bytes 884744 | tf_op jit(solution)/shard_map/ppermute | solution.py:44
  196.2 10.8 %collective-permute-start.49 = (bf16[576,256]{1,0:T(8,128)(2,1)S(1)}, bf16[576,256]{1,0:T(8,128)(2,1)S(1)}, u32[]{:S(2)}, u32[]{:S(2)}) collective-permute-start(bf16[576,256]{1,0:T(8,128)(2,1)S(1)} %get-tuple-element.244), channel_id=1, source_target_pairs={{0,12},{1,13},{2,14},{3,15},{4,0},{5,1},{6,2},{7,3},{8,4},{9,5},{1... | collective-permute-start | bytes 884744 | tf_op jit(solution)/shard_map/ppermute | solution.py:44
  198.1 23.8 %collective-permute-start.43 = (bf16[1152,256]{1,0:T(8,128)(2,1)}, bf16[1152,256]{1,0:T(8,128)(2,1)S(1)}, u32[]{:S(2)}, u32[]{:S(2)}) collective-permute-start(bf16[1152,256]{1,0:T(8,128)(2,1)} %get-tuple-element.220), channel_id=1, source_target_pairs={{0,12},{1,13},{2,14},{3,15},{4,0},{5,1},{6,2},{7,3},{8,4},{9,5},{1... | collective-permute-start | bytes 1769480 | tf_op jit(solution)/shard_map/ppermute | solution.py:44
  199.4 22.6 %collective-permute-start.42 = (bf16[1152,256]{1,0:T(8,128)(2,1)}, bf16[1152,256]{1,0:T(8,128)(2,1)S(1)}, u32[]{:S(2)}, u32[]{:S(2)}) collective-permute-start(bf16[1152,256]{1,0:T(8,128)(2,1)} %get-tuple-element.219), channel_id=1, source_target_pairs={{0,4},{1,5},{2,6},{3,7},{4,8},{5,9},{6,10},{7,11},{8,12},{9,13},{1... | collective-permute-start | bytes 1769480 | tf_op jit(solution)/shard_map/ppermute | solution.py:44
  201.4 20.6 %collective-permute-start.44 = (bf16[1152,256]{1,0:T(8,128)(2,1)}, bf16[1152,256]{1,0:T(8,128)(2,1)S(1)}, u32[]{:S(2)}, u32[]{:S(2)}) collective-permute-start(bf16[1152,256]{1,0:T(8,128)(2,1)} %get-tuple-element.221), channel_id=1, source_target_pairs={{0,2},{1,3},{2,0},{3,1},{4,6},{5,7},{6,4},{7,5},{8,10},{9,11},{10,... | collective-permute-start | bytes 1769480 | tf_op jit(solution)/shard_map/ppermute | solution.py:44
  206.9 10.6 %collective-permute-start.48 = (bf16[576,256]{1,0:T(8,128)(2,1)}, bf16[576,256]{1,0:T(8,128)(2,1)S(1)}, u32[]{:S(2)}, u32[]{:S(2)}) collective-permute-start(bf16[576,256]{1,0:T(8,128)(2,1)} %get-tuple-element.243), channel_id=1, source_target_pairs={{0,4},{1,5},{2,6},{3,7},{4,8},{5,9},{6,10},{7,11},{8,12},{9,13},{1... | collective-permute-start | bytes 884744 | tf_op jit(solution)/shard_map/ppermute | solution.py:44
  207.0 13.9 %collective-permute-start.50 = (bf16[576,256]{1,0:T(8,128)(2,1)}, bf16[576,256]{1,0:T(8,128)(2,1)S(1)}, u32[]{:S(2)}, u32[]{:S(2)}) collective-permute-start(bf16[576,256]{1,0:T(8,128)(2,1)} %get-tuple-element.245), channel_id=1, source_target_pairs={{0,2},{1,3},{2,0},{3,1},{4,6},{5,7},{6,4},{7,5},{8,10},{9,11},{10,... | collective-permute-start | bytes 884744 | tf_op jit(solution)/shard_map/ppermute | solution.py:44
  (48 other events, 443.0 us)

commit v5 on v4

--- a/solution.py
+++ b/solution.py
@@ -186,15 +186,24 @@
 
 
 def early_kernel(slots, normed, *refs):
-    pieces, (acc, wqkv, sem) = refs[:-3], refs[-3:]
-    load_qkv(slots, pieces, wqkv, sem)
-    wait_for(wqkv, sem)
+    pieces, (acc, wqkv, sems) = refs[:-3], refs[-3:]
+    half = QKV_PANELS // 2
+    for part in range(2):
+        panels = pl.ds(half * part, half)
+        for slot, sources in enumerate(slots):
+            for dc, (piece, row) in enumerate(sources):
+                rows = pl.ds(row + THIRD * part, THIRD)
+                to = pl.ds(SLOT_ROWS * slot + QKV_ROWS * dc, QKV_ROWS)
+                source = pieces[piece].at[rows].reshape(half, QKV_ROWS, HEAD)
+                pltpu.make_async_copy(source, wqkv.at[panels, to], sems.at[part]).start()
 
     def one_panel(p, carry):
         acc[p] = nn(normed[...], wqkv[p])
         return carry
 
-    lax.fori_loop(0, QKV_PANELS, one_panel, 0)
+    for part in range(2):
+        wait_for(wqkv.at[pl.ds(half * part, half)], sems.at[part])
+        lax.fori_loop(half * part, half * (part + 1), one_panel, 0)
 
 
 def layer(position, early, slots, x_ref, gains_ref, head_ref, normed, acc, pieces, qkv, context, hidden, wqkv, wo, sems, reached=lambda stage: None):
@@ -388,7 +397,7 @@
         out_shape=shape((QKV_PANELS, SEQ, HEAD), F32),
         in_specs=[VMEM] + [ANY] * len(arrays),
         out_specs=VMEM,
-        scratch_shapes=[some_wqkv(len(slots)), pltpu.SemaphoreType.DMA],
+        scratch_shapes=[some_wqkv(len(slots)), pltpu.SemaphoreType.DMA((2,))],
         compiler_params=limit(14),
         cost_estimate=cost(1_200_000_000, 20_000_000),
         name="early_pass",

time: 224 us -> 224 us (level)
  no operation moved by 1% of the time
where the time goes in v5:
time: 224 us; the launch traced here: 223 us
  waiting for transfers between devices  96.5 us (43%)
  Pallas kernels  54.1 us (24%)
  starting transfers between devices  48.2 us (22%)
  local copies, waits for them, and re-layouts  19.6 us (9%)
  other arithmetic  3.32 us (1%)
    ppermute x50, waiting for transfers between devices, moved(): return lax.ppermute(value, 'fsdp', [(i, target(i)) for i in range(N_FSDP)])  96.5 us
    ppermute x50, starting transfers between devices, moved(): return lax.ppermute(value, 'fsdp', [(i, target(i)) for i in range(N_FSDP)])  48 us
    unnamed x90, local copies, waits for them, and re-layouts  18.8 us
    pallas_call x1, Pallas kernels, own_pass(): pl.pallas_call(functools.partial(own_kernel, slots), out_shape=[shape((HQ...  14.1 us
    pallas_call x1, Pallas kernels, peer_pass(): pl.pallas_call(functools.partial(peer_kernel, slots), out_shape=[shape((S...  11.3 us
    pallas_call x2, Pallas kernels, weight_grads(): pl.pallas_call(kernel, out_shape=[shape((block, HEAD))] * 6 + [shape((blo...  7.52 us
    pallas_call x2, Pallas kernels, early_pass(): pl.pallas_call(functools.partial(early_kernel, slots), out_shape=shape((Q...  7.28 us
    pallas_call x1, Pallas kernels, attention_back(): pl.pallas_call(attention_back_kernel, out_shape=shape((QKV_PANELS, SEQ, H...  5.45 us
  transfers between devices with their start and end apart: 51, of which 24 were waited for; matrix products, arithmetic and copies ran while one was open for 2% of the time, Pallas kernels for 22%

profile of v5, /device:TPU:96, one launch (start us, length us, event | category | flops | bytes accessed | tf_op | source)
XLA Modules:
  0.0 222.9 jit_solution(6690292256803023969)
XLA Ops:
  0.6 2.8 %pack.1 = (bf16[1728,256]{1,0:T(8,128)(2,1)}, bf16[1728,256]{1,0:T(8,128)(2,1)}) custom-call(bf16[144,1024]{1,0:T(8,128)(2,1)} %bitcast.22, bf16[144,512]{1,0:T(8,128)(2,1)} %bitcast.26, bf16[144,512]{1,0:T(8,128)(2,1)} %bitcast.27, bf16[64,2304]{1,0:T(8,128)(2,1)} %bitcast.23, bf16[144,1024]{1,0:T(8,128)(2,1)} %bitcast.24, bf16[144,512]{1,0:T(8,128)(2,1)} %bitcast.28, ...), custom_call_target="tpu_custom_call" | custom-call | bytes 8000000 | tf_op jit(solution)/shard_map/pack/pallas_call | solution.py:81
  3.4 2.8 %collective-permute-start = (bf16[1728,256]{1,0:T(8,128)(2,1)}, bf16[1728,256]{1,0:T(8,128)(2,1)S(1)}, u32[]{:S(2)}, u32[]{:S(2)}) collective-permute-start(bf16[1728,256]{1,0:T(8,128)(2,1)} %get-tuple-element.135.refs_0_), channel_id=1, source_target_pairs={{0,12},{1,13},{2,14},{3,15},{4,0},{5,1},{6,2},{7,3},{8,4},{9,5},{1... | collective-permute-start | bytes 2654216 | tf_op jit(solution)/shard_map/ppermute | solution.py:44
  6.5 1.3 copy-done
  11.4 1.7 collective-permute-done.3.other
  14.0 11.5 %collective-permute-done.refs_3_ = bf16[1728,256]{1,0:T(8,128)(2,1)S(1)} collective-permute-done((bf16[1728,256]{1,0:T(8,128)(2,1)}, bf16[1728,256]{1,0:T(8,128)(2,1)S(1)}, u32[]{:S(2)}, u32[]{:S(2)}) %collective-permute-start) | collective-permute-done | bytes 884768 | tf_op jit(solution)/shard_map/ppermute | solution.py:44
  25.5 3.3 %collective-permute-done.1.refs_1_ = bf16[1728,256]{1,0:T(8,128)(2,1)S(1)} collective-permute-done((bf16[1728,256]{1,0:T(8,128)(2,1)}, bf16[1728,256]{1,0:T(8,128)(2,1)S(1)}, u32[]{:S(2)}, u32[]{:S(2)}) %collective-permute-start.1) | collective-permute-done | bytes 884768 | tf_op jit(solution)/shard_map/ppermute | solution.py:44
  29.1 3.2 %collective-permute-start.5 = (bf16[1728,256]{1,0:T(8,128)(2,1)}, bf16[1728,256]{1,0:T(8,128)(2,1)S(1)}, u32[]{:S(2)}, u32[]{:S(2)}) collective-permute-start(bf16[1728,256]{1,0:T(8,128)(2,1)} %get-tuple-element.135.refs_0_), channel_id=1, source_target_pairs={{0,2},{1,3},{2,0},{3,1},{4,6},{5,7},{6,4},{7,5},{8,10},{9,11},{10,... | collective-permute-start | bytes 2654216 | tf_op jit(solution)/shard_map/ppermute | solution.py:44
  32.6 1.7 collective-permute-start.7
  34.3 14.7 %collective-permute-done.6.refs_5_ = bf16[1728,256]{1,0:T(8,128)(2,1)S(1)} collective-permute-done((bf16[1728,256]{1,0:T(8,128)(2,1)S(1)}, bf16[1728,256]{1,0:T(8,128)(2,1)S(1)}, u32[]{:S(2)}, u32[]{:S(2)}) %collective-permute-start.6) | collective-permute-done | bytes 884768 | tf_op jit(solution)/shard_map/ppermute | solution.py:44
  49.0 3.2 %collective-permute-start.10 = (bf16[1728,256]{1,0:T(8,128)(2,1)S(1)}, bf16[1728,256]{1,0:T(8,128)(2,1)S(1)}, u32[]{:S(2)}, u32[]{:S(2)}) collective-permute-start(bf16[1728,256]{1,0:T(8,128)(2,1)S(1)} %collective-permute-done.4.refs_0_), channel_id=1, source_target_pairs={{0,2},{1,3},{2,0},{3,1},{4,6},{5,7},{6,4},{7,5},{8,10},{9,11},{10,... | collective-permute-start | bytes 2654216 | tf_op jit(solution)/shard_map/ppermute | solution.py:44
  53.3 2.3 %collective-permute-done.7.refs_1_ = bf16[1728,256]{1,0:T(8,128)(2,1)S(1)} collective-permute-done((bf16[1728,256]{1,0:T(8,128)(2,1)S(1)}, bf16[1728,256]{1,0:T(8,128)(2,1)S(1)}, u32[]{:S(2)}, u32[]{:S(2)}) %collective-permute-start.7) | collective-permute-done | bytes 884768 | tf_op jit(solution)/shard_map/ppermute | solution.py:44
  56.1 2.7 %collective-permute-start.12 = (bf16[1728,256]{1,0:T(8,128)(2,1)S(1)}, bf16[1728,256]{1,0:T(8,128)(2,1)S(1)}, u32[]{:S(2)}, u32[]{:S(2)}) collective-permute-start(bf16[1728,256]{1,0:T(8,128)(2,1)S(1)} %collective-permute-done.5.refs_2_), channel_id=1, source_target_pairs={{0,12},{1,13},{2,14},{3,15},{4,0},{5,1},{6,2},{7,3},{8,4},{9,5},{1... | collective-permute-start | bytes 2654216 | tf_op jit(solution)/shard_map/ppermute | solution.py:44
  59.4 12.5 %collective-permute-done.10.refs_2_ = bf16[1728,256]{1,0:T(8,128)(2,1)S(1)} collective-permute-done((bf16[1728,256]{1,0:T(8,128)(2,1)S(1)}, bf16[1728,256]{1,0:T(8,128)(2,1)S(1)}, u32[]{:S(2)}, u32[]{:S(2)}) %collective-permute-start.10) | collective-permute-done | bytes 884768 | tf_op jit(solution)/shard_map/ppermute | solution.py:44
  72.0 5.9 %collective-permute-done.11.refs_4_ = bf16[1728,256]{1,0:T(8,128)(2,1)S(1)} collective-permute-done((bf16[1728,256]{1,0:T(8,128)(2,1)S(1)}, bf16[1728,256]{1,0:T(8,128)(2,1)S(1)}, u32[]{:S(2)}, u32[]{:S(2)}) %collective-permute-start.11) | collective-permute-done | bytes 884768 | tf_op jit(solution)/shard_map/ppermute | solution.py:44
  81.1 3.2 %early_pass.2.acc = f32[8,256,256]{2,1,0:T(8,128)S(1)} custom-call(bf16[256,1152]{1,0:T(8,128)(2,1)S(1)} %get-tuple-element.133.normed, bf16[1728,256]{1,0:T(8,128)(2,1)S(1)} %copy-done.10, bf16[1728,256]{1,0:T(8,128)(2,1)S(1)} %collective-permute-done.1.refs_1_, bf16[1728,256]{1,0:T(8,128)(2,1)S(1)} %collective-permute-done.5.refs_2_, ...), custom_call_target="tpu_custom_call" | custom-call | flops 1200000000 | bytes 20000000 | tf_op jit(solution)/shard_map/early_pass/pallas_call | solution.py:395
  84.4 1.4 copy-done.2
  90.4 1.7 pad_maximum_fusion
  92.1 4.0 %collective-permute-done.16.refs_3_ = bf16[1728,256]{1,0:T(8,128)(2,1)} collective-permute-done((bf16[1728,256]{1,0:T(8,128)(2,1)S(1)}, bf16[1728,256]{1,0:T(8,128)(2,1)}, u32[]{:S(2)}, u32[]{:S(2)}) %collective-permute-start.16) | collective-permute-done | bytes 884768 | tf_op jit(solution)/shard_map/ppermute | solution.py:44
  96.1 3.4 %collective-permute-done.15.refs_7_ = bf16[1728,256]{1,0:T(8,128)(2,1)S(1)} collective-permute-done((bf16[1728,256]{1,0:T(8,128)(2,1)S(1)}, bf16[1728,256]{1,0:T(8,128)(2,1)S(1)}, u32[]{:S(2)}, u32[]{:S(2)}) %collective-permute-start.15) | collective-permute-done | bytes 884768 | tf_op jit(solution)/shard_map/ppermute | solution.py:44
  100.4 2.8 %collective-permute-start.20 = (bf16[1728,256]{1,0:T(8,128)(2,1)}, bf16[1728,256]{1,0:T(8,128)(2,1)}, u32[]{:S(2)}, u32[]{:S(2)}) collective-permute-start(bf16[1728,256]{1,0:T(8,128)(2,1)} %collective-permute-done.16.refs_3_), channel_id=1, source_target_pairs={{0,2},{1,3},{2,0},{3,1},{4,6},{5,7},{6,4},{7,5},{8,10},{9,11},{10,... | collective-permute-start | bytes 2654216 | tf_op jit(solution)/shard_map/ppermute | solution.py:44
  103.2 2.0 collective-permute-start.22
  107.2 14.1 %own_pass.1 = (bf16[512,256]{1,0:T(8,128)(2,1)}, bf16[512,256]{1,0:T(8,128)(2,1)}, bf16[8,256,256]{2,1,0:T(8,128)(2,1)}, f32[256,2304]{1,0:T(8,128)}, f32[256,256]{1,0:T(8,128)}, /*index=5*/bf16[9,1024,256]{2,1,0:T(8,128)(2,1)}) custom-call(s32[1]{0:T(128)} %bitcast.pos_ref, bf16[256,2304]{1,0:T(8,128)(2,1)} %bitcast.16, f32[2,2304]{1,0:T(2,128)} %gains_ref.5, ...), custom_call_target="tpu_custom_call" | custom-call | flops 3000000000 | bytes 30000000 | tf_op jit(solution)/shard_map/own_pass/pallas_call | solution.py:408
  121.3 2.9 %collective-permute-done.20.refs_8_ = bf16[1728,256]{1,0:T(8,128)(2,1)} collective-permute-done((bf16[1728,256]{1,0:T(8,128)(2,1)}, bf16[1728,256]{1,0:T(8,128)(2,1)}, u32[]{:S(2)}, u32[]{:S(2)}) %collective-permute-start.20) | collective-permute-done | bytes 884768 | tf_op jit(solution)/shard_map/ppermute | solution.py:44
  131.4 4.1 %early_pass.3.acc = f32[8,256,256]{2,1,0:T(8,128)S(1)} custom-call(bf16[256,1152]{1,0:T(8,128)(2,1)S(1)} %copy-done.21, bf16[1728,256]{1,0:T(8,128)(2,1)S(1)} %collective-permute-done.4.refs_0_, bf16[1728,256]{1,0:T(8,128)(2,1)S(1)} %copy-done.4, bf16[1728,256]{1,0:T(8,128)(2,1)S(1)} %copy-done.7, bf16[1728,256]{1,0:T(8,128)(2,1)} %collective-permute-done.16.refs_3_, ...), custom_call_target="tpu_custom_call" | custom-call | flops 1200000000 | bytes 20000000 | tf_op jit(solution)/shard_map/early_pass/pallas_call | solution.py:395
  135.7 1.7 copy-done.22
  137.3 11.3 %peer_pass.1 = (f32[256,1]{1,0:T(8,128)S(1)}, bf16[256,2304]{1,0:T(8,128)(2,1)S(1)}) custom-call(s32[1]{0:T(128)} %bitcast.pos_ref, bf16[256,2304]{1,0:T(8,128)(2,1)S(1)} %bitcast.18, f32[2,2304]{1,0:T(2,128)S(1)} %copy-done.27, bf16[2304,256]{1,0:T(8,128)(2,1)S(1)} %copy-done.9, bf16[256,1152]{1,0:T(8,128)(2,1)S(1)} %copy-done.19, ...), custom_call_target="tpu_custom_call" | custom-call | flops 3000000000 | bytes 30000000 | tf_op jit(solution)/shard_map/peer_pass/pallas_call | solution.py:441
  149.0 5.4 %attention_back.1.d_mine = bf16[8,256,256]{2,1,0:T(8,128)(2,1)S(1)} custom-call(bf16[256,2304]{1,0:T(8,128)(2,1)S(1)} %get-tuple-element.169.dhidden.d_mine, bf16[9,1024,256]{2,1,0:T(8,128)(2,1)S(1)} %bitcast.20, bf16[8,256,256]{2,1,0:T(8,128)(2,1)S(1)} %copy-done.23), custom_call_target="tpu_custom_call" | custom-call | flops 2000000000 | bytes 16000000 | tf_op jit(solution)/shard_map/attention_back/pallas_call | solution.py:461
  155.1 2.9 %out_grads.1 = (bf16[576,256]{1,0:T(8,128)(2,1)S(1)}, bf16[576,256]{1,0:T(8,128)(2,1)S(1)}, bf16[576,256]{1,0:T(8,128)(2,1)S(1)}, bf16[576,256]{1,0:T(8,128)(2,1...) custom-call(bf16[512,256]{1,0:T(8,128)(2,1)S(1)} %copy-done.33, ...), custom_call_target="tpu_custom_call" | custom-call | flops 1207959552 | bytes 10000000 | tf_op jit(solution)/shard_map/out_grads/pallas_call | solution.py:480
  158.0 1.5 collective-permute-start.33
  159.9 1.6 collective-permute-start.35
  161.5 4.7 %qkv_grads.1 = (bf16[1152,256]{1,0:T(8,128)(2,1)S(1)}, bf16[1152,256]{1,0:T(8,128)(2,1)S(1)}, bf16[1152,256]{1,0:T(8,128)(2,1)S(1)}, bf16[1152,256]{1,0:T(8,128)...) custom-call(bf16[1152,256]{1,0:T(8,128)(2,1)S(1)} %copy-done.30, ...), custom_call_target="tpu_custom_call" | custom-call | flops 2415919104 | bytes 10000000 | tf_op jit(solution)/shard_map/qkv_grads/pallas_call | solution.py:480
  166.2 2.2 collective-permute-start.36
  168.4 1.6 collective-permute-start.37
  170.4 3.6 %collective-permute-done.36.in_a = bf16[384,256]{1,0:T(8,128)(2,1)S(1)} collective-permute-done((bf16[384,256]{1,0:T(8,128)(2,1)S(1)}, bf16[384,256]{1,0:T(8,128)(2,1)S(1)}, u32[]{:S(2)}, u32[]{:S(2)}) %collective-permute-start.36) | collective-permute-done | bytes 196640 | tf_op jit(solution)/shard_map/ppermute | solution.py:44
  174.3 2.6 %collective-permute-done.38.in_c = bf16[384,256]{1,0:T(8,128)(2,1)S(1)} collective-permute-done((bf16[384,256]{1,0:T(8,128)(2,1)S(1)}, bf16[384,256]{1,0:T(8,128)(2,1)S(1)}, u32[]{:S(2)}, u32[]{:S(2)}) %collective-permute-start.38) | collective-permute-done | bytes 196640 | tf_op jit(solution)/shard_map/ppermute | solution.py:44
  177.1 3.2 %collective-permute-start.40 = (bf16[1152,256]{1,0:T(8,128)(2,1)S(1)}, bf16[1152,256]{1,0:T(8,128)(2,1)S(1)}, u32[]{:S(2)}, u32[]{:S(2)}) collective-permute-start(bf16[1152,256]{1,0:T(8,128)(2,1)S(1)} %get-tuple-element.214), channel_id=1, source_target_pairs={{0,12},{1,13},{2,14},{3,15},{4,0},{5,1},{6,2},{7,3},{8,4},{9,5},{1... | collective-permute-start | bytes 1769480 | tf_op jit(solution)/shard_map/ppermute | solution.py:44
  180.3 1.4 collective-permute-start.41
  181.9 3.2 %collective-permute-start.46 = (bf16[576,256]{1,0:T(8,128)(2,1)S(1)}, bf16[576,256]{1,0:T(8,128)(2,1)S(1)}, u32[]{:S(2)}, u32[]{:S(2)}) collective-permute-start(bf16[576,256]{1,0:T(8,128)(2,1)S(1)} %get-tuple-element.238), channel_id=1, source_target_pairs={{0,12},{1,13},{2,14},{3,15},{4,0},{5,1},{6,2},{7,3},{8,4},{9,5},{1... | collective-permute-start | bytes 884744 | tf_op jit(solution)/shard_map/ppermute | solution.py:44
  185.2 9.2 %collective-permute-done.39.in_x = bf16[1152,256]{1,0:T(8,128)(2,1)S(1)} collective-permute-done((bf16[1152,256]{1,0:T(8,128)(2,1)S(1)}, bf16[1152,256]{1,0:T(8,128)(2,1)S(1)}, u32[]{:S(2)}, u32[]{:S(2)}) %collective-permute-start.39) | collective-permute-done | bytes 589856 | tf_op jit(solution)/shard_map/ppermute | solution.py:44
  194.4 1.6 collective-permute-start.47
  195.9 1.9 collective-permute-start.49
  199.1 2.0 collective-permute-start.42
  201.1 1.4 collective-permute-start.44
  202.5 3.2 %collective-permute-done.47.in_y = bf16[576,256]{1,0:T(8,128)(2,1)S(1)} collective-permute-done((bf16[576,256]{1,0:T(8,128)(2,1)S(1)}, bf16[576,256]{1,0:T(8,128)(2,1)S(1)}, u32[]{:S(2)}, u32[]{:S(2)}) %collective-permute-start.47) | collective-permute-done | bytes 294944 | tf_op jit(solution)/shard_map/ppermute | solution.py:44
  206.8 1.4 collective-permute-start.50
  208.2 1.6 reduce
  209.8 7.4 %collective-permute-done.48.refs_1_ = bf16[576,256]{1,0:T(8,128)(2,1)S(1)} collective-permute-done((bf16[576,256]{1,0:T(8,128)(2,1)}, bf16[576,256]{1,0:T(8,128)(2,1)S(1)}, u32[]{:S(2)}, u32[]{:S(2)}) %collective-permute-start.48) | collective-permute-done | bytes 294944 | tf_op jit(solution)/shard_map/ppermute | solution.py:44
  217.2 3.5 %collective-permute-done.50.refs_3_ = bf16[576,256]{1,0:T(8,128)(2,1)S(1)} collective-permute-done((bf16[576,256]{1,0:T(8,128)(2,1)}, bf16[576,256]{1,0:T(8,128)(2,1)S(1)}, u32[]{:S(2)}, u32[]{:S(2)}) %collective-permute-start.50) | collective-permute-done | bytes 294944 | tf_op jit(solution)/shard_map/ppermute | solution.py:44
  (163 shorter events, 32.3 us)
Async XLA Ops:
  3.4 22.1 %collective-permute-start = (bf16[1728,256]{1,0:T(8,128)(2,1)}, bf16[1728,256]{1,0:T(8,128)(2,1)S(1)}, u32[]{:S(2)}, u32[]{:S(2)}) collective-permute-start(bf16[1728,256]{1,0:T(8,128)(2,1)} %get-tuple-element.135.refs_0_), channel_id=1, source_target_pairs={{0,12},{1,13},{2,14},{3,15},{4,0},{5,1},{6,2},{7,3},{8,4},{9,5},{1... | collective-permute-start | bytes 2654216 | tf_op jit(solution)/shard_map/ppermute | solution.py:44
  6.2 22.5 %collective-permute-start.1 = (bf16[1728,256]{1,0:T(8,128)(2,1)}, bf16[1728,256]{1,0:T(8,128)(2,1)S(1)}, u32[]{:S(2)}, u32[]{:S(2)}) collective-permute-start(bf16[1728,256]{1,0:T(8,128)(2,1)} %get-tuple-element.135.refs_0_), channel_id=1, source_target_pairs={{0,4},{1,5},{2,6},{3,7},{4,8},{5,9},{6,10},{7,11},{8,12},{9,13},{1... | collective-permute-start | bytes 2654216 | tf_op jit(solution)/shard_map/ppermute | solution.py:44
  6.2 22.5 %collective-permute-start.2 = (bf16[1728,256]{1,0:T(8,128)(2,1)}, bf16[1728,256]{1,0:T(8,128)(2,1)S(1)}, u32[]{:S(2)}, u32[]{:S(2)}) collective-permute-start(bf16[1728,256]{1,0:T(8,128)(2,1)} %get-tuple-element.135.refs_0_), channel_id=1, source_target_pairs={{0,1},{1,0},{2,3},{3,2},{4,5},{5,4},{6,7},{7,6},{8,9},{9,8},{10,11... | collective-permute-start | bytes 2654216 | tf_op jit(solution)/shard_map/ppermute | solution.py:44
  6.2 26.3 %collective-permute-start.4 = (bf16[1728,256]{1,0:T(8,128)(2,1)}, bf16[1728,256]{1,0:T(8,128)(2,1)S(1)}, u32[]{:S(2)}, u32[]{:S(2)}) collective-permute-start(bf16[1728,256]{1,0:T(8,128)(2,1)} %get-tuple-element.134), channel_id=1, source_target_pairs={{0,16},{16,32},{32,48},{48,64},{64,80},{80,96},{96,112},{112,0},{1... | collective-permute-start | bytes 2654216 | tf_op jit(solution)/shard_map/ppermute | solution.py:585
  28.8 20.3 %collective-permute-start.6 = (bf16[1728,256]{1,0:T(8,128)(2,1)S(1)}, bf16[1728,256]{1,0:T(8,128)(2,1)S(1)}, u32[]{:S(2)}, u32[]{:S(2)}) collective-permute-start(bf16[1728,256]{1,0:T(8,128)(2,1)S(1)} %collective-permute-done.refs_3_), channel_id=1, source_target_pairs={{0,12},{1,13},{2,14},{3,15},{4,0},{5,1},{6,2},{7,3},{8,4},{9,5},{1... | collective-permute-start | bytes 2654216 | tf_op jit(solution)/shard_map/ppermute | solution.py:44
  29.1 23.1 %collective-permute-start.8 = (bf16[1728,256]{1,0:T(8,128)(2,1)S(1)}, bf16[1728,256]{1,0:T(8,128)(2,1)S(1)}, u32[]{:S(2)}, u32[]{:S(2)}) collective-permute-start(bf16[1728,256]{1,0:T(8,128)(2,1)S(1)} %collective-permute-done.refs_3_), channel_id=1, source_target_pairs={{0,1},{1,0},{2,3},{3,2},{4,5},{5,4},{6,7},{7,6},{8,9},{9,8},{10,11... | collective-permute-start | bytes 2654216 | tf_op jit(solution)/shard_map/ppermute | solution.py:44
  29.1 24.2 %collective-permute-start.5 = (bf16[1728,256]{1,0:T(8,128)(2,1)}, bf16[1728,256]{1,0:T(8,128)(2,1)S(1)}, u32[]{:S(2)}, u32[]{:S(2)}) collective-permute-start(bf16[1728,256]{1,0:T(8,128)(2,1)} %get-tuple-element.135.refs_0_), channel_id=1, source_target_pairs={{0,2},{1,3},{2,0},{3,1},{4,6},{5,7},{6,4},{7,5},{8,10},{9,11},{10,... | collective-permute-start | bytes 2654216 | tf_op jit(solution)/shard_map/ppermute | solution.py:44
  32.3 21.0 %collective-permute-start.9 = (bf16[1728,256]{1,0:T(8,128)(2,1)S(1)}, bf16[1728,256]{1,0:T(8,128)(2,1)S(1)}, u32[]{:S(2)}, u32[]{:S(2)}) collective-permute-start(bf16[1728,256]{1,0:T(8,128)(2,1)S(1)} %collective-permute-done.1.refs_1_), channel_id=1, source_target_pairs={{0,1},{1,0},{2,3},{3,2},{4,5},{5,4},{6,7},{7,6},{8,9},{9,8},{10,11... | collective-permute-start | bytes 2654216 | tf_op jit(solution)/shard_map/ppermute | solution.py:44
  32.6 23.0 %collective-permute-start.7 = (bf16[1728,256]{1,0:T(8,128)(2,1)S(1)}, bf16[1728,256]{1,0:T(8,128)(2,1)S(1)}, u32[]{:S(2)}, u32[]{:S(2)}) collective-permute-start(bf16[1728,256]{1,0:T(8,128)(2,1)S(1)} %collective-permute-done.4.refs_0_), channel_id=1, source_target_pairs={{0,4},{1,5},{2,6},{3,7},{4,8},{5,9},{6,10},{7,11},{8,12},{9,13},{1... | collective-permute-start | bytes 2654216 | tf_op jit(solution)/shard_map/ppermute | solution.py:44
  49.0 22.8 %collective-permute-start.10 = (bf16[1728,256]{1,0:T(8,128)(2,1)S(1)}, bf16[1728,256]{1,0:T(8,128)(2,1)S(1)}, u32[]{:S(2)}, u32[]{:S(2)}) collective-permute-start(bf16[1728,256]{1,0:T(8,128)(2,1)S(1)} %collective-permute-done.4.refs_0_), channel_id=1, source_target_pairs={{0,2},{1,3},{2,0},{3,1},{4,6},{5,7},{6,4},{7,5},{8,10},{9,11},{10,... | collective-permute-start | bytes 2654216 | tf_op jit(solution)/shard_map/ppermute | solution.py:44
  55.6 22.2 %collective-permute-start.11 = (bf16[1728,256]{1,0:T(8,128)(2,1)S(1)}, bf16[1728,256]{1,0:T(8,128)(2,1)S(1)}, u32[]{:S(2)}, u32[]{:S(2)}) collective-permute-start(bf16[1728,256]{1,0:T(8,128)(2,1)S(1)} %collective-permute-done.5.refs_2_), channel_id=1, source_target_pairs={{0,4},{1,5},{2,6},{3,7},{4,8},{5,9},{6,10},{7,11},{8,12},{9,13},{1... | collective-permute-start | bytes 2654216 | tf_op jit(solution)/shard_map/ppermute | solution.py:44
  56.1 22.8 %collective-permute-start.12 = (bf16[1728,256]{1,0:T(8,128)(2,1)S(1)}, bf16[1728,256]{1,0:T(8,128)(2,1)S(1)}, u32[]{:S(2)}, u32[]{:S(2)}) collective-permute-start(bf16[1728,256]{1,0:T(8,128)(2,1)S(1)} %collective-permute-done.5.refs_2_), channel_id=1, source_target_pairs={{0,12},{1,13},{2,14},{3,15},{4,0},{5,1},{6,2},{7,3},{8,4},{9,5},{1... | collective-permute-start | bytes 2654216 | tf_op jit(solution)/shard_map/ppermute | solution.py:44
  58.9 20.1 %collective-permute-start.13 = (bf16[1728,256]{1,0:T(8,128)(2,1)S(1)}, bf16[1728,256]{1,0:T(8,128)(2,1)S(1)}, u32[]{:S(2)}, u32[]{:S(2)}) collective-permute-start(bf16[1728,256]{1,0:T(8,128)(2,1)S(1)} %collective-permute-done.5.refs_2_), channel_id=1, source_target_pairs={{0,1},{1,0},{2,3},{3,2},{4,5},{5,4},{6,7},{7,6},{8,9},{9,8},{10,11... | collective-permute-start | bytes 2654216 | tf_op jit(solution)/shard_map/ppermute | solution.py:44
  58.9 20.1 %collective-permute-start.14 = (bf16[1728,256]{1,0:T(8,128)(2,1)S(1)}, bf16[1728,256]{1,0:T(8,128)(2,1)S(1)}, u32[]{:S(2)}, u32[]{:S(2)}) collective-permute-start(bf16[1728,256]{1,0:T(8,128)(2,1)S(1)} %collective-permute-done.6.refs_5_), channel_id=1, source_target_pairs={{0,1},{1,0},{2,3},{3,2},{4,5},{5,4},{6,7},{7,6},{8,9},{9,8},{10,11... | collective-permute-start | bytes 2654216 | tf_op jit(solution)/shard_map/ppermute | solution.py:44
  71.9 24.2 %collective-permute-start.16 = (bf16[1728,256]{1,0:T(8,128)(2,1)S(1)}, bf16[1728,256]{1,0:T(8,128)(2,1)}, u32[]{:S(2)}, u32[]{:S(2)}) collective-permute-start(bf16[1728,256]{1,0:T(8,128)(2,1)S(1)} %collective-permute-done.4.refs_0_), channel_id=1, source_target_pairs={{0,12},{1,13},{2,14},{3,15},{4,0},{5,1},{6,2},{7,3},{8,4},{9,5},{1... | collective-permute-start | bytes 2654216 | tf_op jit(solution)/shard_map/ppermute | solution.py:44
  77.8 21.6 %collective-permute-start.15 = (bf16[1728,256]{1,0:T(8,128)(2,1)S(1)}, bf16[1728,256]{1,0:T(8,128)(2,1)S(1)}, u32[]{:S(2)}, u32[]{:S(2)}) collective-permute-start(bf16[1728,256]{1,0:T(8,128)(2,1)S(1)} %collective-permute-done.6.refs_5_), channel_id=1, source_target_pairs={{0,2},{1,3},{2,0},{3,1},{4,6},{5,7},{6,4},{7,5},{8,10},{9,11},{10,... | collective-permute-start | bytes 2654216 | tf_op jit(solution)/shard_map/ppermute | solution.py:44
  79.0 20.8 %collective-permute-start.17 = (bf16[1728,256]{1,0:T(8,128)(2,1)S(1)}, bf16[1728,256]{1,0:T(8,128)(2,1)}, u32[]{:S(2)}, u32[]{:S(2)}) collective-permute-start(bf16[1728,256]{1,0:T(8,128)(2,1)S(1)} %collective-permute-done.10.refs_2_), channel_id=1, source_target_pairs={{0,4},{1,5},{2,6},{3,7},{4,8},{5,9},{6,10},{7,11},{8,12},{9,13},{1... | collective-permute-start | bytes 2654216 | tf_op jit(solution)/shard_map/ppermute | solution.py:44
  79.3 20.5 %collective-permute-start.18 = (bf16[1728,256]{1,0:T(8,128)(2,1)S(1)}, bf16[1728,256]{1,0:T(8,128)(2,1)S(1)}, u32[]{:S(2)}, u32[]{:S(2)}) collective-permute-start(bf16[1728,256]{1,0:T(8,128)(2,1)S(1)} %collective-permute-done.11.refs_4_), channel_id=1, source_target_pairs={{0,1},{1,0},{2,3},{3,2},{4,5},{5,4},{6,7},{7,6},{8,9},{9,8},{10,11... | collective-permute-start | bytes 2654216 | tf_op jit(solution)/shard_map/ppermute | solution.py:44
  79.9 19.9 %collective-permute-start.19 = (bf16[1728,256]{1,0:T(8,128)(2,1)S(1)}, bf16[1728,256]{1,0:T(8,128)(2,1)S(1)}, u32[]{:S(2)}, u32[]{:S(2)}) collective-permute-start(bf16[1728,256]{1,0:T(8,128)(2,1)S(1)} %collective-permute-done.12.refs_6_), channel_id=1, source_target_pairs={{0,1},{1,0},{2,3},{3,2},{4,5},{5,4},{6,7},{7,6},{8,9},{9,8},{10,11... | collective-permute-start | bytes 2654216 | tf_op jit(solution)/shard_map/ppermute | solution.py:44
  99.8 26.3 %collective-permute-start.23 = (bf16[5184,256]{1,0:T(8,128)(2,1)}, bf16[5184,256]{1,0:T(8,128)(2,1)S(1)}, u32[]{:S(2)}, u32[]{:S(2)}) collective-permute-start(bf16[5184,256]{1,0:T(8,128)(2,1)} %pad_maximum_fusion), channel_id=1, source_target_pairs={{0,1},{1,0},{2,3},{3,2},{4,5},{5,4},{6,7},{7,6},{8,9},{9,8},{10,11... | collective-permute-start | bytes 7962632 | tf_op jit(solution)/shard_map/ppermute | solution.py:44
  100.4 23.9 %collective-permute-start.20 = (bf16[1728,256]{1,0:T(8,128)(2,1)}, bf16[1728,256]{1,0:T(8,128)(2,1)}, u32[]{:S(2)}, u32[]{:S(2)}) collective-permute-start(bf16[1728,256]{1,0:T(8,128)(2,1)} %collective-permute-done.16.refs_3_), channel_id=1, source_target_pairs={{0,2},{1,3},{2,0},{3,1},{4,6},{5,7},{6,4},{7,5},{8,10},{9,11},{10,... | collective-permute-start | bytes 2654216 | tf_op jit(solution)/shard_map/ppermute | solution.py:44
  103.2 21.7 %collective-permute-start.21 = (bf16[1728,256]{1,0:T(8,128)(2,1)}, bf16[1728,256]{1,0:T(8,128)(2,1)}, u32[]{:S(2)}, u32[]{:S(2)}) collective-permute-start(bf16[1728,256]{1,0:T(8,128)(2,1)} %collective-permute-done.16.refs_3_), channel_id=1, source_target_pairs={{0,12},{1,13},{2,14},{3,15},{4,0},{5,1},{6,2},{7,3},{8,4},{9,5},{1... | collective-permute-start | bytes 2654216 | tf_op jit(solution)/shard_map/ppermute | solution.py:44
  103.2 22.9 %collective-permute-start.22 = (bf16[1728,256]{1,0:T(8,128)(2,1)}, bf16[1728,256]{1,0:T(8,128)(2,1)}, u32[]{:S(2)}, u32[]{:S(2)}) collective-permute-start(bf16[1728,256]{1,0:T(8,128)(2,1)} %collective-permute-done.17.refs_6_), channel_id=1, source_target_pairs={{0,4},{1,5},{2,6},{3,7},{4,8},{5,9},{6,10},{7,11},{8,12},{9,13},{1... | collective-permute-start | bytes 2654216 | tf_op jit(solution)/shard_map/ppermute | solution.py:44
  107.1 19.1 %collective-permute-start.24 = (bf16[1728,256]{1,0:T(8,128)(2,1)}, bf16[1728,256]{1,0:T(8,128)(2,1)}, u32[]{:S(2)}, u32[]{:S(2)}) collective-permute-start(bf16[1728,256]{1,0:T(8,128)(2,1)} %collective-permute-done.16.refs_3_), channel_id=1, source_target_pairs={{0,1},{1,0},{2,3},{3,2},{4,5},{5,4},{6,7},{7,6},{8,9},{9,8},{10,11... | collective-permute-start | bytes 2654216 | tf_op jit(solution)/shard_map/ppermute | solution.py:44
  124.3 11.3 %collective-permute-start.26 = (bf16[1728,256]{1,0:T(8,128)(2,1)}, bf16[1728,256]{1,0:T(8,128)(2,1)}, u32[]{:S(2)}, u32[]{:S(2)}) collective-permute-start(bf16[1728,256]{1,0:T(8,128)(2,1)} %collective-permute-done.17.refs_6_), channel_id=1, source_target_pairs={{0,1},{1,0},{2,3},{3,2},{4,5},{5,4},{6,7},{7,6},{8,9},{9,8},{10,11... | collective-permute-start | bytes 2654216 | tf_op jit(solution)/shard_map/ppermute | solution.py:44
  126.1 9.4 %collective-permute-start.27 = (bf16[1728,256]{1,0:T(8,128)(2,1)}, bf16[1728,256]{1,0:T(8,128)(2,1)}, u32[]{:S(2)}, u32[]{:S(2)}) collective-permute-start(bf16[1728,256]{1,0:T(8,128)(2,1)} %collective-permute-done.21.refs_7_), channel_id=1, source_target_pairs={{0,1},{1,0},{2,3},{3,2},{4,5},{5,4},{6,7},{7,6},{8,9},{9,8},{10,11... | collective-permute-start | bytes 2654216 | tf_op jit(solution)/shard_map/ppermute | solution.py:44
  126.2 9.4 %collective-permute-start.28 = (bf16[1728,256]{1,0:T(8,128)(2,1)}, bf16[1728,256]{1,0:T(8,128)(2,1)}, u32[]{:S(2)}, u32[]{:S(2)}) collective-permute-start(bf16[1728,256]{1,0:T(8,128)(2,1)} %collective-permute-done.20.refs_8_), channel_id=1, source_target_pairs={{0,1},{1,0},{2,3},{3,2},{4,5},{5,4},{6,7},{7,6},{8,9},{9,8},{10,11... | collective-permute-start | bytes 2654216 | tf_op jit(solution)/shard_map/ppermute | solution.py:44
  126.7 8.9 %collective-permute-start.29 = (bf16[1728,256]{1,0:T(8,128)(2,1)}, bf16[1728,256]{1,0:T(8,128)(2,1)}, u32[]{:S(2)}, u32[]{:S(2)}) collective-permute-start(bf16[1728,256]{1,0:T(8,128)(2,1)} %collective-permute-done.22.refs_9_), channel_id=1, source_target_pairs={{0,1},{1,0},{2,3},{3,2},{4,5},{5,4},{6,7},{7,6},{8,9},{9,8},{10,11... | collective-permute-start | bytes 2654216 | tf_op jit(solution)/shard_map/ppermute | solution.py:44
  127.5 21.1 %collective-permute-start.30 = (bf16[512,256]{1,0:T(8,128)(2,1)}, bf16[512,256]{1,0:T(8,128)(2,1)S(1)}, u32[]{:S(2)}, u32[]{:S(2)}) collective-permute-start(bf16[512,256]{1,0:T(8,128)(2,1)} %get-tuple-element.168), channel_id=1, source_target_pairs={{0,1},{1,0},{2,3},{3,2},{4,5},{5,4},{6,7},{7,6},{8,9},{9,8},{10,11... | collective-permute-start | bytes 786440 | tf_op jit(solution)/shard_map/ppermute | solution.py:44
  148.7 6.4 %collective-permute-start.32 = (bf16[256,2304]{1,0:T(8,128)(2,1)S(1)}, bf16[256,2304]{1,0:T(8,128)(2,1)S(1)}, u32[]{:S(2)}, u32[]{:S(2)}) collective-permute-start(bf16[256,2304]{1,0:T(8,128)(2,1)S(1)} %get-tuple-element.169.dhidden.d_mine), channel_id=1, source_target_pairs={{0,1},{1,0},{2,3},{3,2},{4,5},{5,4},{6,7},{7,6},{8,9},{9,8},{10,11... | collective-permute-start | bytes 3538952 | tf_op jit(solution)/shard_map/ppermute | solution.py:44
  158.0 8.2 %collective-permute-start.33 = (bf16[192,256]{1,0:T(8,128)(2,1)S(1)}, bf16[192,256]{1,0:T(8,128)(2,1)S(1)}, u32[]{:S(2)}, u32[]{:S(2)}) collective-permute-start(bf16[192,256]{1,0:T(8,128)(2,1)S(1)} %get-tuple-element.184), channel_id=1, source_target_pairs={{0,2},{1,3},{2,0},{3,1},{4,6},{5,7},{6,4},{7,5},{8,10},{9,11},{10,... | collective-permute-start | bytes 294920 | tf_op jit(solution)/shard_map/ppermute | solution.py:44
  159.5 6.7 %collective-permute-start.34 = (bf16[192,256]{1,0:T(8,128)(2,1)S(1)}, bf16[192,256]{1,0:T(8,128)(2,1)S(1)}, u32[]{:S(2)}, u32[]{:S(2)}) collective-permute-start(bf16[192,256]{1,0:T(8,128)(2,1)S(1)} %get-tuple-element.185), channel_id=1, source_target_pairs={{0,12},{1,13},{2,14},{3,15},{4,0},{5,1},{6,2},{7,3},{8,4},{9,5},{1... | collective-permute-start | bytes 294920 | tf_op jit(solution)/shard_map/ppermute | solution.py:44
  159.9 6.3 %collective-permute-start.35 = (bf16[192,256]{1,0:T(8,128)(2,1)S(1)}, bf16[192,256]{1,0:T(8,128)(2,1)S(1)}, u32[]{:S(2)}, u32[]{:S(2)}) collective-permute-start(bf16[192,256]{1,0:T(8,128)(2,1)S(1)} %get-tuple-element.186), channel_id=1, source_target_pairs={{0,4},{1,5},{2,6},{3,7},{4,8},{5,9},{6,10},{7,11},{8,12},{9,13},{1... | collective-permute-start | bytes 294920 | tf_op jit(solution)/shard_map/ppermute | solution.py:44
  166.2 7.7 %collective-permute-start.36 = (bf16[384,256]{1,0:T(8,128)(2,1)S(1)}, bf16[384,256]{1,0:T(8,128)(2,1)S(1)}, u32[]{:S(2)}, u32[]{:S(2)}) collective-permute-start(bf16[384,256]{1,0:T(8,128)(2,1)S(1)} %get-tuple-element.207), channel_id=1, source_target_pairs={{0,2},{1,3},{2,0},{3,1},{4,6},{5,7},{6,4},{7,5},{8,10},{9,11},{10,... | collective-permute-start | bytes 589832 | tf_op jit(solution)/shard_map/ppermute | solution.py:44
  168.4 5.9 %collective-permute-start.37 = (bf16[384,256]{1,0:T(8,128)(2,1)S(1)}, bf16[384,256]{1,0:T(8,128)(2,1)S(1)}, u32[]{:S(2)}, u32[]{:S(2)}) collective-permute-start(bf16[384,256]{1,0:T(8,128)(2,1)S(1)} %get-tuple-element.208), channel_id=1, source_target_pairs={{0,12},{1,13},{2,14},{3,15},{4,0},{5,1},{6,2},{7,3},{8,4},{9,5},{1... | collective-permute-start | bytes 589832 | tf_op jit(solution)/shard_map/ppermute | solution.py:44
  170.0 6.9 %collective-permute-start.38 = (bf16[384,256]{1,0:T(8,128)(2,1)S(1)}, bf16[384,256]{1,0:T(8,128)(2,1)S(1)}, u32[]{:S(2)}, u32[]{:S(2)}) collective-permute-start(bf16[384,256]{1,0:T(8,128)(2,1)S(1)} %get-tuple-element.209), channel_id=1, source_target_pairs={{0,4},{1,5},{2,6},{3,7},{4,8},{5,9},{6,10},{7,11},{8,12},{9,13},{1... | collective-permute-start | bytes 589832 | tf_op jit(solution)/shard_map/ppermute | solution.py:44
  177.0 17.3 %collective-permute-start.39 = (bf16[1152,256]{1,0:T(8,128)(2,1)S(1)}, bf16[1152,256]{1,0:T(8,128)(2,1)S(1)}, u32[]{:S(2)}, u32[]{:S(2)}) collective-permute-start(bf16[1152,256]{1,0:T(8,128)(2,1)S(1)} %get-tuple-element.213), channel_id=1, source_target_pairs={{0,4},{1,5},{2,6},{3,7},{4,8},{5,9},{6,10},{7,11},{8,12},{9,13},{1... | collective-permute-start | bytes 1769480 | tf_op jit(solution)/shard_map/ppermute | solution.py:44
  177.1 18.8 %collective-permute-start.40 = (bf16[1152,256]{1,0:T(8,128)(2,1)S(1)}, bf16[1152,256]{1,0:T(8,128)(2,1)S(1)}, u32[]{:S(2)}, u32[]{:S(2)}) collective-permute-start(bf16[1152,256]{1,0:T(8,128)(2,1)S(1)} %get-tuple-element.214), channel_id=1, source_target_pairs={{0,12},{1,13},{2,14},{3,15},{4,0},{5,1},{6,2},{7,3},{8,4},{9,5},{1... | collective-permute-start | bytes 1769480 | tf_op jit(solution)/shard_map/ppermute | solution.py:44
  180.3 17.5 %collective-permute-start.41 = (bf16[1152,256]{1,0:T(8,128)(2,1)S(1)}, bf16[1152,256]{1,0:T(8,128)(2,1)S(1)}, u32[]{:S(2)}, u32[]{:S(2)}) collective-permute-start(bf16[1152,256]{1,0:T(8,128)(2,1)S(1)} %get-tuple-element.215), channel_id=1, source_target_pairs={{0,2},{1,3},{2,0},{3,1},{4,6},{5,7},{6,4},{7,5},{8,10},{9,11},{10,... | collective-permute-start | bytes 1769480 | tf_op jit(solution)/shard_map/ppermute | solution.py:44
  181.9 17.2 %collective-permute-start.45 = (bf16[576,256]{1,0:T(8,128)(2,1)S(1)}, bf16[576,256]{1,0:T(8,128)(2,1)S(1)}, u32[]{:S(2)}, u32[]{:S(2)}) collective-permute-start(bf16[576,256]{1,0:T(8,128)(2,1)S(1)} %get-tuple-element.237), channel_id=1, source_target_pairs={{0,4},{1,5},{2,6},{3,7},{4,8},{5,9},{6,10},{7,11},{8,12},{9,13},{1... | collective-permute-start | bytes 884744 | tf_op jit(solution)/shard_map/ppermute | solution.py:44
  181.9 19.1 %collective-permute-start.46 = (bf16[576,256]{1,0:T(8,128)(2,1)S(1)}, bf16[576,256]{1,0:T(8,128)(2,1)S(1)}, u32[]{:S(2)}, u32[]{:S(2)}) collective-permute-start(bf16[576,256]{1,0:T(8,128)(2,1)S(1)} %get-tuple-element.238), channel_id=1, source_target_pairs={{0,12},{1,13},{2,14},{3,15},{4,0},{5,1},{6,2},{7,3},{8,4},{9,5},{1... | collective-permute-start | bytes 884744 | tf_op jit(solution)/shard_map/ppermute | solution.py:44
  194.4 11.4 %collective-permute-start.47 = (bf16[576,256]{1,0:T(8,128)(2,1)S(1)}, bf16[576,256]{1,0:T(8,128)(2,1)S(1)}, u32[]{:S(2)}, u32[]{:S(2)}) collective-permute-start(bf16[576,256]{1,0:T(8,128)(2,1)S(1)} %get-tuple-element.239), channel_id=1, source_target_pairs={{0,2},{1,3},{2,0},{3,1},{4,6},{5,7},{6,4},{7,5},{8,10},{9,11},{10,... | collective-permute-start | bytes 884744 | tf_op jit(solution)/shard_map/ppermute | solution.py:44
  195.9 10.8 %collective-permute-start.49 = (bf16[576,256]{1,0:T(8,128)(2,1)S(1)}, bf16[576,256]{1,0:T(8,128)(2,1)S(1)}, u32[]{:S(2)}, u32[]{:S(2)}) collective-permute-start(bf16[576,256]{1,0:T(8,128)(2,1)S(1)} %get-tuple-element.244), channel_id=1, source_target_pairs={{0,12},{1,13},{2,14},{3,15},{4,0},{5,1},{6,2},{7,3},{8,4},{9,5},{1... | collective-permute-start | bytes 884744 | tf_op jit(solution)/shard_map/ppermute | solution.py:44
  197.8 23.8 %collective-permute-start.43 = (bf16[1152,256]{1,0:T(8,128)(2,1)}, bf16[1152,256]{1,0:T(8,128)(2,1)S(1)}, u32[]{:S(2)}, u32[]{:S(2)}) collective-permute-start(bf16[1152,256]{1,0:T(8,128)(2,1)} %get-tuple-element.220), channel_id=1, source_target_pairs={{0,12},{1,13},{2,14},{3,15},{4,0},{5,1},{6,2},{7,3},{8,4},{9,5},{1... | collective-permute-start | bytes 1769480 | tf_op jit(solution)/shard_map/ppermute | solution.py:44
  199.1 22.5 %collective-permute-start.42 = (bf16[1152,256]{1,0:T(8,128)(2,1)}, bf16[1152,256]{1,0:T(8,128)(2,1)S(1)}, u32[]{:S(2)}, u32[]{:S(2)}) collective-permute-start(bf16[1152,256]{1,0:T(8,128)(2,1)} %get-tuple-element.219), channel_id=1, source_target_pairs={{0,4},{1,5},{2,6},{3,7},{4,8},{5,9},{6,10},{7,11},{8,12},{9,13},{1... | collective-permute-start | bytes 1769480 | tf_op jit(solution)/shard_map/ppermute | solution.py:44
  201.1 20.5 %collective-permute-start.44 = (bf16[1152,256]{1,0:T(8,128)(2,1)}, bf16[1152,256]{1,0:T(8,128)(2,1)S(1)}, u32[]{:S(2)}, u32[]{:S(2)}) collective-permute-start(bf16[1152,256]{1,0:T(8,128)(2,1)} %get-tuple-element.221), channel_id=1, source_target_pairs={{0,2},{1,3},{2,0},{3,1},{4,6},{5,7},{6,4},{7,5},{8,10},{9,11},{10,... | collective-permute-start | bytes 1769480 | tf_op jit(solution)/shard_map/ppermute | solution.py:44
  206.6 10.6 %collective-permute-start.48 = (bf16[576,256]{1,0:T(8,128)(2,1)}, bf16[576,256]{1,0:T(8,128)(2,1)S(1)}, u32[]{:S(2)}, u32[]{:S(2)}) collective-permute-start(bf16[576,256]{1,0:T(8,128)(2,1)} %get-tuple-element.243), channel_id=1, source_target_pairs={{0,4},{1,5},{2,6},{3,7},{4,8},{5,9},{6,10},{7,11},{8,12},{9,13},{1... | collective-permute-start | bytes 884744 | tf_op jit(solution)/shard_map/ppermute | solution.py:44
  206.8 13.9 %collective-permute-start.50 = (bf16[576,256]{1,0:T(8,128)(2,1)}, bf16[576,256]{1,0:T(8,128)(2,1)S(1)}, u32[]{:S(2)}, u32[]{:S(2)}) collective-permute-start(bf16[576,256]{1,0:T(8,128)(2,1)} %get-tuple-element.245), channel_id=1, source_target_pairs={{0,2},{1,3},{2,0},{3,1},{4,6},{5,7},{6,4},{7,5},{8,10},{9,11},{10,... | collective-permute-start | bytes 884744 | tf_op jit(solution)/shard_map/ppermute | solution.py:44
  (48 other events, 441.0 us)
